TPU v7x, 512 devices: a whole 4x8x8 slice. The times are simulated.
512 devices in a mesh: grp: 16 (over z, core), aux: 32 (over x, y).
Axes of the slice: x: 4, y: 8, z: 8, core: 2. Of those that a mesh axis runs over, the one named last changes fastest.
Arguments:
- integrals: bfloat16 [2048, 262144], P('aux', 'grp'), parts along dimension 1, may hold values from -6 to 6
- inverses: bfloat16 [4, 512, 512], P(None, 'aux'), as said below
- lower_blocks: bfloat16 [6, 512, 512], P(None, 'aux'), may hold values from -0.25 to 0.25
Outputs:
- solved: bfloat16 [2048, 262144], P(None, ('grp', 'aux')), parts along dimension 1
There are 16 independent parts, one for each index of `grp`. A program takes and returns all parts, laid end to end along the dimension named above; an argument that names none is the same for every part. Nothing has to cross between parts.
Inputs may be any that keep to these rules, and one draw needn't show every extreme that they name: Each inverses[k] is lower triangular with diagonal entries between 0.5 and 1.5.
All inputs are finite; a program needn't handle non-finite values.
Results may differ from a plain program's by a relative error of at most 0.007.
Values may be sent and summed in bfloat16 or wider, within the bound.
No kernel may reach another device: no remote copies, remote signals or barrier semaphores. Data moves between devices by JAX's collectives and lax.ppermute only.
A program may use at most 64 MiB of HBM per device.

v0:
```python
import jax
import jax.numpy as jnp
from jax import lax
from jax.sharding import PartitionSpec as P


def local(integrals, inverses, lower_blocks):
    inv_all, low_all = (
        lax.all_gather(inverses, "aux", axis=1, tiled=True),
        lax.all_gather(lower_blocks, "aux", axis=1, tiled=True),
    )
    count = inv_all.shape[0]
    panel = inv_all.shape[1]
    width = integrals.shape[0]
    groups = lax.axis_size("aux")
    rows = integrals.shape[1] // groups
    sectioned = integrals.reshape(width, groups, rows)
    block = lax.all_to_all(sectioned, "aux", split_axis=1, concat_axis=0, tiled=True)
    columns = block.reshape(block.shape[0], block.shape[2])
    outs = []
    for k in range(count):
        acc = columns[k * panel : (k + 1) * panel].astype(jnp.float32)
        for j in range(k):
            acc = acc - jnp.dot(
                low_all[k * (k - 1) // 2 + j], outs[j], preferred_element_type=jnp.float32
            )
        rest = acc.astype(jnp.bfloat16)
        outs.append(
            jnp.dot(inv_all[k], rest, preferred_element_type=jnp.float32).astype(jnp.bfloat16)
        )
    return jnp.concatenate(outs, axis=0)


def solution(mesh):
    placed = (P("aux", "grp"), P(None, "aux", None), P(None, "aux", None))
    return jax.shard_map(
        local, mesh=mesh, in_specs=placed, out_specs=P(None, ("grp", "aux")), check_vma=False
    )
```

profile of v0, /device:TPU:1, one launch (start us, length us, event | category | flops | bytes accessed | tf_op | source)
XLA Modules:
  0.0 207.6 jit_solution(11446586706947685064)
XLA Ops:
  6.5 0.0 all-gather.3.cloned.1.call-start
  6.5 0.7 all-gather.3.cloned.1.call-update
  7.3 0.0 all-gather.5.cloned.1.call-start
  7.3 0.7 all-gather.5.cloned.1.call-update
  8.0 1.9 copy.17
  9.9 59.9 %all_to_all.15 = bf16[64,32,512]{2,0,1:T(8,128)(2,1)S(1)} all-to-all(bf16[64,32,512]{2,0,1:T(8,128)(2,1)S(1)} %bitcast.100), channel_id=1, replica_groups=mesh['grp'=16,'aux'=32] {'aux'}, dimensions={1} | all-to-all | bytes 4194304 | tf_op jit(solution)/shard_map/all_to_all | solution.py:18
  69.8 0.1 fusion.10
  69.9 0.2 bitcast_convert_fusion.2
  70.1 1.4 copy.12
  71.4 1.3 bitcast_convert_fusion
  72.8 0.3 copy.13
  73.1 1.6 copy.14
  74.7 25.2 %all-gather.3.cloned.1.call-done = bf16[4,512,512]{2,1,0:T(8,128)(2,1)} async-done(((bf16[4,16,512]{2,1,0:T(8,128)(2,1)}), bf16[4,512,512]{2,1,0:T(8,128)(2,1)}) %all-gather.3.cloned.1.call-update) | async-done | bytes 2097168 | tf_op jit(solution)/shard_map/all_gather | solution.py:9
  99.9 1.5 convolution_convert_fusion.3
  101.4 84.5 %all-gather.5.cloned.1.call-done = bf16[6,512,512]{2,1,0:T(8,128)(2,1)} async-done(((bf16[6,16,512]{2,1,0:T(8,128)(2,1)}), bf16[6,512,512]{2,1,0:T(8,128)(2,1)}) %all-gather.5.cloned.1.call-update) | async-done | bytes 3145744 | tf_op jit(solution)/shard_map/all_gather | solution.py:10
  185.9 2.4 %convolution_convert_fusion.2 = bf16[512,512]{0,1:T(8,128)(2,1)S(1)} fusion(f32[512,512]{0,1:T(8,128)} %copy.12, bf16[512,512]{1,0:T(8,128)(2,1)S(1)} %convolution_convert_fusion.3, bf16[4,512,512]{2,1,0:T(8,128)(2,1)} %all-gather.3.cloned.1.call-done, bf16[6,512,512]{2,1,0:T(8,128)(2,1)} %all-gather.5.cloned.1.call-done), kind=kOutput, calls=%fused_computation.16 | convolution fusion | flops 537657344 | bytes 3145728 | tf_op jit(solution)/shard_map/dot_general | solution.py:29
  188.2 2.5 %fusion.4 = f32[512,512]{0,1:T(8,128)} fusion(f32[512,512]{0,1:T(8,128)S(1)} %copy.13, bf16[512,512]{1,0:T(8,128)(2,1)S(1)} %convolution_convert_fusion.3, bf16[6,512,512]{2,1,0:T(8,128)(2,1)} %all-gather.5.cloned.1.call-done), kind=kOutput, calls=%fused_computation.11 | convolution fusion | flops 268697600 | bytes 3145728 | tf_op jit(solution)/shard_map/dot_general | solution.py:24
  190.7 1.5 fusion.2
  192.3 3.2 %convolution_convert_fusion.1 = bf16[512,512]{0,1:T(8,128)(2,1)} fusion(f32[512,512]{0,1:T(8,128)} %fusion.4, bf16[512,512]{0,1:T(8,128)(2,1)S(1)} %convolution_convert_fusion.2, bf16[4,512,512]{2,1,0:T(8,128)(2,1)} %all-gather.3.cloned.1.call-done, bf16[6,512,512]{2,1,0:T(8,128)(2,1)} %all-gather.5.cloned.1.call-done), kind=kOutput, calls=%fused_computation.15 | convolution fusion | flops 537657344 | bytes 3145728 | tf_op jit(solution)/shard_map/dot_general | solution.py:29
  195.5 1.5 fusion.1
  197.0 0.0 copy-start
  197.0 2.3 %fusion.9 = bf16[512,512]{1,0:T(8,128)(2,1)S(1)} fusion(f32[512,512]{0,1:T(8,128)S(1)} %fusion.1, bf16[512,512]{0,1:T(8,128)(2,1)} %convolution_convert_fusion.1, bf16[4,512,512]{2,1,0:T(8,128)(2,1)} %all-gather.3.cloned.1.call-done, bf16[6,512,512]{2,1,0:T(8,128)(2,1)} %all-gather.5.cloned.1.call-done), kind=kOutput, calls=%fused_computation.21 | convolution fusion | flops 537657344 | bytes 3145728 | tf_op jit(solution)/shard_map/dot_general | solution.py:29
  199.3 0.0 copy-done
  199.3 1.5 pad_maximum_fusion
Async XLA Ops:
  6.5 93.3 %all-gather.3.cloned.1.call-start = ((), (), s32[]{:S(2)}) async-start(), calls=%async_computation.1 | async-start | bytes 2162688 | tf_op jit(solution)/shard_map/all_gather | solution.py:9
  7.3 178.6 %all-gather.5.cloned.1.call-start = ((), (), s32[]{:S(2)}) async-start(), calls=%async_computation.2 | async-start | bytes 3244032 | tf_op jit(solution)/shard_map/all_gather | solution.py:10
  197.0 2.3 %copy-start = (bf16[512,512]{0,1:T(8,128)(2,1)S(1)}, bf16[512,512]{0,1:T(8,128)(2,1)}, u32[]{:S(2)}) copy-start(bf16[512,512]{0,1:T(8,128)(2,1)} %convolution_convert_fusion.1) | copy-start | bytes 1572868
Sparse Core Ops, SparseCore 0:
  10.5 89.3 all-gather.2
  103.0 82.7 all-gather.4
where the time goes:
time: 210 us; the launch traced here: 208 us
  waiting for transfers between devices  111 us (53%)
  blocking collectives  59.9 us (29%)
  matrix products  14.8 us (7%)
  between operations  13.5 us (6%)
  local copies, waits for them, and re-layouts  5.24 us (2%)
  other arithmetic  2.94 us (1%)
    all_gather x1, waiting for transfers between devices, local(): lax.all_gather(lower_blocks, 'aux', axis=1, tiled=True)  84.5 us
    all_to_all x1, blocking collectives, local(): lax.all_to_all(sectioned, 'aux', split_axis=1, concat_axis=0, tiled=True)  59.9 us
    all_gather x1, waiting for transfers between devices, local(): lax.all_gather(inverses, 'aux', axis=1, tiled=True)  25.2 us
    dot_general x4, matrix products, local(): jnp.dot(inv_all[k], rest, preferred_element_type=jnp.float32)  9.29 us
    dot_general x3, matrix products, local(): jnp.dot(low_all[k * (k - 1) // 2 + j], outs[j], preferred_element_type=jn...  5.55 us
  transfers between devices with their start and end apart: 2, of which 2 were waited for; matrix products, arithmetic and copies ran while one was open for 4% of the time, Pallas kernels for 0%

commit v1 on v0

v1 whole, which is shorter than its diff:
```python
import functools

import jax
import jax.numpy as jnp
from jax import lax
from jax.experimental import pallas as pl
from jax.experimental.pallas import tpu as pltpu
from jax.sharding import Mesh, PartitionSpec as P

NX, NY = 4, 8
EARLY = 128
ANY = pl.BlockSpec(memory_space=pl.ANY)
VMEM = pl.BlockSpec(memory_space=pltpu.VMEM)


def run_all(copies):
    for copy in copies:
        copy.start()
    for copy in copies:
        copy.wait()


def pack_first(integrals, inverses, lower_blocks, first, sems):
    x, core = lax.axis_index("x"), lax.axis_index("core")
    width = integrals.shape[2] // (NX * NY)
    copies = []
    for y in range(NY):
        for s in range(NX):
            at = pl.multiple_of(lax.rem(x + s, NX) * (NY * width) + y * width, 128)
            copies.append(
                pltpu.make_async_copy(
                    integrals.at[:, :, pl.ds(at, EARLY)],
                    first.at[y, 0:4, :, s * EARLY : (s + 1) * EARLY],
                    sems.at[len(copies)],
                )
            )
    count = len(copies)
    for copy in copies:
        copy.start()

    @pl.when(core == 0)
    def _():
        mine = []
        for y in range(NY):
            mine.append(
                pltpu.make_async_copy(inverses, first.at[y, 4:8], sems.at[count + 2 * y])
            )
            mine.append(
                pltpu.make_async_copy(
                    lower_blocks.at[0:1], first.at[y, 8:9], sems.at[count + 2 * y + 1]
                )
            )
        run_all(mine)

    @pl.when(core == 1)
    def _():
        run_all(
            [
                pltpu.make_async_copy(
                    lower_blocks.at[1:6], first.at[y, 4:9], sems.at[count + 2 * y]
                )
                for y in range(NY)
            ]
        )

    for copy in copies:
        copy.wait()


def pack_late(integrals, s0, s1, s2, s3, sems):
    x = lax.axis_index("x")
    width = integrals.shape[1] // (NX * NY)
    copies = []
    for s, slab in ((1, s1), (3, s3), (2, s2), (0, s0)):
        for y in range(NY):
            at = pl.multiple_of(
                lax.rem(x + s, NX) * (NY * width) + y * width + EARLY, 128
            )
            copies.append(
                pltpu.make_async_copy(
                    integrals.at[:, pl.ds(at, width - EARLY)],
                    slab.at[y],
                    sems.at[len(copies)],
                )
            )
    run_all(copies)


def assemble(*refs):
    own, other, early = refs[0:4], refs[4:8], refs[8:12]
    factor, columns, sems = refs[12:]
    x, core = lax.axis_index("x"), lax.axis_index("core")
    copies = []
    for s in range(NX):
        source = lax.rem(x + NX - s, NX)
        for pieces, half in ((own, core), (other, 1 - core)):
            for y in range(NY):
                row = pl.multiple_of(source * 128 + y * 16, 16)
                copies.append(
                    pltpu.make_async_copy(
                        pieces[s].at[y],
                        factor.at[half, :, pl.ds(row, 16), :],
                        sems.at[len(copies)],
                    )
                )
        copies.append(
            pltpu.make_async_copy(early[s], columns.at[source], sems.at[len(copies)])
        )
    run_all(copies)


def solve(factor, early, late, out, held, sems):
    x = lax.axis_index("x")
    solved = []
    copies = []
    for k in range(4):
        slot = lax.rem(x + NX - k, NX)
        acc = jnp.concatenate(
            [
                early[k].reshape(512, EARLY),
                late[:, slot].reshape(512, 512 - EARLY),
            ],
            axis=1,
        ).astype(jnp.float32)
        for j in range(k):
            acc = acc - jnp.dot(
                factor[4 + k * (k - 1) // 2 + j],
                held[j],
                preferred_element_type=jnp.float32,
            )
        held[k] = jnp.dot(
            factor[k], acc.astype(jnp.bfloat16), preferred_element_type=jnp.float32
        ).astype(jnp.bfloat16)
        copies.append(
            pltpu.make_async_copy(
                held.at[k], out.at[k * 512 : (k + 1) * 512], sems.at[k]
            )
        )
        copies[-1].start()
    for copy in copies:
        copy.wait()


def cost(flops, moved):
    return pl.CostEstimate(flops=flops, bytes_accessed=moved, transcendentals=0)


def ring(count, shift):
    return [(i, (i + shift) % count) for i in range(count)]


def local(integrals, inverses, lower_blocks):
    rows, total = integrals.shape
    width = total // (NX * NY)
    bf16 = jnp.bfloat16
    late_width = width - EARLY

    first = pl.pallas_call(
        pack_first,
        out_shape=jax.ShapeDtypeStruct((NY, 9, 16, width), bf16),
        in_specs=[ANY] * 3,
        out_specs=ANY,
        scratch_shapes=[pltpu.SemaphoreType.DMA((NX * NY + 2 * NY,))],
        cost_estimate=cost(0, 3 << 20),
    )(integrals.reshape(4, 16, total), inverses, lower_blocks)
    first = lax.all_to_all(first, "y", 0, 0, tiled=True)

    slabs = pl.pallas_call(
        pack_late,
        out_shape=[jax.ShapeDtypeStruct((NY, rows, late_width), bf16)] * NX,
        in_specs=[ANY],
        out_specs=[ANY] * NX,
        scratch_shapes=[pltpu.SemaphoreType.DMA((NX * NY,))],
        cost_estimate=cost(0, 3 << 20),
    )(integrals)
    moved = {0: slabs[0]}
    for s in (1, 3, 2):
        moved[s] = lax.ppermute(slabs[s], "x", ring(NX, s))
    late = jnp.stack([moved[s] for s in range(NX)], axis=1)
    late = lax.all_to_all(late, "y", 0, 0, tiled=True)

    own = {0: first[:, 4:9]}
    for s in (1, 3, 2):
        own[s] = lax.ppermute(own[0], "x", ring(NX, s))
    other = {s: lax.ppermute(own[s], "core", ring(2, 1)) for s in range(NX)}
    early = {
        s: first[:, 0:4, :, s * EARLY : (s + 1) * EARLY] for s in range(NX)
    }
    for s in (1, 3, 2):
        early[s] = lax.ppermute(early[s], "x", ring(NX, s))

    factor, columns = pl.pallas_call(
        assemble,
        out_shape=[
            jax.ShapeDtypeStruct((2, 5, 512, 512), bf16),
            jax.ShapeDtypeStruct((NX, NY, 4, 16, EARLY), bf16),
        ],
        in_specs=[ANY] * (3 * NX),
        out_specs=[ANY] * 2,
        scratch_shapes=[pltpu.SemaphoreType.DMA((NX * (2 * NY + 1),))],
        cost_estimate=cost(0, 11 << 20),
    )(*[d[s] for d in (own, other, early) for s in range(NX)])

    return pl.pallas_call(
        solve,
        out_shape=jax.ShapeDtypeStruct((4 * 512, width), bf16),
        in_specs=[VMEM] * 3,
        out_specs=ANY,
        scratch_shapes=[
            pltpu.VMEM((4, 512, width), bf16),
            pltpu.SemaphoreType.DMA((4,)),
        ],
        compiler_params=pltpu.CompilerParams(vmem_limit_bytes=32 << 20),
        cost_estimate=cost(20 * 512**3, 9 << 20),
    )(factor.reshape(10, 512, 512), columns, late)


def solution(mesh):
    fine = Mesh(mesh.devices.reshape(8, 2, NX, NY), ("z", "core", "x", "y"))
    aux, grp = ("x", "y"), ("z", "core")
    placed = (P(aux, grp), P(None, aux, None), P(None, aux, None))
    return jax.shard_map(
        local,
        mesh=fine,
        in_specs=placed,
        out_specs=P(None, grp + aux),
        check_vma=False,
    )
```

time: 210 us -> 380 us (1.81)
  Pallas kernels: 0 us -> 267 us
  waiting for transfers between devices: 111 us -> 40.1 us
  starting transfers between devices: 0.04 us -> 61 us
  blocking collectives: 59.9 us -> 0 us
  matrix products: 14.8 us -> 0 us
  between operations: 13.5 us -> 0.26 us
    pallas_call x0 -> x4, Pallas kernels: none -> 267 us  [the longest x1 176 us: local(): pl.pallas_call(assemble, out_shape=[jax.ShapeDtypeStruct((2, 5, 512, 512)...]
    all_gather x2 -> x0, waiting for transfers between devices: 110 us -> none  [the longest x1 84.5 us: local(): lax.all_gather(lower_blocks, 'aux', axis=1, tiled=True)]
    all_to_all x1 -> x0, blocking collectives: 59.9 us -> none  [local(): lax.all_to_all(sectioned, 'aux', split_axis=1, concat_axis=0, tiled=True)]
    ppermute x0 -> x13, starting transfers between devices: none -> 47 us  [the longest x4 15.6 us: local(): other = {s: lax.ppermute(own[s], 'core', ring(2, 1)) for s in range(NX)}]
    ppermute x0 -> x13, waiting for transfers between devices: none -> 40.1 us  [the longest x3 14.8 us: local(): own[s] = lax.ppermute(own[0], 'x', ring(NX, s))]
    dot_general x7 -> x0, matrix products: 14.8 us -> none  [the longest x4 9.29 us: local(): jnp.dot(inv_all[k], rest, preferred_element_type=jnp.float32)]
    all_to_all x0 -> x2, starting transfers between devices: none -> 14.1 us  [the longest x1 7.66 us: local(): first = lax.all_to_all(first, 'y', 0, 0, tiled=True)]
    unnamed x2 -> x26, local copies, waits for them, and re-layouts: 0.01 us -> 5.7 us
  transfers between devices with their start and end apart: 2 -> 15, of which waited for: 2 -> 8; matrix products, arithmetic and copies ran while one was open for 4% -> 1% of each run, Pallas kernels for 0% -> 60%
where the time goes in v1:
time: 380 us; the launch traced here: 377 us
  Pallas kernels  267 us (70%)
  starting transfers between devices  61 us (16%)
  waiting for transfers between devices  40.1 us (11%)
  local copies, waits for them, and re-layouts  6.51 us (2%)
    pallas_call x1, Pallas kernels, local(): pl.pallas_call(assemble, out_shape=[jax.ShapeDtypeStruct((2, 5, 512, 512)...  176 us
    pallas_call x1, Pallas kernels, local(): pl.pallas_call(pack_late, out_shape=[jax.ShapeDtypeStruct((NY, rows, late...  49 us
    pallas_call x1, Pallas kernels, local(): pl.pallas_call(pack_first, out_shape=jax.ShapeDtypeStruct((NY, 9, 16, wid...  37.3 us
    ppermute x4, starting transfers between devices, local(): other = {s: lax.ppermute(own[s], 'core', ring(2, 1)) for s in range(NX)}  15.6 us
    ppermute x3, waiting for transfers between devices, local(): own[s] = lax.ppermute(own[0], 'x', ring(NX, s))  14.8 us
    ppermute x3, waiting for transfers between devices, local(): moved[s] = lax.ppermute(slabs[s], 'x', ring(NX, s))  13.4 us
    ppermute x3, waiting for transfers between devices, local(): early[s] = lax.ppermute(early[s], 'x', ring(NX, s))  11.9 us
    ppermute x3, starting transfers between devices, local(): own[s] = lax.ppermute(own[0], 'x', ring(NX, s))  11.2 us
  transfers between devices with their start and end apart: 15, of which 8 were waited for; matrix products, arithmetic and copies ran while one was open for 1% of the time, Pallas kernels for 60%

profile of v1, /device:TPU:1, one launch (start us, length us, event | category | flops | bytes accessed | tf_op | source)
XLA Modules:
  0.0 377.1 jit_solution(15878093981536319625)
XLA Ops:
  0.0 37.3 %shard_map.37 = bf16[8,9,16,512]{3,2,1,0:T(8,128)(2,1)} custom-call(bf16[4,16,16384]{2,1,0:T(8,128)(2,1)} %bitcast.7, bf16[4,16,512]{2,1,0:T(8,128)(2,1)} %inverses.1, bf16[6,16,512]{2,1,0:T(8,128)(2,1)} %lower_blocks.1), custom_call_target="tpu_custom_call" | custom-call | bytes 3145728 | tf_op jit(solution)/shard_map/pallas_call | solution.py:158
  37.3 7.7 %all-to-all-start = ((bf16[8,9,16,512]{3,2,1,0:T(8,128)(2,1)}), bf16[8,9,16,512]{3,2,1,0:T(8,128)(2,1)S(1)}, u32[]{:S(2)}, u32[]{:S(2)}) async-start(bf16[8,9,16,512]{3,2,1,0:T(8,128)(2,1)} %shard_map.37), calls=%async_computation | async-start | bytes 2359296 | tf_op jit(solution)/shard_map/all_to_all | solution.py:166
  45.0 49.0 %shard_map.39 = (bf16[8,64,384]{2,1,0:T(8,128)(2,1)}, bf16[8,64,384]{2,1,0:T(8,128)(2,1)}, bf16[8,64,384]{2,1,0:T(8,128)(2,1)}, bf16[8,64,384]{2,1,0:T(8,128)(2,1)}) custom-call(bf16[64,16384]{1,0:T(8,128)(2,1)} %integrals.1), custom_call_target="tpu_custom_call" | custom-call | bytes 3145728 | tf_op jit(solution)/shard_map/pallas_call | solution.py:168
  94.0 3.1 collective-permute-start.10
  97.2 4.4 %collective-permute-start.11 = (bf16[8,64,384]{2,1,0:T(8,128)(2,1)}, bf16[8,64,384]{2,1,0:T(8,128)(2,1)S(1)}, u32[]{:S(2)}, u32[]{:S(2)}) collective-permute-start(bf16[8,64,384]{2,1,0:T(8,128)(2,1)} %get-tuple-element.15), channel_id=1, source_target_pairs={{0,16},{8,24},{16,0},{24,8},{1,17},{9,25},{17,1},{25,9},{2,18},{10... | collective-permute-start | bytes 1179656 | tf_op jit(solution)/shard_map/ppermute | solution.py:178
  101.5 3.1 collective-permute-start.12
  104.6 0.5 collective-permute-done.10
  105.1 11.3 %collective-permute-done.11 = bf16[8,64,384]{2,1,0:T(8,128)(2,1)S(1)} collective-permute-done((bf16[8,64,384]{2,1,0:T(8,128)(2,1)}, bf16[8,64,384]{2,1,0:T(8,128)(2,1)S(1)}, u32[]{:S(2)}, u32[]{:S(2)}) %collective-permute-start.11) | collective-permute-done | bytes 393248 | tf_op jit(solution)/shard_map/ppermute | solution.py:178
  116.4 1.5 collective-permute-done.12
  117.9 2.4 pad_maximum_fusion
  120.3 0.0 all-to-all-done
  120.3 6.4 %all-to-all-start.1 = ((bf16[8,4,64,384]{3,2,1,0:T(8,128)(2,1)}), bf16[8,4,64,384]{3,2,1,0:T(8,128)(2,1)S(1)}, u32[]{:S(2)}, u32[]{:S(2)}) async-start(bf16[8,4,64,384]{3,2,1,0:T(8,128)(2,1)} %pad_maximum_fusion), calls=%async_computation.1 | async-start | bytes 3145728 | tf_op jit(solution)/shard_map/all_to_all | solution.py:180
  126.8 0.0 copy-start.2
  126.8 5.2 %collective-permute-start.2 = (bf16[8,5,16,512]{3,2,1,0:T(8,128)(2,1)S(1)}, bf16[8,5,16,512]{3,2,1,0:T(8,128)(2,1)S(1)}, u32[]{:S(2)}, u32[]{:S(2)}) collective-permute-start(bf16[8,5,16,512]{3,2,1,0:T(8,128)(2,1)S(1)} %slice.20.refs_0_), channel_id=1, source_target_pairs={{0,24},{8,0},{16,8},{24,16},{1,25},{9,1},{17,9},{25,17},{2,26},{10... | collective-permute-start | bytes 1966088 | tf_op jit(solution)/shard_map/ppermute | solution.py:184
  132.0 4.1 %collective-permute-start.1 = (bf16[8,5,16,512]{3,2,1,0:T(8,128)(2,1)S(1)}, bf16[8,5,16,512]{3,2,1,0:T(8,128)(2,1)S(1)}, u32[]{:S(2)}, u32[]{:S(2)}) collective-permute-start(bf16[8,5,16,512]{3,2,1,0:T(8,128)(2,1)S(1)} %slice.20.refs_0_), channel_id=1, source_target_pairs={{0,16},{8,24},{16,0},{24,8},{1,17},{9,25},{17,1},{25,9},{2,18},{10... | collective-permute-start | bytes 1966088 | tf_op jit(solution)/shard_map/ppermute | solution.py:184
  136.1 1.9 collective-permute-start
  138.1 3.2 collective-permute-start.3
  141.3 5.5 %collective-permute-done.2.refs_3_ = bf16[8,5,16,512]{3,2,1,0:T(8,128)(2,1)S(1)} collective-permute-done((bf16[8,5,16,512]{3,2,1,0:T(8,128)(2,1)S(1)}, bf16[8,5,16,512]{3,2,1,0:T(8,128)(2,1)S(1)}, u32[]{:S(2)}, u32[]{:S(2)}) %collective-permute-start.2) | collective-permute-done | bytes 655392 | tf_op jit(solution)/shard_map/ppermute | solution.py:184
  146.8 0.0 copy-start.3
  146.8 4.2 %collective-permute-start.6 = (bf16[8,5,16,512]{3,2,1,0:T(8,128)(2,1)S(1)}, bf16[8,5,16,512]{3,2,1,0:T(8,128)(2,1)S(1)}, u32[]{:S(2)}, u32[]{:S(2)}) collective-permute-start(bf16[8,5,16,512]{3,2,1,0:T(8,128)(2,1)S(1)} %collective-permute-done.2.refs_3_), channel_id=1, source_target_pairs={{0,32},{32,0},{1,33},{33,1},{2,34},{34,2},{3,35},{35,3},{4,36},{36... | collective-permute-start | bytes 1966088 | tf_op jit(solution)/shard_map/ppermute | solution.py:185
  150.9 0.0 collective-permute-done.1.refs_2_
  151.0 0.0 copy-start.4
  151.0 5.8 %collective-permute-start.5 = (bf16[8,5,16,512]{3,2,1,0:T(8,128)(2,1)S(1)}, bf16[8,5,16,512]{3,2,1,0:T(8,128)(2,1)S(1)}, u32[]{:S(2)}, u32[]{:S(2)}) collective-permute-start(bf16[8,5,16,512]{3,2,1,0:T(8,128)(2,1)S(1)} %collective-permute-done.1.refs_2_), channel_id=1, source_target_pairs={{0,32},{32,0},{1,33},{33,1},{2,34},{34,2},{3,35},{35,3},{4,36},{36... | collective-permute-start | bytes 1966088 | tf_op jit(solution)/shard_map/ppermute | solution.py:185
  156.8 9.4 %collective-permute-done.refs_1_ = bf16[8,5,16,512]{3,2,1,0:T(8,128)(2,1)S(1)} collective-permute-done((bf16[8,5,16,512]{3,2,1,0:T(8,128)(2,1)S(1)}, bf16[8,5,16,512]{3,2,1,0:T(8,128)(2,1)S(1)}, u32[]{:S(2)}, u32[]{:S(2)}) %collective-permute-start) | collective-permute-done | bytes 655392 | tf_op jit(solution)/shard_map/ppermute | solution.py:184
  166.1 0.0 copy-start.5
  166.1 2.4 collective-permute-start.4
  168.5 0.8 fusion
  169.3 2.2 collective-permute-start.9
  171.5 4.8 %collective-permute-done.9.refs_11_ = bf16[8,4,16,128]{3,2,1,0:T(8,128)(2,1)S(1)} collective-permute-done((bf16[8,4,16,128]{3,2,1,0:T(8,128)(2,1)S(1)}, bf16[8,4,16,128]{3,2,1,0:T(8,128)(2,1)S(1)}, u32[]{:S(2)}, u32[]{:S(2)}) %collective-permute-start.9) | collective-permute-done | bytes 131104 | tf_op jit(solution)/shard_map/ppermute | solution.py:190
  176.3 0.0 copy-start.10
  176.3 4.1 %collective-permute-start.8 = (bf16[8,4,16,128]{3,2,1,0:T(8,128)(2,1)S(1)}, bf16[8,4,16,128]{3,2,1,0:T(8,128)(2,1)S(1)}, u32[]{:S(2)}, u32[]{:S(2)}) collective-permute-start(bf16[8,4,16,128]{3,2,1,0:T(8,128)(2,1)S(1)} %get-tuple-element.18), channel_id=1, source_target_pairs={{0,16},{8,24},{16,0},{24,8},{1,17},{9,25},{17,1},{25,9},{2,18},{10... | collective-permute-start | bytes 393224 | tf_op jit(solution)/shard_map/ppermute | solution.py:190
  180.4 3.5 collective-permute-done.8.refs_10_
  183.9 0.0 copy-start.11
  183.9 3.3 collective-permute-start.7
  187.2 3.6 collective-permute-done.7.refs_9_
  190.8 0.0 copy-start.12
  190.8 0.0 collective-permute-done.3.refs_4_
  190.8 0.0 copy-done.3
  190.8 0.0 copy-start.6
  190.8 0.0 collective-permute-done.6.refs_7_
  190.8 0.0 copy-done.4
  190.9 0.0 copy-start.7
  190.9 0.0 collective-permute-done.5.refs_6_
  190.9 0.0 copy-done.5
  190.9 0.0 copy-start.8
  190.9 0.0 collective-permute-done.4.refs_5_
  190.9 0.9 copy-done.6
  191.8 0.2 copy-done.7
  192.0 0.2 copy-done.8
  192.2 0.0 copy-start.9
  192.2 0.9 copy-done.9
  193.1 0.0 copy-done.2
  193.1 0.0 copy-done.10
  193.1 0.0 copy-done.11
  193.1 0.0 copy-done.12
  193.1 176.4 %shard_map.38 = (bf16[2,5,512,512]{3,2,1,0:T(8,128)(2,1)}, bf16[4,8,4,16,128]{4,3,2,1,0:T(8,128)(2,1)}) custom-call(bf16[8,5,16,512]{3,2,1,0:T(8,128)(2,1)} %copy-done.2, bf16[8,5,16,512]{3,2,1,0:T(8,128)(2,1)} %copy-done.5, bf16[8,5,16,512]{3,2,1,0:T(8,128)(2,1)} %copy-done.4, bf16[8,5,16,512]{3,2,1,0:T(8,128)(2,1)} %copy-done.3, ...), custom_call_target="tpu_custom_call" | custom-call | bytes 11534336 | tf_op jit(solution)/shard_map/pallas_call | solution.py:192
  369.5 0.0 all-to-all-done.1.late
  369.5 0.0 copy-start
  369.5 2.5 copy-done
  372.0 0.0 copy-start.1
  372.0 1.0 copy-done.1
  373.1 4.0 %shard_map.40 = bf16[2048,512]{1,0:T(8,128)(2,1)} custom-call(bf16[10,512,512]{2,1,0:T(8,128)(2,1)S(1)} %bitcast.6, bf16[4,8,4,16,128]{4,3,2,1,0:T(8,128)(2,1)S(1)} %copy-done.1, bf16[8,4,64,384]{3,2,1,0:T(8,128)(2,1)S(1)} %all-to-all-done.1.late), custom_call_target="tpu_custom_call" | custom-call | flops 2684354560 | bytes 9437184 | tf_op jit(solution)/shard_map/pallas_call | solution.py:204
  (1 shorter events, 0.0 us)
Async XLA Ops:
  37.3 83.0 %all-to-all-start = ((bf16[8,9,16,512]{3,2,1,0:T(8,128)(2,1)}), bf16[8,9,16,512]{3,2,1,0:T(8,128)(2,1)S(1)}, u32[]{:S(2)}, u32[]{:S(2)}) async-start(bf16[8,9,16,512]{3,2,1,0:T(8,128)(2,1)} %shard_map.37), calls=%async_computation | async-start | bytes 2359296 | tf_op jit(solution)/shard_map/all_to_all | solution.py:166
  94.0 11.1 %collective-permute-start.10 = (bf16[8,64,384]{2,1,0:T(8,128)(2,1)}, bf16[8,64,384]{2,1,0:T(8,128)(2,1)S(1)}, u32[]{:S(2)}, u32[]{:S(2)}) collective-permute-start(bf16[8,64,384]{2,1,0:T(8,128)(2,1)} %get-tuple-element.14), channel_id=1, source_target_pairs={{0,8},{8,16},{16,24},{24,0},{1,9},{9,17},{17,25},{25,1},{2,10},{10... | collective-permute-start | bytes 1179656 | tf_op jit(solution)/shard_map/ppermute | solution.py:178
  97.2 19.3 %collective-permute-start.11 = (bf16[8,64,384]{2,1,0:T(8,128)(2,1)}, bf16[8,64,384]{2,1,0:T(8,128)(2,1)S(1)}, u32[]{:S(2)}, u32[]{:S(2)}) collective-permute-start(bf16[8,64,384]{2,1,0:T(8,128)(2,1)} %get-tuple-element.15), channel_id=1, source_target_pairs={{0,16},{8,24},{16,0},{24,8},{1,17},{9,25},{17,1},{25,9},{2,18},{10... | collective-permute-start | bytes 1179656 | tf_op jit(solution)/shard_map/ppermute | solution.py:178
  101.5 16.4 %collective-permute-start.12 = (bf16[8,64,384]{2,1,0:T(8,128)(2,1)}, bf16[8,64,384]{2,1,0:T(8,128)(2,1)S(1)}, u32[]{:S(2)}, u32[]{:S(2)}) collective-permute-start(bf16[8,64,384]{2,1,0:T(8,128)(2,1)} %get-tuple-element.16), channel_id=1, source_target_pairs={{0,24},{8,0},{16,8},{24,16},{1,25},{9,1},{17,9},{25,17},{2,26},{10... | collective-permute-start | bytes 1179656 | tf_op jit(solution)/shard_map/ppermute | solution.py:178
  120.3 249.2 %all-to-all-start.1 = ((bf16[8,4,64,384]{3,2,1,0:T(8,128)(2,1)}), bf16[8,4,64,384]{3,2,1,0:T(8,128)(2,1)S(1)}, u32[]{:S(2)}, u32[]{:S(2)}) async-start(bf16[8,4,64,384]{3,2,1,0:T(8,128)(2,1)} %pad_maximum_fusion), calls=%async_computation.1 | async-start | bytes 3145728 | tf_op jit(solution)/shard_map/all_to_all | solution.py:180
  126.8 66.3 %copy-start.2 = (bf16[8,5,16,512]{3,2,1,0:T(8,128)(2,1)}, bf16[8,5,16,512]{3,2,1,0:T(8,128)(2,1)S(1)}, u32[]{:S(2)}) copy-start(bf16[8,5,16,512]{3,2,1,0:T(8,128)(2,1)S(1)} %slice.20.refs_0_) | copy-start | bytes 1966084
  126.8 20.0 %collective-permute-start.2 = (bf16[8,5,16,512]{3,2,1,0:T(8,128)(2,1)S(1)}, bf16[8,5,16,512]{3,2,1,0:T(8,128)(2,1)S(1)}, u32[]{:S(2)}, u32[]{:S(2)}) collective-permute-start(bf16[8,5,16,512]{3,2,1,0:T(8,128)(2,1)S(1)} %slice.20.refs_0_), channel_id=1, source_target_pairs={{0,24},{8,0},{16,8},{24,16},{1,25},{9,1},{17,9},{25,17},{2,26},{10... | collective-permute-start | bytes 1966088 | tf_op jit(solution)/shard_map/ppermute | solution.py:184
  132.0 18.9 %collective-permute-start.1 = (bf16[8,5,16,512]{3,2,1,0:T(8,128)(2,1)S(1)}, bf16[8,5,16,512]{3,2,1,0:T(8,128)(2,1)S(1)}, u32[]{:S(2)}, u32[]{:S(2)}) collective-permute-start(bf16[8,5,16,512]{3,2,1,0:T(8,128)(2,1)S(1)} %slice.20.refs_0_), channel_id=1, source_target_pairs={{0,16},{8,24},{16,0},{24,8},{1,17},{9,25},{17,1},{25,9},{2,18},{10... | collective-permute-start | bytes 1966088 | tf_op jit(solution)/shard_map/ppermute | solution.py:184
  136.1 30.0 %collective-permute-start = (bf16[8,5,16,512]{3,2,1,0:T(8,128)(2,1)S(1)}, bf16[8,5,16,512]{3,2,1,0:T(8,128)(2,1)S(1)}, u32[]{:S(2)}, u32[]{:S(2)}) collective-permute-start(bf16[8,5,16,512]{3,2,1,0:T(8,128)(2,1)S(1)} %slice.20.refs_0_), channel_id=1, source_target_pairs={{0,8},{8,16},{16,24},{24,0},{1,9},{9,17},{17,25},{25,1},{2,10},{10... | collective-permute-start | bytes 1966088 | tf_op jit(solution)/shard_map/ppermute | solution.py:184
  138.1 52.8 %collective-permute-start.3 = (bf16[8,5,16,512]{3,2,1,0:T(8,128)(2,1)S(1)}, bf16[8,5,16,512]{3,2,1,0:T(8,128)(2,1)S(1)}, u32[]{:S(2)}, u32[]{:S(2)}) collective-permute-start(bf16[8,5,16,512]{3,2,1,0:T(8,128)(2,1)S(1)} %slice.20.refs_0_), channel_id=1, source_target_pairs={{0,32},{32,0},{1,33},{33,1},{2,34},{34,2},{3,35},{35,3},{4,36},{36... | collective-permute-start | bytes 1966088 | tf_op jit(solution)/shard_map/ppermute | solution.py:185
  146.8 44.1 %copy-start.3 = (bf16[8,5,16,512]{3,2,1,0:T(8,128)(2,1)}, bf16[8,5,16,512]{3,2,1,0:T(8,128)(2,1)S(1)}, u32[]{:S(2)}) copy-start(bf16[8,5,16,512]{3,2,1,0:T(8,128)(2,1)S(1)} %collective-permute-done.2.refs_3_) | copy-start | bytes 1966084
  146.8 44.1 %collective-permute-start.6 = (bf16[8,5,16,512]{3,2,1,0:T(8,128)(2,1)S(1)}, bf16[8,5,16,512]{3,2,1,0:T(8,128)(2,1)S(1)}, u32[]{:S(2)}, u32[]{:S(2)}) collective-permute-start(bf16[8,5,16,512]{3,2,1,0:T(8,128)(2,1)S(1)} %collective-permute-done.2.refs_3_), channel_id=1, source_target_pairs={{0,32},{32,0},{1,33},{33,1},{2,34},{34,2},{3,35},{35,3},{4,36},{36... | collective-permute-start | bytes 1966088 | tf_op jit(solution)/shard_map/ppermute | solution.py:185
  151.0 39.9 %copy-start.4 = (bf16[8,5,16,512]{3,2,1,0:T(8,128)(2,1)}, bf16[8,5,16,512]{3,2,1,0:T(8,128)(2,1)S(1)}, u32[]{:S(2)}) copy-start(bf16[8,5,16,512]{3,2,1,0:T(8,128)(2,1)S(1)} %collective-permute-done.1.refs_2_) | copy-start | bytes 1966084
  151.0 39.9 %collective-permute-start.5 = (bf16[8,5,16,512]{3,2,1,0:T(8,128)(2,1)S(1)}, bf16[8,5,16,512]{3,2,1,0:T(8,128)(2,1)S(1)}, u32[]{:S(2)}, u32[]{:S(2)}) collective-permute-start(bf16[8,5,16,512]{3,2,1,0:T(8,128)(2,1)S(1)} %collective-permute-done.1.refs_2_), channel_id=1, source_target_pairs={{0,32},{32,0},{1,33},{33,1},{2,34},{34,2},{3,35},{35,3},{4,36},{36... | collective-permute-start | bytes 1966088 | tf_op jit(solution)/shard_map/ppermute | solution.py:185
  166.1 24.8 %copy-start.5 = (bf16[8,5,16,512]{3,2,1,0:T(8,128)(2,1)}, bf16[8,5,16,512]{3,2,1,0:T(8,128)(2,1)S(1)}, u32[]{:S(2)}) copy-start(bf16[8,5,16,512]{3,2,1,0:T(8,128)(2,1)S(1)} %collective-permute-done.refs_1_) | copy-start | bytes 1966084
  166.1 24.8 %collective-permute-start.4 = (bf16[8,5,16,512]{3,2,1,0:T(8,128)(2,1)S(1)}, bf16[8,5,16,512]{3,2,1,0:T(8,128)(2,1)S(1)}, u32[]{:S(2)}, u32[]{:S(2)}) collective-permute-start(bf16[8,5,16,512]{3,2,1,0:T(8,128)(2,1)S(1)} %collective-permute-done.refs_1_), channel_id=1, source_target_pairs={{0,32},{32,0},{1,33},{33,1},{2,34},{34,2},{3,35},{35,3},{4,36},{36... | collective-permute-start | bytes 1966088 | tf_op jit(solution)/shard_map/ppermute | solution.py:185
  169.3 7.0 %collective-permute-start.9 = (bf16[8,4,16,128]{3,2,1,0:T(8,128)(2,1)S(1)}, bf16[8,4,16,128]{3,2,1,0:T(8,128)(2,1)S(1)}, u32[]{:S(2)}, u32[]{:S(2)}) collective-permute-start(bf16[8,4,16,128]{3,2,1,0:T(8,128)(2,1)S(1)} %get-tuple-element.17), channel_id=1, source_target_pairs={{0,24},{8,0},{16,8},{24,16},{1,25},{9,1},{17,9},{25,17},{2,26},{10... | collective-permute-start | bytes 393224 | tf_op jit(solution)/shard_map/ppermute | solution.py:190
  176.3 16.8 %copy-start.10 = (bf16[8,4,16,128]{3,2,1,0:T(8,128)(2,1)}, bf16[8,4,16,128]{3,2,1,0:T(8,128)(2,1)S(1)}, u32[]{:S(2)}) copy-start(bf16[8,4,16,128]{3,2,1,0:T(8,128)(2,1)S(1)} %collective-permute-done.9.refs_11_) | copy-start | bytes 393220
  176.3 7.6 %collective-permute-start.8 = (bf16[8,4,16,128]{3,2,1,0:T(8,128)(2,1)S(1)}, bf16[8,4,16,128]{3,2,1,0:T(8,128)(2,1)S(1)}, u32[]{:S(2)}, u32[]{:S(2)}) collective-permute-start(bf16[8,4,16,128]{3,2,1,0:T(8,128)(2,1)S(1)} %get-tuple-element.18), channel_id=1, source_target_pairs={{0,16},{8,24},{16,0},{24,8},{1,17},{9,25},{17,1},{25,9},{2,18},{10... | collective-permute-start | bytes 393224 | tf_op jit(solution)/shard_map/ppermute | solution.py:190
  183.9 9.2 %copy-start.11 = (bf16[8,4,16,128]{3,2,1,0:T(8,128)(2,1)}, bf16[8,4,16,128]{3,2,1,0:T(8,128)(2,1)S(1)}, u32[]{:S(2)}) copy-start(bf16[8,4,16,128]{3,2,1,0:T(8,128)(2,1)S(1)} %collective-permute-done.8.refs_10_) | copy-start | bytes 393220
  183.9 6.9 %collective-permute-start.7 = (bf16[8,4,16,128]{3,2,1,0:T(8,128)(2,1)S(1)}, bf16[8,4,16,128]{3,2,1,0:T(8,128)(2,1)S(1)}, u32[]{:S(2)}, u32[]{:S(2)}) collective-permute-start(bf16[8,4,16,128]{3,2,1,0:T(8,128)(2,1)S(1)} %get-tuple-element.19), channel_id=1, source_target_pairs={{0,8},{8,16},{16,24},{24,0},{1,9},{9,17},{17,25},{25,1},{2,10},{10... | collective-permute-start | bytes 393224 | tf_op jit(solution)/shard_map/ppermute | solution.py:190
  190.8 2.3 copy-start.12
  190.8 0.9 copy-start.6
  190.9 1.1 copy-start.7
  190.9 1.3 copy-start.8
  192.2 0.9 copy-start.9
  369.5 2.5 copy-start
  372.0 1.0 copy-start.1

commit v2 on v1

--- a/solution.py
+++ b/solution.py
@@ -88,31 +88,26 @@
 
 def assemble(*refs):
     own, other, early = refs[0:4], refs[4:8], refs[8:12]
-    factor, columns, sems = refs[12:]
+    factor, columns = refs[12:]
     x, core = lax.axis_index("x"), lax.axis_index("core")
-    copies = []
     for s in range(NX):
         source = lax.rem(x + NX - s, NX)
+        columns[source] = early[s][...]
+        row = pl.multiple_of(source * 128, 128)
         for pieces, half in ((own, core), (other, 1 - core)):
-            for y in range(NY):
-                row = pl.multiple_of(source * 128 + y * 16, 16)
-                copies.append(
-                    pltpu.make_async_copy(
-                        pieces[s].at[y],
-                        factor.at[half, :, pl.ds(row, 16), :],
-                        sems.at[len(copies)],
-                    )
-                )
-        copies.append(
-            pltpu.make_async_copy(early[s], columns.at[source], sems.at[len(copies)])
-        )
-    run_all(copies)
-
-
-def solve(factor, early, late, out, held, sems):
+            for b in range(5):
+                factor[half, b, pl.ds(row, 128), :] = pieces[s][:, b].reshape(128, 512)
+
+
+def solve(factor, early, late, out, panels, held, sems):
     x = lax.axis_index("x")
-    solved = []
-    copies = []
+    order = [b for k in range(4) for b in [4 + k * (k - 1) // 2 + j for j in range(k)] + [k]]
+    loads = {
+        b: pltpu.make_async_copy(factor.at[b], panels.at[b], sems.at[b]) for b in order
+    }
+    for b in order:
+        loads[b].start()
+    stores = []
     for k in range(4):
         slot = lax.rem(x + NX - k, NX)
         acc = jnp.concatenate(
@@ -123,22 +118,23 @@
             axis=1,
         ).astype(jnp.float32)
         for j in range(k):
+            b = 4 + k * (k - 1) // 2 + j
+            loads[b].wait()
             acc = acc - jnp.dot(
-                factor[4 + k * (k - 1) // 2 + j],
-                held[j],
-                preferred_element_type=jnp.float32,
-            )
+                panels[b], held[j], preferred_element_type=jnp.float32
+            )
+        loads[k].wait()
         held[k] = jnp.dot(
-            factor[k], acc.astype(jnp.bfloat16), preferred_element_type=jnp.float32
+            panels[k], acc.astype(jnp.bfloat16), preferred_element_type=jnp.float32
         ).astype(jnp.bfloat16)
-        copies.append(
+        stores.append(
             pltpu.make_async_copy(
-                held.at[k], out.at[k * 512 : (k + 1) * 512], sems.at[k]
+                held.at[k], out.at[k * 512 : (k + 1) * 512], sems.at[10 + k]
             )
         )
-        copies[-1].start()
-    for copy in copies:
-        copy.wait()
+        stores[-1].start()
+    for store in stores:
+        store.wait()
 
 
 def cost(flops, moved):
@@ -159,7 +155,7 @@
         pack_first,
         out_shape=jax.ShapeDtypeStruct((NY, 9, 16, width), bf16),
         in_specs=[ANY] * 3,
-        out_specs=ANY,
+        out_specs=VMEM,
         scratch_shapes=[pltpu.SemaphoreType.DMA((NX * NY + 2 * NY,))],
         cost_estimate=cost(0, 3 << 20),
     )(integrals.reshape(4, 16, total), inverses, lower_blocks)
@@ -169,7 +165,7 @@
         pack_late,
         out_shape=[jax.ShapeDtypeStruct((NY, rows, late_width), bf16)] * NX,
         in_specs=[ANY],
-        out_specs=[ANY] * NX,
+        out_specs=[VMEM] * NX,
         scratch_shapes=[pltpu.SemaphoreType.DMA((NX * NY,))],
         cost_estimate=cost(0, 3 << 20),
     )(integrals)
@@ -195,22 +191,23 @@
             jax.ShapeDtypeStruct((2, 5, 512, 512), bf16),
             jax.ShapeDtypeStruct((NX, NY, 4, 16, EARLY), bf16),
         ],
-        in_specs=[ANY] * (3 * NX),
-        out_specs=[ANY] * 2,
-        scratch_shapes=[pltpu.SemaphoreType.DMA((NX * (2 * NY + 1),))],
+        in_specs=[VMEM] * (3 * NX),
+        out_specs=[VMEM] * 2,
+        compiler_params=pltpu.CompilerParams(vmem_limit_bytes=16 << 20),
         cost_estimate=cost(0, 11 << 20),
     )(*[d[s] for d in (own, other, early) for s in range(NX)])
 
     return pl.pallas_call(
         solve,
         out_shape=jax.ShapeDtypeStruct((4 * 512, width), bf16),
-        in_specs=[VMEM] * 3,
+        in_specs=[ANY, VMEM, VMEM],
         out_specs=ANY,
         scratch_shapes=[
+            pltpu.VMEM((10, 512, 512), bf16),
             pltpu.VMEM((4, 512, width), bf16),
-            pltpu.SemaphoreType.DMA((4,)),
+            pltpu.SemaphoreType.DMA((14,)),
         ],
-        compiler_params=pltpu.CompilerParams(vmem_limit_bytes=32 << 20),
+        compiler_params=pltpu.CompilerParams(vmem_limit_bytes=16 << 20),
         cost_estimate=cost(20 * 512**3, 9 << 20),
     )(factor.reshape(10, 512, 512), columns, late)
 

time: 380 us -> 124 us (0.33)
  the two profiles are of different devices: /device:TPU:1 before, /device:TPU:136 now
where the time goes in v2:
time: 124 us; the launch traced here: 123 us
  starting transfers between devices  55.7 us (45%)
  waiting for transfers between devices  48 us (39%)
  Pallas kernels  12.2 us (10%)
  local copies, waits for them, and re-layouts  4.95 us (4%)
  other arithmetic  2.37 us (2%)
    ppermute x3, waiting for transfers between devices, local(): own[s] = lax.ppermute(own[0], 'x', ring(NX, s))  21.3 us
    ppermute x3, waiting for transfers between devices, local(): early[s] = lax.ppermute(early[s], 'x', ring(NX, s))  13.2 us
    ppermute x3, waiting for transfers between devices, local(): moved[s] = lax.ppermute(slabs[s], 'x', ring(NX, s))  13.1 us
    ppermute x3, starting transfers between devices, local(): early[s] = lax.ppermute(early[s], 'x', ring(NX, s))  11.6 us
    ppermute x3, starting transfers between devices, local(): moved[s] = lax.ppermute(slabs[s], 'x', ring(NX, s))  11.4 us
    ppermute x3, starting transfers between devices, local(): own[s] = lax.ppermute(own[0], 'x', ring(NX, s))  10.2 us
    ppermute x4, starting transfers between devices, local(): other = {s: lax.ppermute(own[s], 'core', ring(2, 1)) for s in range(NX)}  8.15 us
    all_to_all x1, starting transfers between devices, local(): first = lax.all_to_all(first, 'y', 0, 0, tiled=True)  7.56 us
  transfers between devices with their start and end apart: 15, of which 9 were waited for; matrix products, arithmetic and copies ran while one was open for 2% of the time, Pallas kernels for 3%

profile of v2, /device:TPU:136, one launch (start us, length us, event | category | flops | bytes accessed | tf_op | source)
XLA Modules:
  0.0 123.3 jit_solution(89183193252503130)
XLA Ops:
  0.0 3.2 %shard_map.37 = bf16[8,9,16,512]{3,2,1,0:T(8,128)(2,1)} custom-call(bf16[4,16,16384]{2,1,0:T(8,128)(2,1)} %bitcast.7, bf16[4,16,512]{2,1,0:T(8,128)(2,1)} %inverses.1, bf16[6,16,512]{2,1,0:T(8,128)(2,1)} %lower_blocks.1), custom_call_target="tpu_custom_call" | custom-call | bytes 3145728 | tf_op jit(solution)/shard_map/pallas_call | solution.py:154
  3.2 7.6 %all-to-all-start = ((bf16[8,9,16,512]{3,2,1,0:T(8,128)(2,1)}), bf16[8,9,16,512]{3,2,1,0:T(8,128)(2,1)S(1)}, u32[]{:S(2)}, u32[]{:S(2)}) async-start(bf16[8,9,16,512]{3,2,1,0:T(8,128)(2,1)} %shard_map.37), calls=%async_computation | async-start | bytes 2359296 | tf_op jit(solution)/shard_map/all_to_all | solution.py:162
  10.8 2.8 %shard_map.39 = (bf16[8,64,384]{2,1,0:T(8,128)(2,1)}, bf16[8,64,384]{2,1,0:T(8,128)(2,1)}, bf16[8,64,384]{2,1,0:T(8,128)(2,1)}, bf16[8,64,384]{2,1,0:T(8,128)(2,1)}) custom-call(bf16[64,16384]{1,0:T(8,128)(2,1)} %integrals.1), custom_call_target="tpu_custom_call" | custom-call | bytes 3145728 | tf_op jit(solution)/shard_map/pallas_call | solution.py:164
  13.6 3.4 %collective-permute-start.10 = (bf16[8,64,384]{2,1,0:T(8,128)(2,1)}, bf16[8,64,384]{2,1,0:T(8,128)(2,1)S(1)}, u32[]{:S(2)}, u32[]{:S(2)}) collective-permute-start(bf16[8,64,384]{2,1,0:T(8,128)(2,1)} %get-tuple-element.14), channel_id=1, source_target_pairs={{0,8},{8,16},{16,24},{24,0},{1,9},{9,17},{17,25},{25,1},{2,10},{10... | collective-permute-start | bytes 1179656 | tf_op jit(solution)/shard_map/ppermute | solution.py:174
  17.0 4.6 %collective-permute-start.11 = (bf16[8,64,384]{2,1,0:T(8,128)(2,1)}, bf16[8,64,384]{2,1,0:T(8,128)(2,1)S(1)}, u32[]{:S(2)}, u32[]{:S(2)}) collective-permute-start(bf16[8,64,384]{2,1,0:T(8,128)(2,1)} %get-tuple-element.15), channel_id=1, source_target_pairs={{0,16},{8,24},{16,0},{24,8},{1,17},{9,25},{17,1},{25,9},{2,18},{10... | collective-permute-start | bytes 1179656 | tf_op jit(solution)/shard_map/ppermute | solution.py:174
  21.6 3.3 %collective-permute-start.12 = (bf16[8,64,384]{2,1,0:T(8,128)(2,1)}, bf16[8,64,384]{2,1,0:T(8,128)(2,1)S(1)}, u32[]{:S(2)}, u32[]{:S(2)}) collective-permute-start(bf16[8,64,384]{2,1,0:T(8,128)(2,1)} %get-tuple-element.16), channel_id=1, source_target_pairs={{0,24},{8,0},{16,8},{24,16},{1,25},{9,1},{17,9},{25,17},{2,26},{10... | collective-permute-start | bytes 1179656 | tf_op jit(solution)/shard_map/ppermute | solution.py:174
  25.0 3.0 %collective-permute-done.10 = bf16[8,64,384]{2,1,0:T(8,128)(2,1)S(1)} collective-permute-done((bf16[8,64,384]{2,1,0:T(8,128)(2,1)}, bf16[8,64,384]{2,1,0:T(8,128)(2,1)S(1)}, u32[]{:S(2)}, u32[]{:S(2)}) %collective-permute-start.10) | collective-permute-done | bytes 393248 | tf_op jit(solution)/shard_map/ppermute | solution.py:174
  28.0 8.6 %collective-permute-done.11 = bf16[8,64,384]{2,1,0:T(8,128)(2,1)S(1)} collective-permute-done((bf16[8,64,384]{2,1,0:T(8,128)(2,1)}, bf16[8,64,384]{2,1,0:T(8,128)(2,1)S(1)}, u32[]{:S(2)}, u32[]{:S(2)}) %collective-permute-start.11) | collective-permute-done | bytes 393248 | tf_op jit(solution)/shard_map/ppermute | solution.py:174
  36.6 1.6 %collective-permute-done.12 = bf16[8,64,384]{2,1,0:T(8,128)(2,1)S(1)} collective-permute-done((bf16[8,64,384]{2,1,0:T(8,128)(2,1)}, bf16[8,64,384]{2,1,0:T(8,128)(2,1)S(1)}, u32[]{:S(2)}, u32[]{:S(2)}) %collective-permute-start.12) | collective-permute-done | bytes 393248 | tf_op jit(solution)/shard_map/ppermute | solution.py:174
  38.1 2.4 %pad_maximum_fusion = bf16[8,4,64,384]{3,2,1,0:T(8,128)(2,1)} fusion(bf16[8,1,64,384]{3,2,1,0:T(8,128)(2,1)S(1)} %bitcast.11, bf16[8,1,64,384]{3,2,1,0:T(8,128)(2,1)S(1)} %bitcast.10, bf16[8,1,64,384]{3,2,1,0:T(8,128)(2,1)S(1)} %bitcast.9, bf16[8,1,64,384]{3,2,1,0:T(8,128)(2,1)} %bitcast.8), kind=kLoop, calls=%fused_computation | loop fusion | flops 2359296 | bytes 3145728 | tf_op jit(solution)/shard_map/stack | solution.py:175
  40.5 0.3 all-to-all-done
  40.8 6.9 %all-to-all-start.1 = ((bf16[8,4,64,384]{3,2,1,0:T(8,128)(2,1)}), bf16[8,4,64,384]{3,2,1,0:T(8,128)(2,1)S(1)}, u32[]{:S(2)}, u32[]{:S(2)}) async-start(bf16[8,4,64,384]{3,2,1,0:T(8,128)(2,1)} %pad_maximum_fusion), calls=%async_computation.1 | async-start | bytes 3145728 | tf_op jit(solution)/shard_map/all_to_all | solution.py:176
  47.7 4.5 %collective-permute-start.2 = (bf16[8,5,16,512]{3,2,1,0:T(8,128)(2,1)S(1)}, bf16[8,5,16,512]{3,2,1,0:T(8,128)(2,1)S(1)}, u32[]{:S(2)}, u32[]{:S(2)}) collective-permute-start(bf16[8,5,16,512]{3,2,1,0:T(8,128)(2,1)S(1)} %slice.20.refs_0_), channel_id=1, source_target_pairs={{0,24},{8,0},{16,8},{24,16},{1,25},{9,1},{17,9},{25,17},{2,26},{10... | collective-permute-start | bytes 1966088 | tf_op jit(solution)/shard_map/ppermute | solution.py:180
  52.3 3.7 %collective-permute-start.1 = (bf16[8,5,16,512]{3,2,1,0:T(8,128)(2,1)S(1)}, bf16[8,5,16,512]{3,2,1,0:T(8,128)(2,1)S(1)}, u32[]{:S(2)}, u32[]{:S(2)}) collective-permute-start(bf16[8,5,16,512]{3,2,1,0:T(8,128)(2,1)S(1)} %slice.20.refs_0_), channel_id=1, source_target_pairs={{0,16},{8,24},{16,0},{24,8},{1,17},{9,25},{17,1},{25,9},{2,18},{10... | collective-permute-start | bytes 1966088 | tf_op jit(solution)/shard_map/ppermute | solution.py:180
  56.0 1.9 %collective-permute-start = (bf16[8,5,16,512]{3,2,1,0:T(8,128)(2,1)S(1)}, bf16[8,5,16,512]{3,2,1,0:T(8,128)(2,1)S(1)}, u32[]{:S(2)}, u32[]{:S(2)}) collective-permute-start(bf16[8,5,16,512]{3,2,1,0:T(8,128)(2,1)S(1)} %slice.20.refs_0_), channel_id=1, source_target_pairs={{0,8},{8,16},{16,24},{24,0},{1,9},{9,17},{17,25},{25,1},{2,10},{10... | collective-permute-start | bytes 1966088 | tf_op jit(solution)/shard_map/ppermute | solution.py:180
  57.9 1.9 %collective-permute-start.3 = (bf16[8,5,16,512]{3,2,1,0:T(8,128)(2,1)S(1)}, bf16[8,5,16,512]{3,2,1,0:T(8,128)(2,1)S(1)}, u32[]{:S(2)}, u32[]{:S(2)}) collective-permute-start(bf16[8,5,16,512]{3,2,1,0:T(8,128)(2,1)S(1)} %slice.20.refs_0_), channel_id=1, source_target_pairs={{0,32},{32,0},{1,33},{33,1},{2,34},{34,2},{3,35},{35,3},{4,36},{36... | collective-permute-start | bytes 1966088 | tf_op jit(solution)/shard_map/ppermute | solution.py:181
  59.9 20.1 %collective-permute-done.2.refs_3_ = bf16[8,5,16,512]{3,2,1,0:T(8,128)(2,1)S(1)} collective-permute-done((bf16[8,5,16,512]{3,2,1,0:T(8,128)(2,1)S(1)}, bf16[8,5,16,512]{3,2,1,0:T(8,128)(2,1)S(1)}, u32[]{:S(2)}, u32[]{:S(2)}) %collective-permute-start.2) | collective-permute-done | bytes 655392 | tf_op jit(solution)/shard_map/ppermute | solution.py:180
  79.9 1.9 %collective-permute-start.6 = (bf16[8,5,16,512]{3,2,1,0:T(8,128)(2,1)S(1)}, bf16[8,5,16,512]{3,2,1,0:T(8,128)(2,1)S(1)}, u32[]{:S(2)}, u32[]{:S(2)}) collective-permute-start(bf16[8,5,16,512]{3,2,1,0:T(8,128)(2,1)S(1)} %collective-permute-done.2.refs_3_), channel_id=1, source_target_pairs={{0,32},{32,0},{1,33},{33,1},{2,34},{34,2},{3,35},{35,3},{4,36},{36... | collective-permute-start | bytes 1966088 | tf_op jit(solution)/shard_map/ppermute | solution.py:181
  81.9 0.0 collective-permute-done.1.refs_2_
  81.9 2.4 %collective-permute-start.5 = (bf16[8,5,16,512]{3,2,1,0:T(8,128)(2,1)S(1)}, bf16[8,5,16,512]{3,2,1,0:T(8,128)(2,1)S(1)}, u32[]{:S(2)}, u32[]{:S(2)}) collective-permute-start(bf16[8,5,16,512]{3,2,1,0:T(8,128)(2,1)S(1)} %collective-permute-done.1.refs_2_), channel_id=1, source_target_pairs={{0,32},{32,0},{1,33},{33,1},{2,34},{34,2},{3,35},{35,3},{4,36},{36... | collective-permute-start | bytes 1966088 | tf_op jit(solution)/shard_map/ppermute | solution.py:181
  84.3 1.2 %collective-permute-done.refs_1_ = bf16[8,5,16,512]{3,2,1,0:T(8,128)(2,1)S(1)} collective-permute-done((bf16[8,5,16,512]{3,2,1,0:T(8,128)(2,1)S(1)}, bf16[8,5,16,512]{3,2,1,0:T(8,128)(2,1)S(1)}, u32[]{:S(2)}, u32[]{:S(2)}) %collective-permute-start) | collective-permute-done | bytes 655392 | tf_op jit(solution)/shard_map/ppermute | solution.py:180
  85.5 1.9 %collective-permute-start.4 = (bf16[8,5,16,512]{3,2,1,0:T(8,128)(2,1)S(1)}, bf16[8,5,16,512]{3,2,1,0:T(8,128)(2,1)S(1)}, u32[]{:S(2)}, u32[]{:S(2)}) collective-permute-start(bf16[8,5,16,512]{3,2,1,0:T(8,128)(2,1)S(1)} %collective-permute-done.refs_1_), channel_id=1, source_target_pairs={{0,32},{32,0},{1,33},{33,1},{2,34},{34,2},{3,35},{35,3},{4,36},{36... | collective-permute-start | bytes 1966088 | tf_op jit(solution)/shard_map/ppermute | solution.py:181
  87.5 0.1 fusion
  87.6 4.3 %collective-permute-start.9 = (bf16[8,4,16,128]{3,2,1,0:T(8,128)(2,1)S(1)}, bf16[8,4,16,128]{3,2,1,0:T(8,128)(2,1)S(1)}, u32[]{:S(2)}, u32[]{:S(2)}) collective-permute-start(bf16[8,4,16,128]{3,2,1,0:T(8,128)(2,1)S(1)} %get-tuple-element.17), channel_id=1, source_target_pairs={{0,24},{8,0},{16,8},{24,16},{1,25},{9,1},{17,9},{25,17},{2,26},{10... | collective-permute-start | bytes 393224 | tf_op jit(solution)/shard_map/ppermute | solution.py:186
  91.9 3.4 %collective-permute-done.9.refs_11_ = bf16[8,4,16,128]{3,2,1,0:T(8,128)(2,1)S(1)} collective-permute-done((bf16[8,4,16,128]{3,2,1,0:T(8,128)(2,1)S(1)}, bf16[8,4,16,128]{3,2,1,0:T(8,128)(2,1)S(1)}, u32[]{:S(2)}, u32[]{:S(2)}) %collective-permute-start.9) | collective-permute-done | bytes 131104 | tf_op jit(solution)/shard_map/ppermute | solution.py:186
  95.4 4.1 %collective-permute-start.8 = (bf16[8,4,16,128]{3,2,1,0:T(8,128)(2,1)S(1)}, bf16[8,4,16,128]{3,2,1,0:T(8,128)(2,1)S(1)}, u32[]{:S(2)}, u32[]{:S(2)}) collective-permute-start(bf16[8,4,16,128]{3,2,1,0:T(8,128)(2,1)S(1)} %get-tuple-element.18), channel_id=1, source_target_pairs={{0,16},{8,24},{16,0},{24,8},{1,17},{9,25},{17,1},{25,9},{2,18},{10... | collective-permute-start | bytes 393224 | tf_op jit(solution)/shard_map/ppermute | solution.py:186
  99.4 4.4 %collective-permute-done.8.refs_10_ = bf16[8,4,16,128]{3,2,1,0:T(8,128)(2,1)S(1)} collective-permute-done((bf16[8,4,16,128]{3,2,1,0:T(8,128)(2,1)S(1)}, bf16[8,4,16,128]{3,2,1,0:T(8,128)(2,1)S(1)}, u32[]{:S(2)}, u32[]{:S(2)}) %collective-permute-start.8) | collective-permute-done | bytes 131104 | tf_op jit(solution)/shard_map/ppermute | solution.py:186
  103.9 3.2 %collective-permute-start.7 = (bf16[8,4,16,128]{3,2,1,0:T(8,128)(2,1)S(1)}, bf16[8,4,16,128]{3,2,1,0:T(8,128)(2,1)S(1)}, u32[]{:S(2)}, u32[]{:S(2)}) collective-permute-start(bf16[8,4,16,128]{3,2,1,0:T(8,128)(2,1)S(1)} %get-tuple-element.19), channel_id=1, source_target_pairs={{0,8},{8,16},{16,24},{24,0},{1,9},{9,17},{17,25},{25,1},{2,10},{10... | collective-permute-start | bytes 393224 | tf_op jit(solution)/shard_map/ppermute | solution.py:186
  107.0 5.3 %collective-permute-done.7.refs_9_ = bf16[8,4,16,128]{3,2,1,0:T(8,128)(2,1)S(1)} collective-permute-done((bf16[8,4,16,128]{3,2,1,0:T(8,128)(2,1)S(1)}, bf16[8,4,16,128]{3,2,1,0:T(8,128)(2,1)S(1)}, u32[]{:S(2)}, u32[]{:S(2)}) %collective-permute-start.7) | collective-permute-done | bytes 131104 | tf_op jit(solution)/shard_map/ppermute | solution.py:186
  112.4 0.0 collective-permute-done.3.refs_4_
  112.4 0.0 collective-permute-done.6.refs_7_
  112.4 0.0 collective-permute-done.5.refs_6_
  112.4 0.0 collective-permute-done.4.refs_5_
  112.4 0.4 shard_map.38
  112.8 0.0 copy-start
  112.8 2.3 %copy-done = bf16[2,5,512,512]{3,2,1,0:T(8,128)(2,1)} copy-done((bf16[2,5,512,512]{3,2,1,0:T(8,128)(2,1)}, bf16[2,5,512,512]{3,2,1,0:T(8,128)(2,1)S(1)}, u32[]{:S(2)}) %copy-start) | copy-done | bytes 5242904
  115.1 0.0 all-to-all-done.1.late
  115.1 0.0 copy-start.1
  115.1 2.5 %copy-done.1 = bf16[2,5,512,512]{3,2,1,0:T(8,128)(2,1)S(1)} copy-done((bf16[2,5,512,512]{3,2,1,0:T(8,128)(2,1)S(1)}, bf16[2,5,512,512]{3,2,1,0:T(8,128)(2,1)}, u32[]{:S(2)}) %copy-start.1) | copy-done | bytes 5242904
  117.6 5.8 %shard_map.40 = bf16[2048,512]{1,0:T(8,128)(2,1)} custom-call(bf16[10,512,512]{2,1,0:T(8,128)(2,1)S(1)} %bitcast.6, bf16[4,8,4,16,128]{4,3,2,1,0:T(8,128)(2,1)S(1)} %get-tuple-element.12.early, bf16[8,4,64,384]{3,2,1,0:T(8,128)(2,1)S(1)} %all-to-all-done.1.late), custom_call_target="tpu_custom_call" | custom-call | flops 2684354560 | bytes 9437184 | tf_op jit(solution)/shard_map/pallas_call | solution.py:200
  (1 shorter events, 0.0 us)
Async XLA Ops:
  3.2 37.6 %all-to-all-start = ((bf16[8,9,16,512]{3,2,1,0:T(8,128)(2,1)}), bf16[8,9,16,512]{3,2,1,0:T(8,128)(2,1)S(1)}, u32[]{:S(2)}, u32[]{:S(2)}) async-start(bf16[8,9,16,512]{3,2,1,0:T(8,128)(2,1)} %shard_map.37), calls=%async_computation | async-start | bytes 2359296 | tf_op jit(solution)/shard_map/all_to_all | solution.py:162
  13.6 14.4 %collective-permute-start.10 = (bf16[8,64,384]{2,1,0:T(8,128)(2,1)}, bf16[8,64,384]{2,1,0:T(8,128)(2,1)S(1)}, u32[]{:S(2)}, u32[]{:S(2)}) collective-permute-start(bf16[8,64,384]{2,1,0:T(8,128)(2,1)} %get-tuple-element.14), channel_id=1, source_target_pairs={{0,8},{8,16},{16,24},{24,0},{1,9},{9,17},{17,25},{25,1},{2,10},{10... | collective-permute-start | bytes 1179656 | tf_op jit(solution)/shard_map/ppermute | solution.py:174
  17.0 19.6 %collective-permute-start.11 = (bf16[8,64,384]{2,1,0:T(8,128)(2,1)}, bf16[8,64,384]{2,1,0:T(8,128)(2,1)S(1)}, u32[]{:S(2)}, u32[]{:S(2)}) collective-permute-start(bf16[8,64,384]{2,1,0:T(8,128)(2,1)} %get-tuple-element.15), channel_id=1, source_target_pairs={{0,16},{8,24},{16,0},{24,8},{1,17},{9,25},{17,1},{25,9},{2,18},{10... | collective-permute-start | bytes 1179656 | tf_op jit(solution)/shard_map/ppermute | solution.py:174
  21.6 16.5 %collective-permute-start.12 = (bf16[8,64,384]{2,1,0:T(8,128)(2,1)}, bf16[8,64,384]{2,1,0:T(8,128)(2,1)S(1)}, u32[]{:S(2)}, u32[]{:S(2)}) collective-permute-start(bf16[8,64,384]{2,1,0:T(8,128)(2,1)} %get-tuple-element.16), channel_id=1, source_target_pairs={{0,24},{8,0},{16,8},{24,16},{1,25},{9,1},{17,9},{25,17},{2,26},{10... | collective-permute-start | bytes 1179656 | tf_op jit(solution)/shard_map/ppermute | solution.py:174
  40.8 74.3 %all-to-all-start.1 = ((bf16[8,4,64,384]{3,2,1,0:T(8,128)(2,1)}), bf16[8,4,64,384]{3,2,1,0:T(8,128)(2,1)S(1)}, u32[]{:S(2)}, u32[]{:S(2)}) async-start(bf16[8,4,64,384]{3,2,1,0:T(8,128)(2,1)} %pad_maximum_fusion), calls=%async_computation.1 | async-start | bytes 3145728 | tf_op jit(solution)/shard_map/all_to_all | solution.py:176
  47.7 32.2 %collective-permute-start.2 = (bf16[8,5,16,512]{3,2,1,0:T(8,128)(2,1)S(1)}, bf16[8,5,16,512]{3,2,1,0:T(8,128)(2,1)S(1)}, u32[]{:S(2)}, u32[]{:S(2)}) collective-permute-start(bf16[8,5,16,512]{3,2,1,0:T(8,128)(2,1)S(1)} %slice.20.refs_0_), channel_id=1, source_target_pairs={{0,24},{8,0},{16,8},{24,16},{1,25},{9,1},{17,9},{25,17},{2,26},{10... | collective-permute-start | bytes 1966088 | tf_op jit(solution)/shard_map/ppermute | solution.py:180
  52.3 29.6 %collective-permute-start.1 = (bf16[8,5,16,512]{3,2,1,0:T(8,128)(2,1)S(1)}, bf16[8,5,16,512]{3,2,1,0:T(8,128)(2,1)S(1)}, u32[]{:S(2)}, u32[]{:S(2)}) collective-permute-start(bf16[8,5,16,512]{3,2,1,0:T(8,128)(2,1)S(1)} %slice.20.refs_0_), channel_id=1, source_target_pairs={{0,16},{8,24},{16,0},{24,8},{1,17},{9,25},{17,1},{25,9},{2,18},{10... | collective-permute-start | bytes 1966088 | tf_op jit(solution)/shard_map/ppermute | solution.py:180
  56.0 29.5 %collective-permute-start = (bf16[8,5,16,512]{3,2,1,0:T(8,128)(2,1)S(1)}, bf16[8,5,16,512]{3,2,1,0:T(8,128)(2,1)S(1)}, u32[]{:S(2)}, u32[]{:S(2)}) collective-permute-start(bf16[8,5,16,512]{3,2,1,0:T(8,128)(2,1)S(1)} %slice.20.refs_0_), channel_id=1, source_target_pairs={{0,8},{8,16},{16,24},{24,0},{1,9},{9,17},{17,25},{25,1},{2,10},{10... | collective-permute-start | bytes 1966088 | tf_op jit(solution)/shard_map/ppermute | solution.py:180
  57.9 54.4 %collective-permute-start.3 = (bf16[8,5,16,512]{3,2,1,0:T(8,128)(2,1)S(1)}, bf16[8,5,16,512]{3,2,1,0:T(8,128)(2,1)S(1)}, u32[]{:S(2)}, u32[]{:S(2)}) collective-permute-start(bf16[8,5,16,512]{3,2,1,0:T(8,128)(2,1)S(1)} %slice.20.refs_0_), channel_id=1, source_target_pairs={{0,32},{32,0},{1,33},{33,1},{2,34},{34,2},{3,35},{35,3},{4,36},{36... | collective-permute-start | bytes 1966088 | tf_op jit(solution)/shard_map/ppermute | solution.py:181
  79.9 32.4 %collective-permute-start.6 = (bf16[8,5,16,512]{3,2,1,0:T(8,128)(2,1)S(1)}, bf16[8,5,16,512]{3,2,1,0:T(8,128)(2,1)S(1)}, u32[]{:S(2)}, u32[]{:S(2)}) collective-permute-start(bf16[8,5,16,512]{3,2,1,0:T(8,128)(2,1)S(1)} %collective-permute-done.2.refs_3_), channel_id=1, source_target_pairs={{0,32},{32,0},{1,33},{33,1},{2,34},{34,2},{3,35},{35,3},{4,36},{36... | collective-permute-start | bytes 1966088 | tf_op jit(solution)/shard_map/ppermute | solution.py:181
  81.9 30.5 %collective-permute-start.5 = (bf16[8,5,16,512]{3,2,1,0:T(8,128)(2,1)S(1)}, bf16[8,5,16,512]{3,2,1,0:T(8,128)(2,1)S(1)}, u32[]{:S(2)}, u32[]{:S(2)}) collective-permute-start(bf16[8,5,16,512]{3,2,1,0:T(8,128)(2,1)S(1)} %collective-permute-done.1.refs_2_), channel_id=1, source_target_pairs={{0,32},{32,0},{1,33},{33,1},{2,34},{34,2},{3,35},{35,3},{4,36},{36... | collective-permute-start | bytes 1966088 | tf_op jit(solution)/shard_map/ppermute | solution.py:181
  85.5 26.8 %collective-permute-start.4 = (bf16[8,5,16,512]{3,2,1,0:T(8,128)(2,1)S(1)}, bf16[8,5,16,512]{3,2,1,0:T(8,128)(2,1)S(1)}, u32[]{:S(2)}, u32[]{:S(2)}) collective-permute-start(bf16[8,5,16,512]{3,2,1,0:T(8,128)(2,1)S(1)} %collective-permute-done.refs_1_), channel_id=1, source_target_pairs={{0,32},{32,0},{1,33},{33,1},{2,34},{34,2},{3,35},{35,3},{4,36},{36... | collective-permute-start | bytes 1966088 | tf_op jit(solution)/shard_map/ppermute | solution.py:181
  87.6 7.8 %collective-permute-start.9 = (bf16[8,4,16,128]{3,2,1,0:T(8,128)(2,1)S(1)}, bf16[8,4,16,128]{3,2,1,0:T(8,128)(2,1)S(1)}, u32[]{:S(2)}, u32[]{:S(2)}) collective-permute-start(bf16[8,4,16,128]{3,2,1,0:T(8,128)(2,1)S(1)} %get-tuple-element.17), channel_id=1, source_target_pairs={{0,24},{8,0},{16,8},{24,16},{1,25},{9,1},{17,9},{25,17},{2,26},{10... | collective-permute-start | bytes 393224 | tf_op jit(solution)/shard_map/ppermute | solution.py:186
  95.4 8.5 %collective-permute-start.8 = (bf16[8,4,16,128]{3,2,1,0:T(8,128)(2,1)S(1)}, bf16[8,4,16,128]{3,2,1,0:T(8,128)(2,1)S(1)}, u32[]{:S(2)}, u32[]{:S(2)}) collective-permute-start(bf16[8,4,16,128]{3,2,1,0:T(8,128)(2,1)S(1)} %get-tuple-element.18), channel_id=1, source_target_pairs={{0,16},{8,24},{16,0},{24,8},{1,17},{9,25},{17,1},{25,9},{2,18},{10... | collective-permute-start | bytes 393224 | tf_op jit(solution)/shard_map/ppermute | solution.py:186
  103.9 8.5 %collective-permute-start.7 = (bf16[8,4,16,128]{3,2,1,0:T(8,128)(2,1)S(1)}, bf16[8,4,16,128]{3,2,1,0:T(8,128)(2,1)S(1)}, u32[]{:S(2)}, u32[]{:S(2)}) collective-permute-start(bf16[8,4,16,128]{3,2,1,0:T(8,128)(2,1)S(1)} %get-tuple-element.19), channel_id=1, source_target_pairs={{0,8},{8,16},{16,24},{24,0},{1,9},{9,17},{17,25},{25,1},{2,10},{10... | collective-permute-start | bytes 393224 | tf_op jit(solution)/shard_map/ppermute | solution.py:186
  112.8 2.3 %copy-start = (bf16[2,5,512,512]{3,2,1,0:T(8,128)(2,1)}, bf16[2,5,512,512]{3,2,1,0:T(8,128)(2,1)S(1)}, u32[]{:S(2)}) copy-start(bf16[2,5,512,512]{3,2,1,0:T(8,128)(2,1)S(1)} %get-tuple-element.11) | copy-start | bytes 15728644
  115.1 2.5 %copy-start.1 = (bf16[2,5,512,512]{3,2,1,0:T(8,128)(2,1)S(1)}, bf16[2,5,512,512]{3,2,1,0:T(8,128)(2,1)}, u32[]{:S(2)}) copy-start(bf16[2,5,512,512]{3,2,1,0:T(8,128)(2,1)} %copy-done) | copy-start | bytes 15728644

commit v3 on v0

v3 whole, which is shorter than its diff:
```python
import jax
import jax.numpy as jnp
from jax import lax
from jax.experimental import pallas as pl
from jax.experimental.pallas import tpu as pltpu
from jax.sharding import Mesh, PartitionSpec as P

NX, NY = 4, 8
ANY = pl.BlockSpec(memory_space=pl.ANY)
VMEM = pl.BlockSpec(memory_space=pltpu.VMEM)


def pack_first(integrals, inverses, lower_blocks, first, half, sems):
    x, core = lax.axis_index("x"), lax.axis_index("core")
    width = integrals.shape[2] // (NX * NY)
    copies = []
    for y in range(NY):
        at = pl.multiple_of(x * (NY * width) + y * width, 128)
        copies.append(
            pltpu.make_async_copy(
                integrals.at[:, :, pl.ds(at, width)], first.at[y, 0:4], sems.at[y]
            )
        )
    for copy in copies:
        copy.start()

    @pl.when(core == 0)
    def _():
        half[0:4] = inverses[...]
        half[4] = lower_blocks[0]

    @pl.when(core == 1)
    def _():
        half[...] = lower_blocks[1:6]

    for y in range(NY):
        first[y, 4:9] = half[...]
    for copy in copies:
        copy.wait()


def pack_late(integrals, s1, s2, s3, sems):
    x = lax.axis_index("x")
    width = integrals.shape[1] // (NX * NY)
    copies = []
    for s, slab in ((1, s1), (3, s3), (2, s2)):
        for y in range(NY):
            at = pl.multiple_of(lax.rem(x + s, NX) * (NY * width) + y * width, 128)
            copies.append(
                pltpu.make_async_copy(
                    integrals.at[:, pl.ds(at, width)], slab.at[y], sems.at[len(copies)]
                )
            )
    for copy in copies:
        copy.start()
    for copy in copies:
        copy.wait()


def solve(*refs):
    own, other, first, late = refs[0:4], refs[4:8], refs[8], refs[9]
    out, factor, held, sems = refs[10:]
    x, core = lax.axis_index("x"), lax.axis_index("core")
    for s in range(NX):
        row = pl.multiple_of(lax.rem(x + NX - s, NX) * 128, 128)
        for pieces, half in ((own, core), (other, 1 - core)):
            for b in range(5):
                factor[half * 5 + b, pl.ds(row, 128), :] = pieces[s][:, b].reshape(
                    128, 512
                )
    stores = []
    for k in range(4):
        slot = lax.rem(x + NX - k, NX)
        acc = jnp.where(
            slot == 0,
            first[:, 0:4].reshape(512, 512),
            late[:, jnp.maximum(slot - 1, 0)].reshape(512, 512),
        ).astype(jnp.float32)
        for j in range(k):
            acc = acc - jnp.dot(
                factor[4 + k * (k - 1) // 2 + j],
                held[j],
                preferred_element_type=jnp.float32,
            )
        held[k] = jnp.dot(
            factor[k], acc.astype(jnp.bfloat16), preferred_element_type=jnp.float32
        ).astype(jnp.bfloat16)
        stores.append(
            pltpu.make_async_copy(
                held.at[k], out.at[k * 512 : (k + 1) * 512], sems.at[k]
            )
        )
        stores[-1].start()
    for store in stores:
        store.wait()


def cost(flops, moved):
    return pl.CostEstimate(flops=flops, bytes_accessed=moved, transcendentals=0)


def ring(count, shift):
    return [(i, (i + shift) % count) for i in range(count)]


def local(integrals, inverses, lower_blocks):
    rows, total = integrals.shape
    width = total // (NX * NY)
    bf16 = jnp.bfloat16

    first = pl.pallas_call(
        pack_first,
        out_shape=jax.ShapeDtypeStruct((NY, 9, 16, width), bf16),
        in_specs=[ANY, VMEM, VMEM],
        out_specs=VMEM,
        scratch_shapes=[
            pltpu.VMEM((5, 16, 512), bf16),
            pltpu.SemaphoreType.DMA((NY,)),
        ],
        cost_estimate=cost(0, 3 << 20),
    )(integrals.reshape(4, 16, total), inverses, lower_blocks)
    first = lax.all_to_all(first, "y", 0, 0, tiled=True)

    slabs = pl.pallas_call(
        pack_late,
        out_shape=[jax.ShapeDtypeStruct((NY, rows, width), bf16)] * 3,
        in_specs=[ANY],
        out_specs=[VMEM] * 3,
        scratch_shapes=[pltpu.SemaphoreType.DMA((3 * NY,))],
        cost_estimate=cost(0, 3 << 20),
    )(integrals)
    moved = {s: lax.ppermute(slabs[s - 1], "x", ring(NX, s)) for s in (1, 3, 2)}
    late = jnp.stack([moved[s] for s in (1, 2, 3)], axis=1)
    late = lax.all_to_all(late, "y", 0, 0, tiled=True)

    own = {0: first[:, 4:9]}
    for s in (1, 3, 2):
        own[s] = lax.ppermute(own[0], "x", ring(NX, s))
    other = {s: lax.ppermute(own[s], "core", ring(2, 1)) for s in range(NX)}

    return pl.pallas_call(
        solve,
        out_shape=jax.ShapeDtypeStruct((4 * 512, width), bf16),
        in_specs=[VMEM] * 10,
        out_specs=ANY,
        scratch_shapes=[
            pltpu.VMEM((10, 512, 512), bf16),
            pltpu.VMEM((4, 512, width), bf16),
            pltpu.SemaphoreType.DMA((4,)),
        ],
        compiler_params=pltpu.CompilerParams(vmem_limit_bytes=24 << 20),
        cost_estimate=cost(20 * 512**3, 9 << 20),
    )(
        *[own[s] for s in range(NX)],
        *[other[s] for s in range(NX)],
        first,
        late,
    )


def solution(mesh):
    fine = Mesh(mesh.devices.reshape(8, 2, NX, NY), ("z", "core", "x", "y"))
    aux, grp = ("x", "y"), ("z", "core")
    placed = (P(aux, grp), P(None, aux, None), P(None, aux, None))
    return jax.shard_map(
        local,
        mesh=fine,
        in_specs=placed,
        out_specs=P(None, grp + aux),
        check_vma=False,
    )
```

time: 210 us -> 104 us (0.50)
  waiting for transfers between devices: 111 us -> 27.5 us
  blocking collectives: 59.9 us -> 0 us
  starting transfers between devices: 0.04 us -> 59.7 us
  matrix products: 14.8 us -> 0 us
  between operations: 13.5 us -> 0.14 us
  Pallas kernels: 0 us -> 12.3 us
  local copies, waits for them, and re-layouts: 5.24 us -> 1.98 us
    all_gather x2 -> x0, waiting for transfers between devices: 110 us -> none  [the longest x1 84.5 us: local(): lax.all_gather(lower_blocks, 'aux', axis=1, tiled=True)]
    all_to_all x1 -> x0, blocking collectives: 59.9 us -> none  [local(): lax.all_to_all(sectioned, 'aux', split_axis=1, concat_axis=0, tiled=True)]
    ppermute x0 -> x10, starting transfers between devices: none -> 45.4 us  [the longest x4 24.3 us: local(): other = {s: lax.ppermute(own[s], 'core', ring(2, 1)) for s in range(NX)}]
    ppermute x0 -> x10, waiting for transfers between devices: none -> 27.5 us  [the longest x3 19.4 us: local(): moved = {s: lax.ppermute(slabs[s - 1], 'x', ring(NX, s)) for s in (1, 3, 2)}]
    dot_general x7 -> x0, matrix products: 14.8 us -> none  [the longest x4 9.29 us: local(): jnp.dot(inv_all[k], rest, preferred_element_type=jnp.float32)]
    all_to_all x0 -> x2, starting transfers between devices: none -> 14.3 us  [the longest x1 7.66 us: local(): first = lax.all_to_all(first, 'y', 0, 0, tiled=True)]
    pallas_call x0 -> x3, Pallas kernels: none -> 12.3 us  [the longest x1 6.44 us: local(): pl.pallas_call(solve, out_shape=jax.ShapeDtypeStruct((4 * 512, width), bf...]
    convert_element_type x3 -> x0, local copies, waits for them, and re-layouts: 3.24 us -> none  [local(): acc = columns[k * panel:(k + 1) * panel].astype(jnp.float32)]
  transfers between devices with their start and end apart: 2 -> 12, of which waited for: 2 -> 6; matrix products, arithmetic and copies ran while one was open for 4% -> 1% of each run, Pallas kernels for 0% -> 3%
where the time goes in v3:
time: 104 us; the launch traced here: 103 us
  starting transfers between devices  59.7 us (57%)
  waiting for transfers between devices  27.5 us (26%)
  Pallas kernels  12.3 us (12%)
  local copies, waits for them, and re-layouts  1.98 us (2%)
  other arithmetic  1.31 us (1%)
    ppermute x4, starting transfers between devices, local(): other = {s: lax.ppermute(own[s], 'core', ring(2, 1)) for s in range(NX)}  24.3 us
    ppermute x3, waiting for transfers between devices, local(): moved = {s: lax.ppermute(slabs[s - 1], 'x', ring(NX, s)) for s in (1, 3, 2)}  19.4 us
    ppermute x3, starting transfers between devices, local(): own[s] = lax.ppermute(own[0], 'x', ring(NX, s))  10.6 us
    ppermute x3, starting transfers between devices, local(): moved = {s: lax.ppermute(slabs[s - 1], 'x', ring(NX, s)) for s in (1, 3, 2)}  10.5 us
    all_to_all x1, starting transfers between devices, local(): first = lax.all_to_all(first, 'y', 0, 0, tiled=True)  7.66 us
    ppermute x3, waiting for transfers between devices, local(): own[s] = lax.ppermute(own[0], 'x', ring(NX, s))  6.91 us
    all_to_all x1, starting transfers between devices, local(): late = lax.all_to_all(late, 'y', 0, 0, tiled=True)  6.63 us
    pallas_call x1, Pallas kernels, local(): pl.pallas_call(solve, out_shape=jax.ShapeDtypeStruct((4 * 512, width), bf...  6.44 us
  transfers between devices with their start and end apart: 12, of which 6 were waited for; matrix products, arithmetic and copies ran while one was open for 1% of the time, Pallas kernels for 3%

profile of v3, /device:TPU:1, one launch (start us, length us, event | category | flops | bytes accessed | tf_op | source)
XLA Modules:
  0.0 102.9 jit_solution(17199978457808883584)
XLA Ops:
  0.0 3.1 %shard_map.37 = bf16[8,9,16,512]{3,2,1,0:T(8,128)(2,1)} custom-call(bf16[4,16,16384]{2,1,0:T(8,128)(2,1)} %bitcast.4, bf16[4,16,512]{2,1,0:T(8,128)(2,1)} %inverses.1, bf16[6,16,512]{2,1,0:T(8,128)(2,1)} %lower_blocks.1), custom_call_target="tpu_custom_call" | custom-call | bytes 3145728 | tf_op jit(solution)/shard_map/pallas_call | solution.py:111
  3.1 7.7 %all-to-all-start = ((bf16[8,9,16,512]{3,2,1,0:T(8,128)(2,1)}), bf16[8,9,16,512]{3,2,1,0:T(8,128)(2,1)S(1)}, u32[]{:S(2)}, u32[]{:S(2)}) async-start(bf16[8,9,16,512]{3,2,1,0:T(8,128)(2,1)} %shard_map.37), calls=%async_computation | async-start | bytes 2359296 | tf_op jit(solution)/shard_map/all_to_all | solution.py:122
  10.8 2.8 %shard_map.38 = (bf16[8,64,512]{2,1,0:T(8,128)(2,1)}, bf16[8,64,512]{2,1,0:T(8,128)(2,1)}, bf16[8,64,512]{2,1,0:T(8,128)(2,1)}) custom-call(bf16[64,16384]{1,0:T(8,128)(2,1)} %integrals.1), custom_call_target="tpu_custom_call" | custom-call | bytes 3145728 | tf_op jit(solution)/shard_map/pallas_call | solution.py:124
  13.5 3.1 %collective-permute-start.7 = (bf16[8,64,512]{2,1,0:T(8,128)(2,1)}, bf16[8,64,512]{2,1,0:T(8,128)(2,1)S(1)}, u32[]{:S(2)}, u32[]{:S(2)}) collective-permute-start(bf16[8,64,512]{2,1,0:T(8,128)(2,1)} %get-tuple-element.8), channel_id=1, source_target_pairs={{0,8},{8,16},{16,24},{24,0},{1,9},{9,17},{17,25},{25,1},{2,10},{10... | collective-permute-start | bytes 1572872 | tf_op jit(solution)/shard_map/ppermute | solution.py:132
  16.7 4.4 %collective-permute-start.8 = (bf16[8,64,512]{2,1,0:T(8,128)(2,1)}, bf16[8,64,512]{2,1,0:T(8,128)(2,1)S(1)}, u32[]{:S(2)}, u32[]{:S(2)}) collective-permute-start(bf16[8,64,512]{2,1,0:T(8,128)(2,1)} %get-tuple-element.9), channel_id=1, source_target_pairs={{0,16},{8,24},{16,0},{24,8},{1,17},{9,25},{17,1},{25,9},{2,18},{10... | collective-permute-start | bytes 1572872 | tf_op jit(solution)/shard_map/ppermute | solution.py:132
  21.0 3.1 %collective-permute-start.9 = (bf16[8,64,512]{2,1,0:T(8,128)(2,1)}, bf16[8,64,512]{2,1,0:T(8,128)(2,1)S(1)}, u32[]{:S(2)}, u32[]{:S(2)}) collective-permute-start(bf16[8,64,512]{2,1,0:T(8,128)(2,1)} %get-tuple-element.10), channel_id=1, source_target_pairs={{0,24},{8,0},{16,8},{24,16},{1,25},{9,1},{17,9},{25,17},{2,26},{10... | collective-permute-start | bytes 1572872 | tf_op jit(solution)/shard_map/ppermute | solution.py:132
  24.1 3.4 %collective-permute-done.7 = bf16[8,64,512]{2,1,0:T(8,128)(2,1)S(1)} collective-permute-done((bf16[8,64,512]{2,1,0:T(8,128)(2,1)}, bf16[8,64,512]{2,1,0:T(8,128)(2,1)S(1)}, u32[]{:S(2)}, u32[]{:S(2)}) %collective-permute-start.7) | collective-permute-done | bytes 524320 | tf_op jit(solution)/shard_map/ppermute | solution.py:132
  27.5 14.1 %collective-permute-done.8 = bf16[8,64,512]{2,1,0:T(8,128)(2,1)S(1)} collective-permute-done((bf16[8,64,512]{2,1,0:T(8,128)(2,1)}, bf16[8,64,512]{2,1,0:T(8,128)(2,1)S(1)}, u32[]{:S(2)}, u32[]{:S(2)}) %collective-permute-start.8) | collective-permute-done | bytes 524320 | tf_op jit(solution)/shard_map/ppermute | solution.py:132
  41.5 2.0 %collective-permute-done.9 = bf16[8,64,512]{2,1,0:T(8,128)(2,1)S(1)} collective-permute-done((bf16[8,64,512]{2,1,0:T(8,128)(2,1)}, bf16[8,64,512]{2,1,0:T(8,128)(2,1)S(1)}, u32[]{:S(2)}, u32[]{:S(2)}) %collective-permute-start.9) | collective-permute-done | bytes 524320 | tf_op jit(solution)/shard_map/ppermute | solution.py:132
  43.5 1.3 %pad_maximum_fusion = bf16[8,3,64,512]{3,2,1,0:T(8,128)(2,1)} fusion(bf16[8,1,64,512]{3,2,1,0:T(8,128)(2,1)S(1)} %bitcast.7, bf16[8,1,64,512]{3,2,1,0:T(8,128)(2,1)S(1)} %bitcast.6, bf16[8,1,64,512]{3,2,1,0:T(8,128)(2,1)S(1)} %bitcast.5), kind=kLoop, calls=%fused_computation | loop fusion | flops 1572864 | bytes 3145728 | tf_op jit(solution)/shard_map/stack | solution.py:133
  44.8 0.0 all-to-all-done.refs_8_
  44.8 6.6 %all-to-all-start.1 = ((bf16[8,3,64,512]{3,2,1,0:T(8,128)(2,1)}), bf16[8,3,64,512]{3,2,1,0:T(8,128)(2,1)S(1)}, u32[]{:S(2)}, u32[]{:S(2)}) async-start(bf16[8,3,64,512]{3,2,1,0:T(8,128)(2,1)} %pad_maximum_fusion), calls=%async_computation.1 | async-start | bytes 3145728 | tf_op jit(solution)/shard_map/all_to_all | solution.py:134
  51.5 5.2 %collective-permute-start.2 = (bf16[8,5,16,512]{3,2,1,0:T(8,128)(2,1)S(1)}, bf16[8,5,16,512]{3,2,1,0:T(8,128)(2,1)}, u32[]{:S(2)}, u32[]{:S(2)}) collective-permute-start(bf16[8,5,16,512]{3,2,1,0:T(8,128)(2,1)S(1)} %slice.4.refs_0_), channel_id=1, source_target_pairs={{0,24},{8,0},{16,8},{24,16},{1,25},{9,1},{17,9},{25,17},{2,26},{10... | collective-permute-start | bytes 1966088 | tf_op jit(solution)/shard_map/ppermute | solution.py:138
  56.7 3.4 %collective-permute-start.1 = (bf16[8,5,16,512]{3,2,1,0:T(8,128)(2,1)S(1)}, bf16[8,5,16,512]{3,2,1,0:T(8,128)(2,1)}, u32[]{:S(2)}, u32[]{:S(2)}) collective-permute-start(bf16[8,5,16,512]{3,2,1,0:T(8,128)(2,1)S(1)} %slice.4.refs_0_), channel_id=1, source_target_pairs={{0,16},{8,24},{16,0},{24,8},{1,17},{9,25},{17,1},{25,9},{2,18},{10... | collective-permute-start | bytes 1966088 | tf_op jit(solution)/shard_map/ppermute | solution.py:138
  60.2 1.9 %collective-permute-start = (bf16[8,5,16,512]{3,2,1,0:T(8,128)(2,1)S(1)}, bf16[8,5,16,512]{3,2,1,0:T(8,128)(2,1)}, u32[]{:S(2)}, u32[]{:S(2)}) collective-permute-start(bf16[8,5,16,512]{3,2,1,0:T(8,128)(2,1)S(1)} %slice.4.refs_0_), channel_id=1, source_target_pairs={{0,8},{8,16},{16,24},{24,0},{1,9},{9,17},{17,25},{25,1},{2,10},{10... | collective-permute-start | bytes 1966088 | tf_op jit(solution)/shard_map/ppermute | solution.py:138
  62.1 3.2 %collective-permute-start.3 = (bf16[8,5,16,512]{3,2,1,0:T(8,128)(2,1)S(1)}, bf16[8,5,16,512]{3,2,1,0:T(8,128)(2,1)S(1)}, u32[]{:S(2)}, u32[]{:S(2)}) collective-permute-start(bf16[8,5,16,512]{3,2,1,0:T(8,128)(2,1)S(1)} %slice.4.refs_0_), channel_id=1, source_target_pairs={{0,32},{32,0},{1,33},{33,1},{2,34},{34,2},{3,35},{35,3},{4,36},{36... | collective-permute-start | bytes 1966088 | tf_op jit(solution)/shard_map/ppermute | solution.py:139
  65.4 5.6 %collective-permute-done.2.refs_3_ = bf16[8,5,16,512]{3,2,1,0:T(8,128)(2,1)} collective-permute-done((bf16[8,5,16,512]{3,2,1,0:T(8,128)(2,1)S(1)}, bf16[8,5,16,512]{3,2,1,0:T(8,128)(2,1)}, u32[]{:S(2)}, u32[]{:S(2)}) %collective-permute-start.2) | collective-permute-done | bytes 655392 | tf_op jit(solution)/shard_map/ppermute | solution.py:138
  70.9 16.7 %collective-permute-start.6 = (bf16[8,5,16,512]{3,2,1,0:T(8,128)(2,1)}, bf16[8,5,16,512]{3,2,1,0:T(8,128)(2,1)}, u32[]{:S(2)}, u32[]{:S(2)}) collective-permute-start(bf16[8,5,16,512]{3,2,1,0:T(8,128)(2,1)} %collective-permute-done.2.refs_3_), channel_id=1, source_target_pairs={{0,32},{32,0},{1,33},{33,1},{2,34},{34,2},{3,35},{35,3},{4,36},{36... | collective-permute-start | bytes 1966088 | tf_op jit(solution)/shard_map/ppermute | solution.py:139
  87.6 0.0 collective-permute-done.1.refs_2_
  87.7 1.9 %collective-permute-start.5 = (bf16[8,5,16,512]{3,2,1,0:T(8,128)(2,1)}, bf16[8,5,16,512]{3,2,1,0:T(8,128)(2,1)}, u32[]{:S(2)}, u32[]{:S(2)}) collective-permute-start(bf16[8,5,16,512]{3,2,1,0:T(8,128)(2,1)} %collective-permute-done.1.refs_2_), channel_id=1, source_target_pairs={{0,32},{32,0},{1,33},{33,1},{2,34},{34,2},{3,35},{35,3},{4,36},{36... | collective-permute-start | bytes 1966088 | tf_op jit(solution)/shard_map/ppermute | solution.py:139
  89.6 1.4 %collective-permute-done.refs_1_ = bf16[8,5,16,512]{3,2,1,0:T(8,128)(2,1)} collective-permute-done((bf16[8,5,16,512]{3,2,1,0:T(8,128)(2,1)S(1)}, bf16[8,5,16,512]{3,2,1,0:T(8,128)(2,1)}, u32[]{:S(2)}, u32[]{:S(2)}) %collective-permute-start) | collective-permute-done | bytes 655392 | tf_op jit(solution)/shard_map/ppermute | solution.py:138
  90.9 2.4 %collective-permute-start.4 = (bf16[8,5,16,512]{3,2,1,0:T(8,128)(2,1)}, bf16[8,5,16,512]{3,2,1,0:T(8,128)(2,1)}, u32[]{:S(2)}, u32[]{:S(2)}) collective-permute-start(bf16[8,5,16,512]{3,2,1,0:T(8,128)(2,1)} %collective-permute-done.refs_1_), channel_id=1, source_target_pairs={{0,32},{32,0},{1,33},{33,1},{2,34},{34,2},{3,35},{35,3},{4,36},{36... | collective-permute-start | bytes 1966088 | tf_op jit(solution)/shard_map/ppermute | solution.py:139
  93.3 0.0 collective-permute-done.3.refs_4_
  93.3 0.0 copy-start
  93.4 0.8 copy-done
  94.2 0.0 all-to-all-done.1.refs_9_
  94.2 0.0 collective-permute-done.6.refs_7_
  94.2 0.0 collective-permute-done.5.refs_6_
  94.2 1.2 %collective-permute-done.4.refs_5_ = bf16[8,5,16,512]{3,2,1,0:T(8,128)(2,1)} collective-permute-done((bf16[8,5,16,512]{3,2,1,0:T(8,128)(2,1)}, bf16[8,5,16,512]{3,2,1,0:T(8,128)(2,1)}, u32[]{:S(2)}, u32[]{:S(2)}) %collective-permute-start.4) | collective-permute-done | bytes 655392 | tf_op jit(solution)/shard_map/ppermute | solution.py:139
  95.4 0.0 copy-start.1
  95.4 1.1 %copy-done.1 = bf16[8,5,16,512]{3,2,1,0:T(8,128)(2,1)S(1)} copy-done((bf16[8,5,16,512]{3,2,1,0:T(8,128)(2,1)S(1)}, bf16[8,5,16,512]{3,2,1,0:T(8,128)(2,1)}, u32[]{:S(2)}) %copy-start.1) | copy-done | bytes 655384
  96.5 6.4 %shard_map.39 = bf16[2048,512]{1,0:T(8,128)(2,1)} custom-call(bf16[8,5,16,512]{3,2,1,0:T(8,128)(2,1)S(1)} %slice.4.refs_0_, bf16[8,5,16,512]{3,2,1,0:T(8,128)(2,1)} %collective-permute-done.refs_1_, bf16[8,5,16,512]{3,2,1,0:T(8,128)(2,1)} %collective-permute-done.1.refs_2_, bf16[8,5,16,512]{3,2,1,0:T(8,128)(2,1)} %collective-permute-done.2.refs_3_, ...), custom_call_target="tpu_custom_call" | custom-call | flops 2684354560 | bytes 9437184 | tf_op jit(solution)/shard_map/pallas_call | solution.py:141
  (1 shorter events, 0.0 us)
Async XLA Ops:
  3.1 41.7 %all-to-all-start = ((bf16[8,9,16,512]{3,2,1,0:T(8,128)(2,1)}), bf16[8,9,16,512]{3,2,1,0:T(8,128)(2,1)S(1)}, u32[]{:S(2)}, u32[]{:S(2)}) async-start(bf16[8,9,16,512]{3,2,1,0:T(8,128)(2,1)} %shard_map.37), calls=%async_computation | async-start | bytes 2359296 | tf_op jit(solution)/shard_map/all_to_all | solution.py:122
  13.5 13.9 %collective-permute-start.7 = (bf16[8,64,512]{2,1,0:T(8,128)(2,1)}, bf16[8,64,512]{2,1,0:T(8,128)(2,1)S(1)}, u32[]{:S(2)}, u32[]{:S(2)}) collective-permute-start(bf16[8,64,512]{2,1,0:T(8,128)(2,1)} %get-tuple-element.8), channel_id=1, source_target_pairs={{0,8},{8,16},{16,24},{24,0},{1,9},{9,17},{17,25},{25,1},{2,10},{10... | collective-permute-start | bytes 1572872 | tf_op jit(solution)/shard_map/ppermute | solution.py:132
  16.7 24.9 %collective-permute-start.8 = (bf16[8,64,512]{2,1,0:T(8,128)(2,1)}, bf16[8,64,512]{2,1,0:T(8,128)(2,1)S(1)}, u32[]{:S(2)}, u32[]{:S(2)}) collective-permute-start(bf16[8,64,512]{2,1,0:T(8,128)(2,1)} %get-tuple-element.9), channel_id=1, source_target_pairs={{0,16},{8,24},{16,0},{24,8},{1,17},{9,25},{17,1},{25,9},{2,18},{10... | collective-permute-start | bytes 1572872 | tf_op jit(solution)/shard_map/ppermute | solution.py:132
  21.0 22.5 %collective-permute-start.9 = (bf16[8,64,512]{2,1,0:T(8,128)(2,1)}, bf16[8,64,512]{2,1,0:T(8,128)(2,1)S(1)}, u32[]{:S(2)}, u32[]{:S(2)}) collective-permute-start(bf16[8,64,512]{2,1,0:T(8,128)(2,1)} %get-tuple-element.10), channel_id=1, source_target_pairs={{0,24},{8,0},{16,8},{24,16},{1,25},{9,1},{17,9},{25,17},{2,26},{10... | collective-permute-start | bytes 1572872 | tf_op jit(solution)/shard_map/ppermute | solution.py:132
  44.8 49.4 %all-to-all-start.1 = ((bf16[8,3,64,512]{3,2,1,0:T(8,128)(2,1)}), bf16[8,3,64,512]{3,2,1,0:T(8,128)(2,1)S(1)}, u32[]{:S(2)}, u32[]{:S(2)}) async-start(bf16[8,3,64,512]{3,2,1,0:T(8,128)(2,1)} %pad_maximum_fusion), calls=%async_computation.1 | async-start | bytes 3145728 | tf_op jit(solution)/shard_map/all_to_all | solution.py:134
  51.5 19.4 %collective-permute-start.2 = (bf16[8,5,16,512]{3,2,1,0:T(8,128)(2,1)S(1)}, bf16[8,5,16,512]{3,2,1,0:T(8,128)(2,1)}, u32[]{:S(2)}, u32[]{:S(2)}) collective-permute-start(bf16[8,5,16,512]{3,2,1,0:T(8,128)(2,1)S(1)} %slice.4.refs_0_), channel_id=1, source_target_pairs={{0,24},{8,0},{16,8},{24,16},{1,25},{9,1},{17,9},{25,17},{2,26},{10... | collective-permute-start | bytes 1966088 | tf_op jit(solution)/shard_map/ppermute | solution.py:138
  56.7 30.9 %collective-permute-start.1 = (bf16[8,5,16,512]{3,2,1,0:T(8,128)(2,1)S(1)}, bf16[8,5,16,512]{3,2,1,0:T(8,128)(2,1)}, u32[]{:S(2)}, u32[]{:S(2)}) collective-permute-start(bf16[8,5,16,512]{3,2,1,0:T(8,128)(2,1)S(1)} %slice.4.refs_0_), channel_id=1, source_target_pairs={{0,16},{8,24},{16,0},{24,8},{1,17},{9,25},{17,1},{25,9},{2,18},{10... | collective-permute-start | bytes 1966088 | tf_op jit(solution)/shard_map/ppermute | solution.py:138
  60.2 30.8 %collective-permute-start = (bf16[8,5,16,512]{3,2,1,0:T(8,128)(2,1)S(1)}, bf16[8,5,16,512]{3,2,1,0:T(8,128)(2,1)}, u32[]{:S(2)}, u32[]{:S(2)}) collective-permute-start(bf16[8,5,16,512]{3,2,1,0:T(8,128)(2,1)S(1)} %slice.4.refs_0_), channel_id=1, source_target_pairs={{0,8},{8,16},{16,24},{24,0},{1,9},{9,17},{17,25},{25,1},{2,10},{10... | collective-permute-start | bytes 1966088 | tf_op jit(solution)/shard_map/ppermute | solution.py:138
  62.1 31.2 %collective-permute-start.3 = (bf16[8,5,16,512]{3,2,1,0:T(8,128)(2,1)S(1)}, bf16[8,5,16,512]{3,2,1,0:T(8,128)(2,1)S(1)}, u32[]{:S(2)}, u32[]{:S(2)}) collective-permute-start(bf16[8,5,16,512]{3,2,1,0:T(8,128)(2,1)S(1)} %slice.4.refs_0_), channel_id=1, source_target_pairs={{0,32},{32,0},{1,33},{33,1},{2,34},{34,2},{3,35},{35,3},{4,36},{36... | collective-permute-start | bytes 1966088 | tf_op jit(solution)/shard_map/ppermute | solution.py:139
  70.9 23.3 %collective-permute-start.6 = (bf16[8,5,16,512]{3,2,1,0:T(8,128)(2,1)}, bf16[8,5,16,512]{3,2,1,0:T(8,128)(2,1)}, u32[]{:S(2)}, u32[]{:S(2)}) collective-permute-start(bf16[8,5,16,512]{3,2,1,0:T(8,128)(2,1)} %collective-permute-done.2.refs_3_), channel_id=1, source_target_pairs={{0,32},{32,0},{1,33},{33,1},{2,34},{34,2},{3,35},{35,3},{4,36},{36... | collective-permute-start | bytes 1966088 | tf_op jit(solution)/shard_map/ppermute | solution.py:139
  87.7 6.6 %collective-permute-start.5 = (bf16[8,5,16,512]{3,2,1,0:T(8,128)(2,1)}, bf16[8,5,16,512]{3,2,1,0:T(8,128)(2,1)}, u32[]{:S(2)}, u32[]{:S(2)}) collective-permute-start(bf16[8,5,16,512]{3,2,1,0:T(8,128)(2,1)} %collective-permute-done.1.refs_2_), channel_id=1, source_target_pairs={{0,32},{32,0},{1,33},{33,1},{2,34},{34,2},{3,35},{35,3},{4,36},{36... | collective-permute-start | bytes 1966088 | tf_op jit(solution)/shard_map/ppermute | solution.py:139
  90.9 4.4 %collective-permute-start.4 = (bf16[8,5,16,512]{3,2,1,0:T(8,128)(2,1)}, bf16[8,5,16,512]{3,2,1,0:T(8,128)(2,1)}, u32[]{:S(2)}, u32[]{:S(2)}) collective-permute-start(bf16[8,5,16,512]{3,2,1,0:T(8,128)(2,1)} %collective-permute-done.refs_1_), channel_id=1, source_target_pairs={{0,32},{32,0},{1,33},{33,1},{2,34},{34,2},{3,35},{35,3},{4,36},{36... | collective-permute-start | bytes 1966088 | tf_op jit(solution)/shard_map/ppermute | solution.py:139
  93.3 0.9 copy-start
  95.4 1.1 %copy-start.1 = (bf16[8,5,16,512]{3,2,1,0:T(8,128)(2,1)S(1)}, bf16[8,5,16,512]{3,2,1,0:T(8,128)(2,1)}, u32[]{:S(2)}) copy-start(bf16[8,5,16,512]{3,2,1,0:T(8,128)(2,1)} %copy-done) | copy-start | bytes 1966084

commit v4 on v0

v4 whole, which is shorter than its diff:
```python
import jax
import jax.numpy as jnp
from jax import lax
from jax.experimental import pallas as pl
from jax.experimental.pallas import tpu as pltpu
from jax.sharding import Mesh, PartitionSpec as P

NX, NY, NZ = 4, 8, 8
NAUX = NX * NY
AHEAD = 3
SPLIT = 1
UNITS = 5
GROUPS = ((0, 1, 7), (2, 6), (3, 5), (4,))
ANY = pl.BlockSpec(memory_space=pl.ANY)
VMEM = pl.BlockSpec(memory_space=pltpu.VMEM)


def assemble(*refs):
    own, swapped, factor = refs[:NZ], refs[NZ:-1], refs[-1]
    z, core = lax.axis_index("z"), lax.axis_index("core")
    other = {}
    for group, ref in zip(GROUPS, swapped):
        for at, d in enumerate(group):
            other[d] = (ref, at * UNITS)
    for d in range(NZ):
        unit = lax.rem(z + NZ - d, NZ) * UNITS
        for (ref, at), half in (((own[d], 0), core), (other[d], 1 - core)):
            row = pl.multiple_of(half * 256, 256)
            for i in range(UNITS):
                factor[unit + i, pl.ds(row, 256), :] = ref[at + i]


def product(panels, block, solved):
    left = jnp.concatenate([panels[4 * block + q] for q in range(4)], axis=1)
    out = jnp.dot(left, solved, preferred_element_type=jnp.float32)
    return jnp.concatenate(
        [
            out[half * 256 + aux * 8 : half * 256 + aux * 8 + 8]
            for aux in range(NAUX)
            for half in range(2)
        ],
        axis=0,
    )


def solve(factor, columns, out, panels, held, sems):
    below = [[4 + k * (k - 1) // 2 + j for j in range(k)] for k in range(4)]
    order = [b for k in range(4) for b in below[k] + [k]]
    loads = {}
    for b in order:
        units = pl.ds(4 * b, 4)
        loads[b] = pltpu.make_async_copy(
            factor.at[units], panels.at[units], sems.at[b]
        )

    def ready(b):
        loads[b].wait()
        ahead = order.index(b) + AHEAD
        if ahead < len(order):
            loads[order[ahead]].start()

    for b in order[:AHEAD]:
        loads[b].start()
    stores = []
    width = columns.shape[1] // SPLIT
    for k in range(4):
        rows = slice(k * 512, (k + 1) * 512)
        cuts = [slice(h * width, (h + 1) * width) for h in range(SPLIT)]
        acc = [columns[rows, cut].astype(jnp.float32) for cut in cuts]
        for j, b in enumerate(below[k]):
            ready(b)
            for h, cut in enumerate(cuts):
                acc[h] = acc[h] - product(panels, b, held[j, :, cut])
        ready(k)
        for h, cut in enumerate(cuts):
            held[k, :, cut] = product(panels, k, acc[h].astype(jnp.bfloat16)).astype(
                jnp.bfloat16
            )
        stores.append(pltpu.make_async_copy(held.at[k], out.at[rows], sems.at[10 + k]))
        stores[-1].start()
    for store in stores:
        store.wait()


def cost(flops, moved):
    return pl.CostEstimate(flops=flops, bytes_accessed=moved, transcendentals=0)


def ring(count, shift):
    return [(i, (i + shift) % count) for i in range(count)]


def local(integrals, inverses, lower_blocks):
    rows, total = integrals.shape
    width = total // NAUX
    bf16 = jnp.bfloat16

    blocks = jnp.concatenate([inverses, lower_blocks], axis=0)
    blocks = lax.dynamic_slice_in_dim(blocks, 8 * lax.axis_index("core"), 8, 1)
    units = blocks.reshape(10, 8, 4, 128).transpose(0, 2, 1, 3).reshape(40, 8, 128)
    units = lax.dynamic_slice_in_dim(units, UNITS * lax.axis_index("z"), UNITS, 0)
    piece = jnp.broadcast_to(units[None], (NAUX, UNITS, 8, 128))
    piece = lax.all_to_all(piece, ("x", "y"), 0, 0, tiled=True)

    sections = integrals.reshape(rows, NAUX, width).transpose(1, 0, 2)
    sections, piece = lax.optimization_barrier((sections, piece))
    columns = lax.all_to_all(sections, ("x", "y"), 0, 0, tiled=True)

    own = {0: piece.transpose(1, 0, 2, 3).reshape(UNITS, NAUX * 8, 128)}
    for d in range(1, 5):
        own[d] = lax.ppermute(own[d - 1], "z", ring(NZ, 1))
        if d < 4:
            own[-d % NZ] = lax.ppermute(own[(1 - d) % NZ], "z", ring(NZ, -1))
    swapped = []
    for group in GROUPS:
        held = jnp.concatenate([own[d] for d in group], axis=0)
        swapped.append(lax.ppermute(held, "core", ring(2, 1)))

    factor = pl.pallas_call(
        assemble,
        out_shape=jax.ShapeDtypeStruct((40, 512, 128), bf16),
        in_specs=[VMEM] * (NZ + len(GROUPS)),
        out_specs=VMEM,
        compiler_params=pltpu.CompilerParams(vmem_limit_bytes=16 << 20),
        cost_estimate=cost(0, 10 << 20),
    )(*[own[d] for d in range(NZ)], *swapped)

    return pl.pallas_call(
        solve,
        out_shape=jax.ShapeDtypeStruct((4 * 512, width), bf16),
        in_specs=[ANY, VMEM],
        out_specs=ANY,
        scratch_shapes=[
            pltpu.VMEM((40, 512, 128), bf16),
            pltpu.VMEM((4, 512, width), bf16),
            pltpu.SemaphoreType.DMA((14,)),
        ],
        compiler_params=pltpu.CompilerParams(vmem_limit_bytes=48 << 20),
        cost_estimate=cost(20 * 512**3, 9 << 20),
    )(factor, columns.reshape(4 * 512, width))


def solution(mesh):
    fine = Mesh(mesh.devices.reshape(NZ, 2, NX, NY), ("z", "core", "x", "y"))
    aux, grp = ("x", "y"), ("z", "core")
    placed = (P(aux, grp), P(None, aux, None), P(None, aux, None))
    return jax.shard_map(
        local,
        mesh=fine,
        in_specs=placed,
        out_specs=P(None, grp + aux),
        check_vma=False,
    )
```

time: 210 us -> 97.6 us (0.46)
  waiting for transfers between devices: 111 us -> 15.3 us
  starting transfers between devices: 0.04 us -> 67.2 us
  blocking collectives: 59.9 us -> 0 us
  matrix products: 14.8 us -> 0 us
  between operations: 13.5 us -> 0.22 us
  Pallas kernels: 0 us -> 6.78 us
    all_gather x2 -> x0, waiting for transfers between devices: 110 us -> none  [the longest x1 84.5 us: local(): lax.all_gather(lower_blocks, 'aux', axis=1, tiled=True)]
    all_to_all x1 -> x0, blocking collectives: 59.9 us -> none  [local(): lax.all_to_all(sectioned, 'aux', split_axis=1, concat_axis=0, tiled=True)]
    ppermute x0 -> x11, starting transfers between devices: none -> 49.5 us  [the longest x3 21.3 us: local(): own[-d % NZ] = lax.ppermute(own[(1 - d) % NZ], 'z', ring(NZ, -1))]
    all_to_all x0 -> x2, starting transfers between devices: none -> 17.7 us  [the longest x1 10.5 us: local(): piece = lax.all_to_all(piece, ('x', 'y'), 0, 0, tiled=True)]
    dot_general x7 -> x0, matrix products: 14.8 us -> none  [the longest x4 9.29 us: local(): jnp.dot(inv_all[k], rest, preferred_element_type=jnp.float32)]
    ppermute x0 -> x11, waiting for transfers between devices: none -> 8.29 us  [the longest x3 5.58 us: local(): own[-d % NZ] = lax.ppermute(own[(1 - d) % NZ], 'z', ring(NZ, -1))]
    all_to_all x0 -> x2, waiting for transfers between devices: none -> 6.99 us  [the longest x1 6.99 us: local(): piece = lax.all_to_all(piece, ('x', 'y'), 0, 0, tiled=True)]
    pallas_call x0 -> x2, Pallas kernels: none -> 6.78 us  [the longest x1 6.42 us: local(): pl.pallas_call(solve, out_shape=jax.ShapeDtypeStruct((4 * 512, width), bf...]
  transfers between devices with their start and end apart: 2 -> 13, of which waited for: 2 -> 5; matrix products, arithmetic and copies ran while one was open for 4% -> 4% of each run, Pallas kernels for 0% -> 0%
where the time goes in v4:
time: 97.6 us; the launch traced here: 96.9 us
  starting transfers between devices  67.2 us (69%)
  waiting for transfers between devices  15.3 us (16%)
  Pallas kernels  6.78 us (7%)
  local copies, waits for them, and re-layouts  6.34 us (6%)
  other arithmetic  1.07 us (1%)
    ppermute x3, starting transfers between devices, local(): own[-d % NZ] = lax.ppermute(own[(1 - d) % NZ], 'z', ring(NZ, -1))  21.3 us
    ppermute x4, starting transfers between devices, local(): swapped.append(lax.ppermute(held, 'core', ring(2, 1)))  20.5 us
    all_to_all x1, starting transfers between devices, local(): piece = lax.all_to_all(piece, ('x', 'y'), 0, 0, tiled=True)  10.5 us
    ppermute x4, starting transfers between devices, local(): own[d] = lax.ppermute(own[d - 1], 'z', ring(NZ, 1))  7.68 us
    all_to_all x1, starting transfers between devices, local(): columns = lax.all_to_all(sections, ('x', 'y'), 0, 0, tiled=True)  7.23 us
    all_to_all x1, waiting for transfers between devices, local(): piece = lax.all_to_all(piece, ('x', 'y'), 0, 0, tiled=True)  6.99 us
    pallas_call x1, Pallas kernels, local(): pl.pallas_call(solve, out_shape=jax.ShapeDtypeStruct((4 * 512, width), bf...  6.42 us
    ppermute x3, waiting for transfers between devices, local(): own[-d % NZ] = lax.ppermute(own[(1 - d) % NZ], 'z', ring(NZ, -1))  5.58 us
  transfers between devices with their start and end apart: 13, of which 5 were waited for; matrix products, arithmetic and copies ran while one was open for 4% of the time, Pallas kernels for 0%

profile of v4, /device:TPU:1, one launch (start us, length us, event | category | flops | bytes accessed | tf_op | source)
XLA Modules:
  0.0 96.9 jit_solution(12757452315358325085)
XLA Ops:
  0.0 0.8 fusion
  0.9 0.8 broadcast_in_dim.2
  1.7 10.5 %all-to-all-start = ((bf16[32,5,8,128]{3,2,1,0:T(8,128)(2,1)}), bf16[32,5,8,128]{3,2,1,0:T(8,128)(2,1)S(1)}, u32[]{:S(2)}, u32[]{:S(2)}) async-start(bf16[32,5,8,128]{3,2,1,0:T(8,128)(2,1)} %broadcast_in_dim.2), calls=%async_computation | async-start | bytes 655360 | tf_op jit(solution)/shard_map/all_to_all | solution.py:103
  12.2 3.2 %copy.10 = bf16[8,32,8,512]{3,2,0,1:T(8,128)(2,1)} copy(bf16[8,32,8,512]{3,2,1,0:T(8,128)(2,1)} %bitcast.16) | data formatting | bytes 4194304 | tf_op jit(solution)/shard_map/reshape | solution.py:105
  15.4 7.0 %all-to-all-done = bf16[32,5,8,128]{3,2,1,0:T(8,128)(2,1)S(1)} async-done(((bf16[32,5,8,128]{3,2,1,0:T(8,128)(2,1)}), bf16[32,5,8,128]{3,2,1,0:T(8,128)(2,1)S(1)}, u32[]{:S(2)}, u32[]{:S(2)}) %all-to-all-start) | async-done | bytes 327712 | tf_op jit(solution)/shard_map/all_to_all | solution.py:103
  22.3 7.2 %all-to-all-start.1 = ((bf16[32,64,512]{2,1,0:T(8,128)(2,1)}), bf16[32,64,512]{2,1,0:T(8,128)(2,1)S(1)}, u32[]{:S(2)}, u32[]{:S(2)}) async-start(bf16[32,64,512]{2,1,0:T(8,128)(2,1)} %bitcast.15), calls=%async_computation.1 | async-start | bytes 4194304 | tf_op jit(solution)/shard_map/all_to_all | solution.py:107
  29.6 0.1 copy_bitcast_fusion.refs_0_
  29.6 10.7 %collective-permute-start.4 = (bf16[5,256,128]{2,1,0:T(8,128)(2,1)S(1)}, bf16[5,256,128]{2,1,0:T(8,128)(2,1)S(1)}, u32[]{:S(2)}, u32[]{:S(2)}) collective-permute-start(bf16[5,256,128]{2,1,0:T(8,128)(2,1)S(1)} %copy_bitcast_fusion.refs_0_), channel_id=1, source_target_pairs={{0,448},{64,0},{128,64},{192,128},{256,192},{320,256},{384,320},{4... | collective-permute-start | bytes 983048 | tf_op jit(solution)/shard_map/ppermute | solution.py:113
  40.3 1.9 %collective-permute-start = (bf16[5,256,128]{2,1,0:T(8,128)(2,1)S(1)}, bf16[5,256,128]{2,1,0:T(8,128)(2,1)S(1)}, u32[]{:S(2)}, u32[]{:S(2)}) collective-permute-start(bf16[5,256,128]{2,1,0:T(8,128)(2,1)S(1)} %copy_bitcast_fusion.refs_0_), channel_id=1, source_target_pairs={{0,64},{64,128},{128,192},{192,256},{256,320},{320,384},{384,448},... | collective-permute-start | bytes 983048 | tf_op jit(solution)/shard_map/ppermute | solution.py:111
  42.3 3.3 %collective-permute-done.4.refs_7_ = bf16[5,256,128]{2,1,0:T(8,128)(2,1)S(1)} collective-permute-done((bf16[5,256,128]{2,1,0:T(8,128)(2,1)S(1)}, bf16[5,256,128]{2,1,0:T(8,128)(2,1)S(1)}, u32[]{:S(2)}, u32[]{:S(2)}) %collective-permute-start.4) | collective-permute-done | bytes 327712 | tf_op jit(solution)/shard_map/ppermute | solution.py:113
  45.5 5.3 %collective-permute-start.5 = (bf16[5,256,128]{2,1,0:T(8,128)(2,1)S(1)}, bf16[5,256,128]{2,1,0:T(8,128)(2,1)S(1)}, u32[]{:S(2)}, u32[]{:S(2)}) collective-permute-start(bf16[5,256,128]{2,1,0:T(8,128)(2,1)S(1)} %collective-permute-done.4.refs_7_), channel_id=1, source_target_pairs={{0,448},{64,0},{128,64},{192,128},{256,192},{320,256},{384,320},{4... | collective-permute-start | bytes 983048 | tf_op jit(solution)/shard_map/ppermute | solution.py:113
  50.8 0.0 collective-permute-done.refs_1_
  50.8 1.9 %collective-permute-start.1 = (bf16[5,256,128]{2,1,0:T(8,128)(2,1)S(1)}, bf16[5,256,128]{2,1,0:T(8,128)(2,1)S(1)}, u32[]{:S(2)}, u32[]{:S(2)}) collective-permute-start(bf16[5,256,128]{2,1,0:T(8,128)(2,1)S(1)} %collective-permute-done.refs_1_), channel_id=1, source_target_pairs={{0,64},{64,128},{128,192},{192,256},{256,320},{320,384},{384,448},... | collective-permute-start | bytes 983048 | tf_op jit(solution)/shard_map/ppermute | solution.py:111
  52.8 2.3 %collective-permute-done.5.refs_6_ = bf16[5,256,128]{2,1,0:T(8,128)(2,1)S(1)} collective-permute-done((bf16[5,256,128]{2,1,0:T(8,128)(2,1)S(1)}, bf16[5,256,128]{2,1,0:T(8,128)(2,1)S(1)}, u32[]{:S(2)}, u32[]{:S(2)}) %collective-permute-start.5) | collective-permute-done | bytes 327712 | tf_op jit(solution)/shard_map/ppermute | solution.py:113
  55.1 5.3 %collective-permute-start.6 = (bf16[5,256,128]{2,1,0:T(8,128)(2,1)S(1)}, bf16[5,256,128]{2,1,0:T(8,128)(2,1)S(1)}, u32[]{:S(2)}, u32[]{:S(2)}) collective-permute-start(bf16[5,256,128]{2,1,0:T(8,128)(2,1)S(1)} %collective-permute-done.5.refs_6_), channel_id=1, source_target_pairs={{0,448},{64,0},{128,64},{192,128},{256,192},{320,256},{384,320},{4... | collective-permute-start | bytes 983048 | tf_op jit(solution)/shard_map/ppermute | solution.py:113
  60.4 0.0 collective-permute-done.1.refs_2_
  60.4 1.9 %collective-permute-start.2 = (bf16[5,256,128]{2,1,0:T(8,128)(2,1)S(1)}, bf16[5,256,128]{2,1,0:T(8,128)(2,1)S(1)}, u32[]{:S(2)}, u32[]{:S(2)}) collective-permute-start(bf16[5,256,128]{2,1,0:T(8,128)(2,1)S(1)} %collective-permute-done.1.refs_2_), channel_id=1, source_target_pairs={{0,64},{64,128},{128,192},{192,256},{256,320},{320,384},{384,448},... | collective-permute-start | bytes 983048 | tf_op jit(solution)/shard_map/ppermute | solution.py:111
  62.3 0.1 pad_maximum_fusion
  62.5 5.8 %collective-permute-start.7 = (bf16[15,256,128]{2,1,0:T(8,128)(2,1)S(1)}, bf16[15,256,128]{2,1,0:T(8,128)(2,1)S(1)}, u32[]{:S(2)}, u32[]{:S(2)}) collective-permute-start(bf16[15,256,128]{2,1,0:T(8,128)(2,1)S(1)} %pad_maximum_fusion), channel_id=1, source_target_pairs={{0,32},{32,0},{1,33},{33,1},{2,34},{34,2},{3,35},{35,3},{4,36},{36... | collective-permute-start | bytes 2949128 | tf_op jit(solution)/shard_map/ppermute | solution.py:117
  68.3 0.1 pad_maximum_fusion.1
  68.4 1.9 %collective-permute-start.8 = (bf16[10,256,128]{2,1,0:T(8,128)(2,1)S(1)}, bf16[10,256,128]{2,1,0:T(8,128)(2,1)S(1)}, u32[]{:S(2)}, u32[]{:S(2)}) collective-permute-start(bf16[10,256,128]{2,1,0:T(8,128)(2,1)S(1)} %pad_maximum_fusion.1), channel_id=1, source_target_pairs={{0,32},{32,0},{1,33},{33,1},{2,34},{34,2},{3,35},{35,3},{4,36},{36... | collective-permute-start | bytes 1966088 | tf_op jit(solution)/shard_map/ppermute | solution.py:117
  70.3 0.0 collective-permute-done.2.refs_3_
  70.3 1.9 %collective-permute-start.3 = (bf16[5,256,128]{2,1,0:T(8,128)(2,1)S(1)}, bf16[5,256,128]{2,1,0:T(8,128)(2,1)S(1)}, u32[]{:S(2)}, u32[]{:S(2)}) collective-permute-start(bf16[5,256,128]{2,1,0:T(8,128)(2,1)S(1)} %collective-permute-done.2.refs_3_), channel_id=1, source_target_pairs={{0,64},{64,128},{128,192},{192,256},{256,320},{320,384},{384,448},... | collective-permute-start | bytes 983048 | tf_op jit(solution)/shard_map/ppermute | solution.py:111
  72.2 0.0 collective-permute-done.6.refs_5_
  72.2 0.1 pad_maximum_fusion.2
  72.3 6.1 %collective-permute-start.9 = (bf16[10,256,128]{2,1,0:T(8,128)(2,1)S(1)}, bf16[10,256,128]{2,1,0:T(8,128)(2,1)S(1)}, u32[]{:S(2)}, u32[]{:S(2)}) collective-permute-start(bf16[10,256,128]{2,1,0:T(8,128)(2,1)S(1)} %pad_maximum_fusion.2), channel_id=1, source_target_pairs={{0,32},{32,0},{1,33},{33,1},{2,34},{34,2},{3,35},{35,3},{4,36},{36... | collective-permute-start | bytes 1966088 | tf_op jit(solution)/shard_map/ppermute | solution.py:117
  78.4 1.5 %collective-permute-done.3.refs_4_ = bf16[5,256,128]{2,1,0:T(8,128)(2,1)S(1)} collective-permute-done((bf16[5,256,128]{2,1,0:T(8,128)(2,1)S(1)}, bf16[5,256,128]{2,1,0:T(8,128)(2,1)S(1)}, u32[]{:S(2)}, u32[]{:S(2)}) %collective-permute-start.3) | collective-permute-done | bytes 327712 | tf_op jit(solution)/shard_map/ppermute | solution.py:111
  79.9 6.7 %collective-permute-start.10 = (bf16[5,256,128]{2,1,0:T(8,128)(2,1)S(1)}, bf16[5,256,128]{2,1,0:T(8,128)(2,1)S(1)}, u32[]{:S(2)}, u32[]{:S(2)}) collective-permute-start(bf16[5,256,128]{2,1,0:T(8,128)(2,1)S(1)} %collective-permute-done.3.refs_4_), channel_id=1, source_target_pairs={{0,32},{32,0},{1,33},{33,1},{2,34},{34,2},{3,35},{35,3},{4,36},{36... | collective-permute-start | bytes 983048 | tf_op jit(solution)/shard_map/ppermute | solution.py:117
  86.6 0.0 collective-permute-done.8.refs_9_
  86.6 0.0 collective-permute-done.7.refs_8_
  86.6 1.2 %collective-permute-done.10.refs_11_ = bf16[5,256,128]{2,1,0:T(8,128)(2,1)S(1)} collective-permute-done((bf16[5,256,128]{2,1,0:T(8,128)(2,1)S(1)}, bf16[5,256,128]{2,1,0:T(8,128)(2,1)S(1)}, u32[]{:S(2)}, u32[]{:S(2)}) %collective-permute-start.10) | collective-permute-done | bytes 327712 | tf_op jit(solution)/shard_map/ppermute | solution.py:117
  87.8 0.0 collective-permute-done.9.refs_10_
  87.8 0.4 shard_map.37.factor
  88.2 0.0 copy-start
  88.2 2.3 %copy-done = bf16[40,512,128]{2,1,0:T(8,128)(2,1)} copy-done((bf16[40,512,128]{2,1,0:T(8,128)(2,1)}, bf16[40,512,128]{2,1,0:T(8,128)(2,1)S(1)}, u32[]{:S(2)}) %copy-start) | copy-done | bytes 5242904
  90.5 0.0 all-to-all-done.1
  90.5 6.4 %shard_map.38 = bf16[2048,512]{1,0:T(8,128)(2,1)} custom-call(bf16[40,512,128]{2,1,0:T(8,128)(2,1)} %copy-done, bf16[2048,512]{1,0:T(8,128)(2,1)S(1)} %bitcast.14), custom_call_target="tpu_custom_call" | custom-call | flops 2684354560 | bytes 9437184 | tf_op jit(solution)/shard_map/pallas_call | solution.py:128
  (3 shorter events, 0.0 us)
Async XLA Ops:
  1.7 20.7 %all-to-all-start = ((bf16[32,5,8,128]{3,2,1,0:T(8,128)(2,1)}), bf16[32,5,8,128]{3,2,1,0:T(8,128)(2,1)S(1)}, u32[]{:S(2)}, u32[]{:S(2)}) async-start(bf16[32,5,8,128]{3,2,1,0:T(8,128)(2,1)} %broadcast_in_dim.2), calls=%async_computation | async-start | bytes 655360 | tf_op jit(solution)/shard_map/all_to_all | solution.py:103
  22.3 68.1 %all-to-all-start.1 = ((bf16[32,64,512]{2,1,0:T(8,128)(2,1)}), bf16[32,64,512]{2,1,0:T(8,128)(2,1)S(1)}, u32[]{:S(2)}, u32[]{:S(2)}) async-start(bf16[32,64,512]{2,1,0:T(8,128)(2,1)} %bitcast.15), calls=%async_computation.1 | async-start | bytes 4194304 | tf_op jit(solution)/shard_map/all_to_all | solution.py:107
  29.6 15.9 %collective-permute-start.4 = (bf16[5,256,128]{2,1,0:T(8,128)(2,1)S(1)}, bf16[5,256,128]{2,1,0:T(8,128)(2,1)S(1)}, u32[]{:S(2)}, u32[]{:S(2)}) collective-permute-start(bf16[5,256,128]{2,1,0:T(8,128)(2,1)S(1)} %copy_bitcast_fusion.refs_0_), channel_id=1, source_target_pairs={{0,448},{64,0},{128,64},{192,128},{256,192},{320,256},{384,320},{4... | collective-permute-start | bytes 983048 | tf_op jit(solution)/shard_map/ppermute | solution.py:113
  40.3 10.5 %collective-permute-start = (bf16[5,256,128]{2,1,0:T(8,128)(2,1)S(1)}, bf16[5,256,128]{2,1,0:T(8,128)(2,1)S(1)}, u32[]{:S(2)}, u32[]{:S(2)}) collective-permute-start(bf16[5,256,128]{2,1,0:T(8,128)(2,1)S(1)} %copy_bitcast_fusion.refs_0_), channel_id=1, source_target_pairs={{0,64},{64,128},{128,192},{192,256},{256,320},{320,384},{384,448},... | collective-permute-start | bytes 983048 | tf_op jit(solution)/shard_map/ppermute | solution.py:111
  45.5 9.6 %collective-permute-start.5 = (bf16[5,256,128]{2,1,0:T(8,128)(2,1)S(1)}, bf16[5,256,128]{2,1,0:T(8,128)(2,1)S(1)}, u32[]{:S(2)}, u32[]{:S(2)}) collective-permute-start(bf16[5,256,128]{2,1,0:T(8,128)(2,1)S(1)} %collective-permute-done.4.refs_7_), channel_id=1, source_target_pairs={{0,448},{64,0},{128,64},{192,128},{256,192},{320,256},{384,320},{4... | collective-permute-start | bytes 983048 | tf_op jit(solution)/shard_map/ppermute | solution.py:113
  50.8 9.6 %collective-permute-start.1 = (bf16[5,256,128]{2,1,0:T(8,128)(2,1)S(1)}, bf16[5,256,128]{2,1,0:T(8,128)(2,1)S(1)}, u32[]{:S(2)}, u32[]{:S(2)}) collective-permute-start(bf16[5,256,128]{2,1,0:T(8,128)(2,1)S(1)} %collective-permute-done.refs_1_), channel_id=1, source_target_pairs={{0,64},{64,128},{128,192},{192,256},{256,320},{320,384},{384,448},... | collective-permute-start | bytes 983048 | tf_op jit(solution)/shard_map/ppermute | solution.py:111
  55.1 17.1 %collective-permute-start.6 = (bf16[5,256,128]{2,1,0:T(8,128)(2,1)S(1)}, bf16[5,256,128]{2,1,0:T(8,128)(2,1)S(1)}, u32[]{:S(2)}, u32[]{:S(2)}) collective-permute-start(bf16[5,256,128]{2,1,0:T(8,128)(2,1)S(1)} %collective-permute-done.5.refs_6_), channel_id=1, source_target_pairs={{0,448},{64,0},{128,64},{192,128},{256,192},{320,256},{384,320},{4... | collective-permute-start | bytes 983048 | tf_op jit(solution)/shard_map/ppermute | solution.py:113
  60.4 9.9 %collective-permute-start.2 = (bf16[5,256,128]{2,1,0:T(8,128)(2,1)S(1)}, bf16[5,256,128]{2,1,0:T(8,128)(2,1)S(1)}, u32[]{:S(2)}, u32[]{:S(2)}) collective-permute-start(bf16[5,256,128]{2,1,0:T(8,128)(2,1)S(1)} %collective-permute-done.1.refs_2_), channel_id=1, source_target_pairs={{0,64},{64,128},{128,192},{192,256},{256,320},{320,384},{384,448},... | collective-permute-start | bytes 983048 | tf_op jit(solution)/shard_map/ppermute | solution.py:111
  62.5 24.1 %collective-permute-start.7 = (bf16[15,256,128]{2,1,0:T(8,128)(2,1)S(1)}, bf16[15,256,128]{2,1,0:T(8,128)(2,1)S(1)}, u32[]{:S(2)}, u32[]{:S(2)}) collective-permute-start(bf16[15,256,128]{2,1,0:T(8,128)(2,1)S(1)} %pad_maximum_fusion), channel_id=1, source_target_pairs={{0,32},{32,0},{1,33},{33,1},{2,34},{34,2},{3,35},{35,3},{4,36},{36... | collective-permute-start | bytes 2949128 | tf_op jit(solution)/shard_map/ppermute | solution.py:117
  68.4 18.2 %collective-permute-start.8 = (bf16[10,256,128]{2,1,0:T(8,128)(2,1)S(1)}, bf16[10,256,128]{2,1,0:T(8,128)(2,1)S(1)}, u32[]{:S(2)}, u32[]{:S(2)}) collective-permute-start(bf16[10,256,128]{2,1,0:T(8,128)(2,1)S(1)} %pad_maximum_fusion.1), channel_id=1, source_target_pairs={{0,32},{32,0},{1,33},{33,1},{2,34},{34,2},{3,35},{35,3},{4,36},{36... | collective-permute-start | bytes 1966088 | tf_op jit(solution)/shard_map/ppermute | solution.py:117
  70.3 9.6 %collective-permute-start.3 = (bf16[5,256,128]{2,1,0:T(8,128)(2,1)S(1)}, bf16[5,256,128]{2,1,0:T(8,128)(2,1)S(1)}, u32[]{:S(2)}, u32[]{:S(2)}) collective-permute-start(bf16[5,256,128]{2,1,0:T(8,128)(2,1)S(1)} %collective-permute-done.2.refs_3_), channel_id=1, source_target_pairs={{0,64},{64,128},{128,192},{192,256},{256,320},{320,384},{384,448},... | collective-permute-start | bytes 983048 | tf_op jit(solution)/shard_map/ppermute | solution.py:111
  72.3 15.5 %collective-permute-start.9 = (bf16[10,256,128]{2,1,0:T(8,128)(2,1)S(1)}, bf16[10,256,128]{2,1,0:T(8,128)(2,1)S(1)}, u32[]{:S(2)}, u32[]{:S(2)}) collective-permute-start(bf16[10,256,128]{2,1,0:T(8,128)(2,1)S(1)} %pad_maximum_fusion.2), channel_id=1, source_target_pairs={{0,32},{32,0},{1,33},{33,1},{2,34},{34,2},{3,35},{35,3},{4,36},{36... | collective-permute-start | bytes 1966088 | tf_op jit(solution)/shard_map/ppermute | solution.py:117
  79.9 7.9 %collective-permute-start.10 = (bf16[5,256,128]{2,1,0:T(8,128)(2,1)S(1)}, bf16[5,256,128]{2,1,0:T(8,128)(2,1)S(1)}, u32[]{:S(2)}, u32[]{:S(2)}) collective-permute-start(bf16[5,256,128]{2,1,0:T(8,128)(2,1)S(1)} %collective-permute-done.3.refs_4_), channel_id=1, source_target_pairs={{0,32},{32,0},{1,33},{33,1},{2,34},{34,2},{3,35},{35,3},{4,36},{36... | collective-permute-start | bytes 983048 | tf_op jit(solution)/shard_map/ppermute | solution.py:117
  88.2 2.3 %copy-start = (bf16[40,512,128]{2,1,0:T(8,128)(2,1)}, bf16[40,512,128]{2,1,0:T(8,128)(2,1)S(1)}, u32[]{:S(2)}) copy-start(bf16[40,512,128]{2,1,0:T(8,128)(2,1)S(1)} %shard_map.37.factor) | copy-start | bytes 15728644

commit v5 on v4

--- a/solution.py
+++ b/solution.py
@@ -10,24 +10,29 @@
 AHEAD = 3
 SPLIT = 1
 UNITS = 5
-GROUPS = ((0, 1, 7), (2, 6), (3, 5), (4,))
 ANY = pl.BlockSpec(memory_space=pl.ANY)
 VMEM = pl.BlockSpec(memory_space=pltpu.VMEM)
 
 
 def assemble(*refs):
-    own, swapped, factor = refs[:NZ], refs[NZ:-1], refs[-1]
+    mine, theirs, swapped, factor = refs[:5], refs[5:9], refs[9:13], refs[13]
     z, core = lax.axis_index("z"), lax.axis_index("core")
-    other = {}
-    for group, ref in zip(GROUPS, swapped):
-        for at, d in enumerate(group):
-            other[d] = (ref, at * UNITS)
-    for d in range(NZ):
-        unit = lax.rem(z + NZ - d, NZ) * UNITS
-        for (ref, at), half in (((own[d], 0), core), (other[d], 1 - core)):
-            row = pl.multiple_of(half * 256, 256)
-            for i in range(UNITS):
-                factor[unit + i, pl.ds(row, 256), :] = ref[at + i]
+    along = 1 - 2 * core
+    places = []
+    for d in range(5):
+        near, far = z - along * d, z + along * d
+        places.append((mine[d], 0, near, core))
+        if d < 4:
+            places.append((theirs[d], 0, near, 1 - core))
+        if d > 0:
+            places.append((swapped[d - 1], 0, far, 1 - core))
+        if 0 < d < 4:
+            places.append((swapped[d - 1], UNITS, far, core))
+    for ref, at, source, half in places:
+        unit = lax.rem(source + NZ, NZ) * UNITS
+        row = pl.multiple_of(half * 256, 256)
+        for i in range(UNITS):
+            factor[unit + i, pl.ds(row, 256), :] = ref[at + i]
 
 
 def product(panels, block, solved):
@@ -106,24 +111,32 @@
     sections, piece = lax.optimization_barrier((sections, piece))
     columns = lax.all_to_all(sections, ("x", "y"), 0, 0, tiled=True)
 
-    own = {0: piece.transpose(1, 0, 2, 3).reshape(UNITS, NAUX * 8, 128)}
+    def swap(value):
+        return lax.ppermute(value, "core", ring(2, 1))
+
+    def pass_on(value):
+        up = [(2 * z, 2 * ((z + 1) % NZ)) for z in range(NZ)]
+        down = [(2 * z + 1, 2 * ((z - 1) % NZ) + 1) for z in range(NZ)]
+        return lax.ppermute(value, ("z", "core"), up + down)
+
+    mine = [piece.transpose(1, 0, 2, 3).reshape(UNITS, NAUX * 8, 128)]
+    theirs = [swap(mine[0])]
+    swapped = []
     for d in range(1, 5):
-        own[d] = lax.ppermute(own[d - 1], "z", ring(NZ, 1))
+        mine.append(pass_on(mine[-1]))
         if d < 4:
-            own[-d % NZ] = lax.ppermute(own[(1 - d) % NZ], "z", ring(NZ, -1))
-    swapped = []
-    for group in GROUPS:
-        held = jnp.concatenate([own[d] for d in group], axis=0)
-        swapped.append(lax.ppermute(held, "core", ring(2, 1)))
+            theirs.append(pass_on(theirs[-1]))
+            swapped.append(swap(jnp.concatenate([mine[d], theirs[d]], axis=0)))
+    swapped.append(swap(mine[4]))
 
     factor = pl.pallas_call(
         assemble,
         out_shape=jax.ShapeDtypeStruct((40, 512, 128), bf16),
-        in_specs=[VMEM] * (NZ + len(GROUPS)),
+        in_specs=[VMEM] * 13,
         out_specs=VMEM,
         compiler_params=pltpu.CompilerParams(vmem_limit_bytes=16 << 20),
         cost_estimate=cost(0, 10 << 20),
-    )(*[own[d] for d in range(NZ)], *swapped)
+    )(*mine, *theirs, *swapped)
 
     return pl.pallas_call(
         solve,

time: 97.6 us -> 93.8 us (0.961)
  starting transfers between devices: 67.2 us -> 65.3 us
  waiting for transfers between devices: 15.3 us -> 13.5 us
    ppermute x11 -> x12, starting transfers between devices: 49.5 us -> 47.5 us  [the longest x7 33.6 us: pass_on(): return lax.ppermute(value, ('z', 'core'), up + down)]
    ppermute x11 -> x12, waiting for transfers between devices: 8.29 us -> 6.48 us  [the longest x7 5.25 us: pass_on(): return lax.ppermute(value, ('z', 'core'), up + down)]
  transfers between devices with their start and end apart: 13 -> 14, of which waited for: 5 -> 5; matrix products, arithmetic and copies ran while one was open for 4% -> 4% of each run, Pallas kernels for 0% -> 0%
where the time goes in v5:
time: 93.8 us; the launch traced here: 93.1 us
  starting transfers between devices  65.3 us (70%)
  waiting for transfers between devices  13.5 us (14%)
  Pallas kernels  6.79 us (7%)
  local copies, waits for them, and re-layouts  6.33 us (7%)
  other arithmetic  1.02 us (1%)
    ppermute x7, starting transfers between devices, pass_on(): return lax.ppermute(value, ('z', 'core'), up + down)  33.6 us
    ppermute x5, starting transfers between devices, swap(): return lax.ppermute(value, 'core', ring(2, 1))  13.9 us
    all_to_all x1, starting transfers between devices, local(): piece = lax.all_to_all(piece, ('x', 'y'), 0, 0, tiled=True)  10.5 us
    all_to_all x1, starting transfers between devices, local(): columns = lax.all_to_all(sections, ('x', 'y'), 0, 0, tiled=True)  7.23 us
    all_to_all x1, waiting for transfers between devices, local(): piece = lax.all_to_all(piece, ('x', 'y'), 0, 0, tiled=True)  6.99 us
    pallas_call x1, Pallas kernels, local(): pl.pallas_call(solve, out_shape=jax.ShapeDtypeStruct((4 * 512, width), bf...  6.42 us
    ppermute x7, waiting for transfers between devices, pass_on(): return lax.ppermute(value, ('z', 'core'), up + down)  5.25 us
    reshape x1, local copies, waits for them, and re-layouts, local(): sections = integrals.reshape(rows, NAUX, width).transpose(1, 0, 2)  3.19 us
  transfers between devices with their start and end apart: 14, of which 5 were waited for; matrix products, arithmetic and copies ran while one was open for 4% of the time, Pallas kernels for 0%

profile of v5, /device:TPU:1, one launch (start us, length us, event | category | flops | bytes accessed | tf_op | source)
XLA Modules:
  0.0 93.1 jit_solution(3658010428512499248)
XLA Ops:
  0.0 0.8 fusion
  0.9 0.8 broadcast_in_dim.2
  1.6 10.5 %all-to-all-start = ((bf16[32,5,8,128]{3,2,1,0:T(8,128)(2,1)}), bf16[32,5,8,128]{3,2,1,0:T(8,128)(2,1)S(1)}, u32[]{:S(2)}, u32[]{:S(2)}) async-start(bf16[32,5,8,128]{3,2,1,0:T(8,128)(2,1)} %broadcast_in_dim.2), calls=%async_computation | async-start | bytes 655360 | tf_op jit(solution)/shard_map/all_to_all | solution.py:108
  12.2 3.2 %copy.10 = bf16[8,32,8,512]{3,2,0,1:T(8,128)(2,1)} copy(bf16[8,32,8,512]{3,2,1,0:T(8,128)(2,1)} %bitcast.16) | data formatting | bytes 4194304 | tf_op jit(solution)/shard_map/reshape | solution.py:110
  15.3 7.0 %all-to-all-done = bf16[32,5,8,128]{3,2,1,0:T(8,128)(2,1)S(1)} async-done(((bf16[32,5,8,128]{3,2,1,0:T(8,128)(2,1)}), bf16[32,5,8,128]{3,2,1,0:T(8,128)(2,1)S(1)}, u32[]{:S(2)}, u32[]{:S(2)}) %all-to-all-start) | async-done | bytes 327712 | tf_op jit(solution)/shard_map/all_to_all | solution.py:108
  22.3 7.2 %all-to-all-start.1 = ((bf16[32,64,512]{2,1,0:T(8,128)(2,1)}), bf16[32,64,512]{2,1,0:T(8,128)(2,1)S(1)}, u32[]{:S(2)}, u32[]{:S(2)}) async-start(bf16[32,64,512]{2,1,0:T(8,128)(2,1)} %bitcast.15), calls=%async_computation.1 | async-start | bytes 4194304 | tf_op jit(solution)/shard_map/all_to_all | solution.py:112
  29.6 0.1 copy_bitcast_fusion.refs_0_
  29.6 3.7 %collective-permute-start.4 = (bf16[5,256,128]{2,1,0:T(8,128)(2,1)S(1)}, bf16[5,256,128]{2,1,0:T(8,128)(2,1)S(1)}, u32[]{:S(2)}, u32[]{:S(2)}) collective-permute-start(bf16[5,256,128]{2,1,0:T(8,128)(2,1)S(1)} %copy_bitcast_fusion.refs_0_), channel_id=1, source_target_pairs={{0,32},{32,0},{1,33},{33,1},{2,34},{34,2},{3,35},{35,3},{4,36},{36... | collective-permute-start | bytes 983048 | tf_op jit(solution)/shard_map/ppermute | solution.py:115
  33.4 10.7 %collective-permute-start = (bf16[5,256,128]{2,1,0:T(8,128)(2,1)S(1)}, bf16[5,256,128]{2,1,0:T(8,128)(2,1)S(1)}, u32[]{:S(2)}, u32[]{:S(2)}) collective-permute-start(bf16[5,256,128]{2,1,0:T(8,128)(2,1)S(1)} %copy_bitcast_fusion.refs_0_), channel_id=1, source_target_pairs={{0,64},{64,128},{128,192},{192,256},{256,320},{320,384},{384,448},... | collective-permute-start | bytes 983048 | tf_op jit(solution)/shard_map/ppermute | solution.py:120
  44.0 0.0 collective-permute-done.4.refs_5_
  44.0 2.2 %collective-permute-start.5 = (bf16[5,256,128]{2,1,0:T(8,128)(2,1)S(1)}, bf16[5,256,128]{2,1,0:T(8,128)(2,1)S(1)}, u32[]{:S(2)}, u32[]{:S(2)}) collective-permute-start(bf16[5,256,128]{2,1,0:T(8,128)(2,1)S(1)} %collective-permute-done.4.refs_5_), channel_id=1, source_target_pairs={{0,64},{64,128},{128,192},{192,256},{256,320},{320,384},{384,448},... | collective-permute-start | bytes 983048 | tf_op jit(solution)/shard_map/ppermute | solution.py:120
  46.2 1.8 %collective-permute-done.refs_1_ = bf16[5,256,128]{2,1,0:T(8,128)(2,1)S(1)} collective-permute-done((bf16[5,256,128]{2,1,0:T(8,128)(2,1)S(1)}, bf16[5,256,128]{2,1,0:T(8,128)(2,1)S(1)}, u32[]{:S(2)}, u32[]{:S(2)}) %collective-permute-start) | collective-permute-done | bytes 327712 | tf_op jit(solution)/shard_map/ppermute | solution.py:120
  48.0 5.3 %collective-permute-start.1 = (bf16[5,256,128]{2,1,0:T(8,128)(2,1)S(1)}, bf16[5,256,128]{2,1,0:T(8,128)(2,1)S(1)}, u32[]{:S(2)}, u32[]{:S(2)}) collective-permute-start(bf16[5,256,128]{2,1,0:T(8,128)(2,1)S(1)} %collective-permute-done.refs_1_), channel_id=1, source_target_pairs={{0,64},{64,128},{128,192},{192,256},{256,320},{320,384},{384,448},... | collective-permute-start | bytes 983048 | tf_op jit(solution)/shard_map/ppermute | solution.py:120
  53.3 0.0 collective-permute-done.5.refs_6_
  53.4 3.5 %collective-permute-start.6 = (bf16[5,256,128]{2,1,0:T(8,128)(2,1)S(1)}, bf16[5,256,128]{2,1,0:T(8,128)(2,1)S(1)}, u32[]{:S(2)}, u32[]{:S(2)}) collective-permute-start(bf16[5,256,128]{2,1,0:T(8,128)(2,1)S(1)} %collective-permute-done.5.refs_6_), channel_id=1, source_target_pairs={{0,64},{64,128},{128,192},{192,256},{256,320},{320,384},{384,448},... | collective-permute-start | bytes 983048 | tf_op jit(solution)/shard_map/ppermute | solution.py:120
  56.9 0.5 collective-permute-done.1.refs_2_
  57.3 5.3 %collective-permute-start.2 = (bf16[5,256,128]{2,1,0:T(8,128)(2,1)S(1)}, bf16[5,256,128]{2,1,0:T(8,128)(2,1)S(1)}, u32[]{:S(2)}, u32[]{:S(2)}) collective-permute-start(bf16[5,256,128]{2,1,0:T(8,128)(2,1)S(1)} %collective-permute-done.1.refs_2_), channel_id=1, source_target_pairs={{0,64},{64,128},{128,192},{192,256},{256,320},{320,384},{384,448},... | collective-permute-start | bytes 983048 | tf_op jit(solution)/shard_map/ppermute | solution.py:120
  62.7 0.0 collective-permute-done.6.refs_7_
  62.7 3.5 %collective-permute-start.7 = (bf16[5,256,128]{2,1,0:T(8,128)(2,1)S(1)}, bf16[5,256,128]{2,1,0:T(8,128)(2,1)S(1)}, u32[]{:S(2)}, u32[]{:S(2)}) collective-permute-start(bf16[5,256,128]{2,1,0:T(8,128)(2,1)S(1)} %collective-permute-done.6.refs_7_), channel_id=1, source_target_pairs={{0,64},{64,128},{128,192},{192,256},{256,320},{320,384},{384,448},... | collective-permute-start | bytes 983048 | tf_op jit(solution)/shard_map/ppermute | solution.py:120
  66.2 0.1 pad_maximum_fusion
  66.2 1.9 %collective-permute-start.8 = (bf16[10,256,128]{2,1,0:T(8,128)(2,1)S(1)}, bf16[10,256,128]{2,1,0:T(8,128)(2,1)S(1)}, u32[]{:S(2)}, u32[]{:S(2)}) collective-permute-start(bf16[10,256,128]{2,1,0:T(8,128)(2,1)S(1)} %pad_maximum_fusion), channel_id=1, source_target_pairs={{0,32},{32,0},{1,33},{33,1},{2,34},{34,2},{3,35},{35,3},{4,36},{36... | collective-permute-start | bytes 1966088 | tf_op jit(solution)/shard_map/ppermute | solution.py:115
  68.2 0.1 pad_maximum_fusion.1
  68.2 2.4 %collective-permute-start.9 = (bf16[10,256,128]{2,1,0:T(8,128)(2,1)S(1)}, bf16[10,256,128]{2,1,0:T(8,128)(2,1)S(1)}, u32[]{:S(2)}, u32[]{:S(2)}) collective-permute-start(bf16[10,256,128]{2,1,0:T(8,128)(2,1)S(1)} %pad_maximum_fusion.1), channel_id=1, source_target_pairs={{0,32},{32,0},{1,33},{33,1},{2,34},{34,2},{3,35},{35,3},{4,36},{36... | collective-permute-start | bytes 1966088 | tf_op jit(solution)/shard_map/ppermute | solution.py:115
  70.6 0.0 collective-permute-done.2.refs_3_
  70.7 3.1 %collective-permute-start.3 = (bf16[5,256,128]{2,1,0:T(8,128)(2,1)S(1)}, bf16[5,256,128]{2,1,0:T(8,128)(2,1)S(1)}, u32[]{:S(2)}, u32[]{:S(2)}) collective-permute-start(bf16[5,256,128]{2,1,0:T(8,128)(2,1)S(1)} %collective-permute-done.2.refs_3_), channel_id=1, source_target_pairs={{0,64},{64,128},{128,192},{192,256},{256,320},{320,384},{384,448},... | collective-permute-start | bytes 983048 | tf_op jit(solution)/shard_map/ppermute | solution.py:120
  73.8 0.0 collective-permute-done.7.refs_8_
  73.8 0.1 pad_maximum_fusion.2
  73.9 1.9 %collective-permute-start.10 = (bf16[10,256,128]{2,1,0:T(8,128)(2,1)S(1)}, bf16[10,256,128]{2,1,0:T(8,128)(2,1)S(1)}, u32[]{:S(2)}, u32[]{:S(2)}) collective-permute-start(bf16[10,256,128]{2,1,0:T(8,128)(2,1)S(1)} %pad_maximum_fusion.2), channel_id=1, source_target_pairs={{0,32},{32,0},{1,33},{33,1},{2,34},{34,2},{3,35},{35,3},{4,36},{36... | collective-permute-start | bytes 1966088 | tf_op jit(solution)/shard_map/ppermute | solution.py:115
  75.8 3.0 %collective-permute-done.3.refs_4_ = bf16[5,256,128]{2,1,0:T(8,128)(2,1)S(1)} collective-permute-done((bf16[5,256,128]{2,1,0:T(8,128)(2,1)S(1)}, bf16[5,256,128]{2,1,0:T(8,128)(2,1)S(1)}, u32[]{:S(2)}, u32[]{:S(2)}) %collective-permute-start.3) | collective-permute-done | bytes 327712 | tf_op jit(solution)/shard_map/ppermute | solution.py:120
  78.8 4.0 %collective-permute-start.11 = (bf16[5,256,128]{2,1,0:T(8,128)(2,1)S(1)}, bf16[5,256,128]{2,1,0:T(8,128)(2,1)S(1)}, u32[]{:S(2)}, u32[]{:S(2)}) collective-permute-start(bf16[5,256,128]{2,1,0:T(8,128)(2,1)S(1)} %collective-permute-done.3.refs_4_), channel_id=1, source_target_pairs={{0,32},{32,0},{1,33},{33,1},{2,34},{34,2},{3,35},{35,3},{4,36},{36... | collective-permute-start | bytes 983048 | tf_op jit(solution)/shard_map/ppermute | solution.py:115
  82.8 0.0 collective-permute-done.8.refs_9_
  82.8 1.2 %collective-permute-done.11.refs_12_ = bf16[5,256,128]{2,1,0:T(8,128)(2,1)S(1)} collective-permute-done((bf16[5,256,128]{2,1,0:T(8,128)(2,1)S(1)}, bf16[5,256,128]{2,1,0:T(8,128)(2,1)S(1)}, u32[]{:S(2)}, u32[]{:S(2)}) %collective-permute-start.11) | collective-permute-done | bytes 327712 | tf_op jit(solution)/shard_map/ppermute | solution.py:115
  84.0 0.0 collective-permute-done.9.refs_10_
  84.0 0.0 collective-permute-done.10.refs_11_
  84.0 0.4 shard_map.37.factor
  84.4 0.0 copy-start
  84.4 2.3 %copy-done = bf16[40,512,128]{2,1,0:T(8,128)(2,1)} copy-done((bf16[40,512,128]{2,1,0:T(8,128)(2,1)}, bf16[40,512,128]{2,1,0:T(8,128)(2,1)S(1)}, u32[]{:S(2)}) %copy-start) | copy-done | bytes 5242904
  86.7 0.0 all-to-all-done.1
  86.7 6.4 %shard_map.38 = bf16[2048,512]{1,0:T(8,128)(2,1)} custom-call(bf16[40,512,128]{2,1,0:T(8,128)(2,1)} %copy-done, bf16[2048,512]{1,0:T(8,128)(2,1)S(1)} %bitcast.14), custom_call_target="tpu_custom_call" | custom-call | flops 2684354560 | bytes 9437184 | tf_op jit(solution)/shard_map/pallas_call | solution.py:141
  (3 shorter events, 0.0 us)
Async XLA Ops:
  1.6 20.7 %all-to-all-start = ((bf16[32,5,8,128]{3,2,1,0:T(8,128)(2,1)}), bf16[32,5,8,128]{3,2,1,0:T(8,128)(2,1)S(1)}, u32[]{:S(2)}, u32[]{:S(2)}) async-start(bf16[32,5,8,128]{3,2,1,0:T(8,128)(2,1)} %broadcast_in_dim.2), calls=%async_computation | async-start | bytes 655360 | tf_op jit(solution)/shard_map/all_to_all | solution.py:108
  22.3 64.3 %all-to-all-start.1 = ((bf16[32,64,512]{2,1,0:T(8,128)(2,1)}), bf16[32,64,512]{2,1,0:T(8,128)(2,1)S(1)}, u32[]{:S(2)}, u32[]{:S(2)}) async-start(bf16[32,64,512]{2,1,0:T(8,128)(2,1)} %bitcast.15), calls=%async_computation.1 | async-start | bytes 4194304 | tf_op jit(solution)/shard_map/all_to_all | solution.py:112
  29.6 14.4 %collective-permute-start.4 = (bf16[5,256,128]{2,1,0:T(8,128)(2,1)S(1)}, bf16[5,256,128]{2,1,0:T(8,128)(2,1)S(1)}, u32[]{:S(2)}, u32[]{:S(2)}) collective-permute-start(bf16[5,256,128]{2,1,0:T(8,128)(2,1)S(1)} %copy_bitcast_fusion.refs_0_), channel_id=1, source_target_pairs={{0,32},{32,0},{1,33},{33,1},{2,34},{34,2},{3,35},{35,3},{4,36},{36... | collective-permute-start | bytes 983048 | tf_op jit(solution)/shard_map/ppermute | solution.py:115
  33.4 14.7 %collective-permute-start = (bf16[5,256,128]{2,1,0:T(8,128)(2,1)S(1)}, bf16[5,256,128]{2,1,0:T(8,128)(2,1)S(1)}, u32[]{:S(2)}, u32[]{:S(2)}) collective-permute-start(bf16[5,256,128]{2,1,0:T(8,128)(2,1)S(1)} %copy_bitcast_fusion.refs_0_), channel_id=1, source_target_pairs={{0,64},{64,128},{128,192},{192,256},{256,320},{320,384},{384,448},... | collective-permute-start | bytes 983048 | tf_op jit(solution)/shard_map/ppermute | solution.py:120
  44.0 9.3 %collective-permute-start.5 = (bf16[5,256,128]{2,1,0:T(8,128)(2,1)S(1)}, bf16[5,256,128]{2,1,0:T(8,128)(2,1)S(1)}, u32[]{:S(2)}, u32[]{:S(2)}) collective-permute-start(bf16[5,256,128]{2,1,0:T(8,128)(2,1)S(1)} %collective-permute-done.4.refs_5_), channel_id=1, source_target_pairs={{0,64},{64,128},{128,192},{192,256},{256,320},{320,384},{384,448},... | collective-permute-start | bytes 983048 | tf_op jit(solution)/shard_map/ppermute | solution.py:120
  48.0 9.3 %collective-permute-start.1 = (bf16[5,256,128]{2,1,0:T(8,128)(2,1)S(1)}, bf16[5,256,128]{2,1,0:T(8,128)(2,1)S(1)}, u32[]{:S(2)}, u32[]{:S(2)}) collective-permute-start(bf16[5,256,128]{2,1,0:T(8,128)(2,1)S(1)} %collective-permute-done.refs_1_), channel_id=1, source_target_pairs={{0,64},{64,128},{128,192},{192,256},{256,320},{320,384},{384,448},... | collective-permute-start | bytes 983048 | tf_op jit(solution)/shard_map/ppermute | solution.py:120
  53.4 9.3 %collective-permute-start.6 = (bf16[5,256,128]{2,1,0:T(8,128)(2,1)S(1)}, bf16[5,256,128]{2,1,0:T(8,128)(2,1)S(1)}, u32[]{:S(2)}, u32[]{:S(2)}) collective-permute-start(bf16[5,256,128]{2,1,0:T(8,128)(2,1)S(1)} %collective-permute-done.5.refs_6_), channel_id=1, source_target_pairs={{0,64},{64,128},{128,192},{192,256},{256,320},{320,384},{384,448},... | collective-permute-start | bytes 983048 | tf_op jit(solution)/shard_map/ppermute | solution.py:120
  57.3 13.3 %collective-permute-start.2 = (bf16[5,256,128]{2,1,0:T(8,128)(2,1)S(1)}, bf16[5,256,128]{2,1,0:T(8,128)(2,1)S(1)}, u32[]{:S(2)}, u32[]{:S(2)}) collective-permute-start(bf16[5,256,128]{2,1,0:T(8,128)(2,1)S(1)} %collective-permute-done.1.refs_2_), channel_id=1, source_target_pairs={{0,64},{64,128},{128,192},{192,256},{256,320},{320,384},{384,448},... | collective-permute-start | bytes 983048 | tf_op jit(solution)/shard_map/ppermute | solution.py:120
  62.7 11.1 %collective-permute-start.7 = (bf16[5,256,128]{2,1,0:T(8,128)(2,1)S(1)}, bf16[5,256,128]{2,1,0:T(8,128)(2,1)S(1)}, u32[]{:S(2)}, u32[]{:S(2)}) collective-permute-start(bf16[5,256,128]{2,1,0:T(8,128)(2,1)S(1)} %collective-permute-done.6.refs_7_), channel_id=1, source_target_pairs={{0,64},{64,128},{128,192},{192,256},{256,320},{320,384},{384,448},... | collective-permute-start | bytes 983048 | tf_op jit(solution)/shard_map/ppermute | solution.py:120
  66.2 16.5 %collective-permute-start.8 = (bf16[10,256,128]{2,1,0:T(8,128)(2,1)S(1)}, bf16[10,256,128]{2,1,0:T(8,128)(2,1)S(1)}, u32[]{:S(2)}, u32[]{:S(2)}) collective-permute-start(bf16[10,256,128]{2,1,0:T(8,128)(2,1)S(1)} %pad_maximum_fusion), channel_id=1, source_target_pairs={{0,32},{32,0},{1,33},{33,1},{2,34},{34,2},{3,35},{35,3},{4,36},{36... | collective-permute-start | bytes 1966088 | tf_op jit(solution)/shard_map/ppermute | solution.py:115
  68.2 15.8 %collective-permute-start.9 = (bf16[10,256,128]{2,1,0:T(8,128)(2,1)S(1)}, bf16[10,256,128]{2,1,0:T(8,128)(2,1)S(1)}, u32[]{:S(2)}, u32[]{:S(2)}) collective-permute-start(bf16[10,256,128]{2,1,0:T(8,128)(2,1)S(1)} %pad_maximum_fusion.1), channel_id=1, source_target_pairs={{0,32},{32,0},{1,33},{33,1},{2,34},{34,2},{3,35},{35,3},{4,36},{36... | collective-permute-start | bytes 1966088 | tf_op jit(solution)/shard_map/ppermute | solution.py:115
  70.7 8.1 %collective-permute-start.3 = (bf16[5,256,128]{2,1,0:T(8,128)(2,1)S(1)}, bf16[5,256,128]{2,1,0:T(8,128)(2,1)S(1)}, u32[]{:S(2)}, u32[]{:S(2)}) collective-permute-start(bf16[5,256,128]{2,1,0:T(8,128)(2,1)S(1)} %collective-permute-done.2.refs_3_), channel_id=1, source_target_pairs={{0,64},{64,128},{128,192},{192,256},{256,320},{320,384},{384,448},... | collective-permute-start | bytes 983048 | tf_op jit(solution)/shard_map/ppermute | solution.py:120
  73.9 10.1 %collective-permute-start.10 = (bf16[10,256,128]{2,1,0:T(8,128)(2,1)S(1)}, bf16[10,256,128]{2,1,0:T(8,128)(2,1)S(1)}, u32[]{:S(2)}, u32[]{:S(2)}) collective-permute-start(bf16[10,256,128]{2,1,0:T(8,128)(2,1)S(1)} %pad_maximum_fusion.2), channel_id=1, source_target_pairs={{0,32},{32,0},{1,33},{33,1},{2,34},{34,2},{3,35},{35,3},{4,36},{36... | collective-permute-start | bytes 1966088 | tf_op jit(solution)/shard_map/ppermute | solution.py:115
  78.8 5.2 %collective-permute-start.11 = (bf16[5,256,128]{2,1,0:T(8,128)(2,1)S(1)}, bf16[5,256,128]{2,1,0:T(8,128)(2,1)S(1)}, u32[]{:S(2)}, u32[]{:S(2)}) collective-permute-start(bf16[5,256,128]{2,1,0:T(8,128)(2,1)S(1)} %collective-permute-done.3.refs_4_), channel_id=1, source_target_pairs={{0,32},{32,0},{1,33},{33,1},{2,34},{34,2},{3,35},{35,3},{4,36},{36... | collective-permute-start | bytes 983048 | tf_op jit(solution)/shard_map/ppermute | solution.py:115
  84.4 2.3 %copy-start = (bf16[40,512,128]{2,1,0:T(8,128)(2,1)}, bf16[40,512,128]{2,1,0:T(8,128)(2,1)S(1)}, u32[]{:S(2)}) copy-start(bf16[40,512,128]{2,1,0:T(8,128)(2,1)S(1)} %shard_map.37.factor) | copy-start | bytes 15728644

commit v6 on v5

--- a/solution.py
+++ b/solution.py
@@ -121,13 +121,15 @@
 
     mine = [piece.transpose(1, 0, 2, 3).reshape(UNITS, NAUX * 8, 128)]
     theirs = [swap(mine[0])]
-    swapped = []
-    for d in range(1, 5):
+    for d in range(1, 4):
         mine.append(pass_on(mine[-1]))
-        if d < 4:
-            theirs.append(pass_on(theirs[-1]))
-            swapped.append(swap(jnp.concatenate([mine[d], theirs[d]], axis=0)))
-    swapped.append(swap(mine[4]))
+        theirs.append(pass_on(theirs[-1]))
+    pairs = [jnp.concatenate([mine[d], theirs[d]], axis=0) for d in range(1, 4)]
+    pairs[0], pairs[1], mine[3] = lax.optimization_barrier(
+        (pairs[0], pairs[1], mine[3])
+    )
+    mine.append(pass_on(mine[3]))
+    swapped = [swap(pair) for pair in pairs] + [swap(mine[4])]
 
     factor = pl.pallas_call(
         assemble,

time: 93.8 us -> 92.9 us (level)
  waiting for transfers between devices: 13.5 us -> 10.9 us
  starting transfers between devices: 65.3 us -> 66.9 us
    ppermute x7, waiting for transfers between devices: 5.25 us -> 2.65 us  [pass_on(): return lax.ppermute(value, ('z', 'core'), up + down)]
    ppermute x7, starting transfers between devices: 33.6 us -> 35.8 us  [pass_on(): return lax.ppermute(value, ('z', 'core'), up + down)]
where the time goes in v6:
time: 92.9 us; the launch traced here: 92.1 us
  starting transfers between devices  66.9 us (72%)
  waiting for transfers between devices  10.9 us (12%)
  Pallas kernels  6.78 us (7%)
  local copies, waits for them, and re-layouts  6.33 us (7%)
  other arithmetic  1.02 us (1%)
    ppermute x7, starting transfers between devices, pass_on(): return lax.ppermute(value, ('z', 'core'), up + down)  35.8 us
    ppermute x5, starting transfers between devices, swap(): return lax.ppermute(value, 'core', ring(2, 1))  13.4 us
    all_to_all x1, starting transfers between devices, local(): piece = lax.all_to_all(piece, ('x', 'y'), 0, 0, tiled=True)  10.5 us
    all_to_all x1, starting transfers between devices, local(): columns = lax.all_to_all(sections, ('x', 'y'), 0, 0, tiled=True)  7.23 us
    all_to_all x1, waiting for transfers between devices, local(): piece = lax.all_to_all(piece, ('x', 'y'), 0, 0, tiled=True)  6.99 us
    pallas_call x1, Pallas kernels, local(): pl.pallas_call(solve, out_shape=jax.ShapeDtypeStruct((4 * 512, width), bf...  6.42 us
    reshape x1, local copies, waits for them, and re-layouts, local(): sections = integrals.reshape(rows, NAUX, width).transpose(1, 0, 2)  3.19 us
    ppermute x7, waiting for transfers between devices, pass_on(): return lax.ppermute(value, ('z', 'core'), up + down)  2.65 us
  transfers between devices with their start and end apart: 14, of which 5 were waited for; matrix products, arithmetic and copies ran while one was open for 4% of the time, Pallas kernels for 0%

profile of v6, /device:TPU:1, one launch (start us, length us, event | category | flops | bytes accessed | tf_op | source)
XLA Modules:
  0.0 92.1 jit_solution(16687529224526841456)
XLA Ops:
  0.0 0.8 fusion
  0.9 0.8 broadcast_in_dim.2
  1.6 10.5 %all-to-all-start = ((bf16[32,5,8,128]{3,2,1,0:T(8,128)(2,1)}), bf16[32,5,8,128]{3,2,1,0:T(8,128)(2,1)S(1)}, u32[]{:S(2)}, u32[]{:S(2)}) async-start(bf16[32,5,8,128]{3,2,1,0:T(8,128)(2,1)} %broadcast_in_dim.2), calls=%async_computation | async-start | bytes 655360 | tf_op jit(solution)/shard_map/all_to_all | solution.py:108
  12.2 3.2 %copy.10 = bf16[8,32,8,512]{3,2,0,1:T(8,128)(2,1)} copy(bf16[8,32,8,512]{3,2,1,0:T(8,128)(2,1)} %bitcast.16) | data formatting | bytes 4194304 | tf_op jit(solution)/shard_map/reshape | solution.py:110
  15.3 7.0 %all-to-all-done = bf16[32,5,8,128]{3,2,1,0:T(8,128)(2,1)S(1)} async-done(((bf16[32,5,8,128]{3,2,1,0:T(8,128)(2,1)}), bf16[32,5,8,128]{3,2,1,0:T(8,128)(2,1)S(1)}, u32[]{:S(2)}, u32[]{:S(2)}) %all-to-all-start) | async-done | bytes 327712 | tf_op jit(solution)/shard_map/all_to_all | solution.py:108
  22.3 7.2 %all-to-all-start.1 = ((bf16[32,64,512]{2,1,0:T(8,128)(2,1)}), bf16[32,64,512]{2,1,0:T(8,128)(2,1)S(1)}, u32[]{:S(2)}, u32[]{:S(2)}) async-start(bf16[32,64,512]{2,1,0:T(8,128)(2,1)} %bitcast.15), calls=%async_computation.1 | async-start | bytes 4194304 | tf_op jit(solution)/shard_map/all_to_all | solution.py:112
  29.6 0.1 copy_bitcast_fusion.refs_0_
  29.6 3.7 %collective-permute-start.2 = (bf16[5,256,128]{2,1,0:T(8,128)(2,1)S(1)}, bf16[5,256,128]{2,1,0:T(8,128)(2,1)S(1)}, u32[]{:S(2)}, u32[]{:S(2)}) collective-permute-start(bf16[5,256,128]{2,1,0:T(8,128)(2,1)S(1)} %copy_bitcast_fusion.refs_0_), channel_id=1, source_target_pairs={{0,32},{32,0},{1,33},{33,1},{2,34},{34,2},{3,35},{35,3},{4,36},{36... | collective-permute-start | bytes 983048 | tf_op jit(solution)/shard_map/ppermute | solution.py:115
  33.4 10.7 %collective-permute-start = (bf16[5,256,128]{2,1,0:T(8,128)(2,1)S(1)}, bf16[5,256,128]{2,1,0:T(8,128)(2,1)S(1)}, u32[]{:S(2)}, u32[]{:S(2)}) collective-permute-start(bf16[5,256,128]{2,1,0:T(8,128)(2,1)S(1)} %copy_bitcast_fusion.refs_0_), channel_id=1, source_target_pairs={{0,64},{64,128},{128,192},{192,256},{256,320},{320,384},{384,448},... | collective-permute-start | bytes 983048 | tf_op jit(solution)/shard_map/ppermute | solution.py:120
  44.0 0.0 collective-permute-done.2.refs_5_
  44.0 2.2 %collective-permute-start.3 = (bf16[5,256,128]{2,1,0:T(8,128)(2,1)S(1)}, bf16[5,256,128]{2,1,0:T(8,128)(2,1)S(1)}, u32[]{:S(2)}, u32[]{:S(2)}) collective-permute-start(bf16[5,256,128]{2,1,0:T(8,128)(2,1)S(1)} %collective-permute-done.2.refs_5_), channel_id=1, source_target_pairs={{0,64},{64,128},{128,192},{192,256},{256,320},{320,384},{384,448},... | collective-permute-start | bytes 983048 | tf_op jit(solution)/shard_map/ppermute | solution.py:120
  46.2 1.8 %collective-permute-done.refs_1_ = bf16[5,256,128]{2,1,0:T(8,128)(2,1)S(1)} collective-permute-done((bf16[5,256,128]{2,1,0:T(8,128)(2,1)S(1)}, bf16[5,256,128]{2,1,0:T(8,128)(2,1)S(1)}, u32[]{:S(2)}, u32[]{:S(2)}) %collective-permute-start) | collective-permute-done | bytes 327712 | tf_op jit(solution)/shard_map/ppermute | solution.py:120
  48.0 5.3 %collective-permute-start.1 = (bf16[5,256,128]{2,1,0:T(8,128)(2,1)S(1)}, bf16[5,256,128]{2,1,0:T(8,128)(2,1)S(1)}, u32[]{:S(2)}, u32[]{:S(2)}) collective-permute-start(bf16[5,256,128]{2,1,0:T(8,128)(2,1)S(1)} %collective-permute-done.refs_1_), channel_id=1, source_target_pairs={{0,64},{64,128},{128,192},{192,256},{256,320},{320,384},{384,448},... | collective-permute-start | bytes 983048 | tf_op jit(solution)/shard_map/ppermute | solution.py:120
  53.3 0.0 collective-permute-done.3.refs_6_
  53.4 3.5 %collective-permute-start.4 = (bf16[5,256,128]{2,1,0:T(8,128)(2,1)S(1)}, bf16[5,256,128]{2,1,0:T(8,128)(2,1)S(1)}, u32[]{:S(2)}, u32[]{:S(2)}) collective-permute-start(bf16[5,256,128]{2,1,0:T(8,128)(2,1)S(1)} %collective-permute-done.3.refs_6_), channel_id=1, source_target_pairs={{0,64},{64,128},{128,192},{192,256},{256,320},{320,384},{384,448},... | collective-permute-start | bytes 983048 | tf_op jit(solution)/shard_map/ppermute | solution.py:120
  56.9 0.5 collective-permute-done.1.refs_2_
  57.3 5.3 %collective-permute-start.5 = (bf16[5,256,128]{2,1,0:T(8,128)(2,1)S(1)}, bf16[5,256,128]{2,1,0:T(8,128)(2,1)S(1)}, u32[]{:S(2)}, u32[]{:S(2)}) collective-permute-start(bf16[5,256,128]{2,1,0:T(8,128)(2,1)S(1)} %collective-permute-done.1.refs_2_), channel_id=1, source_target_pairs={{0,64},{64,128},{128,192},{192,256},{256,320},{320,384},{384,448},... | collective-permute-start | bytes 983048 | tf_op jit(solution)/shard_map/ppermute | solution.py:120
  62.7 0.0 collective-permute-done.4.refs_7_
  62.7 3.5 %collective-permute-start.7 = (bf16[5,256,128]{2,1,0:T(8,128)(2,1)S(1)}, bf16[5,256,128]{2,1,0:T(8,128)(2,1)S(1)}, u32[]{:S(2)}, u32[]{:S(2)}) collective-permute-start(bf16[5,256,128]{2,1,0:T(8,128)(2,1)S(1)} %collective-permute-done.4.refs_7_), channel_id=1, source_target_pairs={{0,64},{64,128},{128,192},{192,256},{256,320},{320,384},{384,448},... | collective-permute-start | bytes 983048 | tf_op jit(solution)/shard_map/ppermute | solution.py:120
  66.2 0.1 pad_maximum_fusion
  66.2 0.1 pad_maximum_fusion.1
  66.3 0.4 collective-permute-done.5.refs_3_
  66.7 5.3 %collective-permute-start.6 = (bf16[5,256,128]{2,1,0:T(8,128)(2,1)S(1)}, bf16[5,256,128]{2,1,0:T(8,128)(2,1)S(1)}, u32[]{:S(2)}, u32[]{:S(2)}) collective-permute-start(bf16[5,256,128]{2,1,0:T(8,128)(2,1)S(1)} %collective-permute-done.5.refs_3_), channel_id=1, source_target_pairs={{0,64},{64,128},{128,192},{192,256},{256,320},{320,384},{384,448},... | collective-permute-start | bytes 983048 | tf_op jit(solution)/shard_map/ppermute | solution.py:120
  72.0 1.9 %collective-permute-start.8 = (bf16[10,256,128]{2,1,0:T(8,128)(2,1)S(1)}, bf16[10,256,128]{2,1,0:T(8,128)(2,1)S(1)}, u32[]{:S(2)}, u32[]{:S(2)}) collective-permute-start(bf16[10,256,128]{2,1,0:T(8,128)(2,1)S(1)} %pad_maximum_fusion), channel_id=1, source_target_pairs={{0,32},{32,0},{1,33},{33,1},{2,34},{34,2},{3,35},{35,3},{4,36},{36... | collective-permute-start | bytes 1966088 | tf_op jit(solution)/shard_map/ppermute | solution.py:115
  73.9 2.4 %collective-permute-start.9 = (bf16[10,256,128]{2,1,0:T(8,128)(2,1)S(1)}, bf16[10,256,128]{2,1,0:T(8,128)(2,1)S(1)}, u32[]{:S(2)}, u32[]{:S(2)}) collective-permute-start(bf16[10,256,128]{2,1,0:T(8,128)(2,1)S(1)} %pad_maximum_fusion.1), channel_id=1, source_target_pairs={{0,32},{32,0},{1,33},{33,1},{2,34},{34,2},{3,35},{35,3},{4,36},{36... | collective-permute-start | bytes 1966088 | tf_op jit(solution)/shard_map/ppermute | solution.py:115
  76.3 0.0 collective-permute-done.7.refs_8_
  76.3 0.1 pad_maximum_fusion.2
  76.4 1.9 %collective-permute-start.10 = (bf16[10,256,128]{2,1,0:T(8,128)(2,1)S(1)}, bf16[10,256,128]{2,1,0:T(8,128)(2,1)S(1)}, u32[]{:S(2)}, u32[]{:S(2)}) collective-permute-start(bf16[10,256,128]{2,1,0:T(8,128)(2,1)S(1)} %pad_maximum_fusion.2), channel_id=1, source_target_pairs={{0,32},{32,0},{1,33},{33,1},{2,34},{34,2},{3,35},{35,3},{4,36},{36... | collective-permute-start | bytes 1966088 | tf_op jit(solution)/shard_map/ppermute | solution.py:115
  78.3 0.0 collective-permute-done.6.refs_4_
  78.3 3.4 %collective-permute-start.11 = (bf16[5,256,128]{2,1,0:T(8,128)(2,1)S(1)}, bf16[5,256,128]{2,1,0:T(8,128)(2,1)S(1)}, u32[]{:S(2)}, u32[]{:S(2)}) collective-permute-start(bf16[5,256,128]{2,1,0:T(8,128)(2,1)S(1)} %collective-permute-done.6.refs_4_), channel_id=1, source_target_pairs={{0,32},{32,0},{1,33},{33,1},{2,34},{34,2},{3,35},{35,3},{4,36},{36... | collective-permute-start | bytes 983048 | tf_op jit(solution)/shard_map/ppermute | solution.py:115
  81.8 1.2 %collective-permute-done.11.refs_12_ = bf16[5,256,128]{2,1,0:T(8,128)(2,1)S(1)} collective-permute-done((bf16[5,256,128]{2,1,0:T(8,128)(2,1)S(1)}, bf16[5,256,128]{2,1,0:T(8,128)(2,1)S(1)}, u32[]{:S(2)}, u32[]{:S(2)}) %collective-permute-start.11) | collective-permute-done | bytes 327712 | tf_op jit(solution)/shard_map/ppermute | solution.py:115
  83.0 0.0 collective-permute-done.8.refs_9_
  83.0 0.0 collective-permute-done.9.refs_10_
  83.0 0.0 collective-permute-done.10.refs_11_
  83.0 0.4 shard_map.37.factor
  83.4 0.0 copy-start
  83.4 2.3 %copy-done = bf16[40,512,128]{2,1,0:T(8,128)(2,1)} copy-done((bf16[40,512,128]{2,1,0:T(8,128)(2,1)}, bf16[40,512,128]{2,1,0:T(8,128)(2,1)S(1)}, u32[]{:S(2)}) %copy-start) | copy-done | bytes 5242904
  85.7 0.0 all-to-all-done.1
  85.7 6.4 %shard_map.38 = bf16[2048,512]{1,0:T(8,128)(2,1)} custom-call(bf16[40,512,128]{2,1,0:T(8,128)(2,1)} %copy-done, bf16[2048,512]{1,0:T(8,128)(2,1)S(1)} %bitcast.14), custom_call_target="tpu_custom_call" | custom-call | flops 2684354560 | bytes 9437184 | tf_op jit(solution)/shard_map/pallas_call | solution.py:143
  (3 shorter events, 0.0 us)
Async XLA Ops:
  1.6 20.7 %all-to-all-start = ((bf16[32,5,8,128]{3,2,1,0:T(8,128)(2,1)}), bf16[32,5,8,128]{3,2,1,0:T(8,128)(2,1)S(1)}, u32[]{:S(2)}, u32[]{:S(2)}) async-start(bf16[32,5,8,128]{3,2,1,0:T(8,128)(2,1)} %broadcast_in_dim.2), calls=%async_computation | async-start | bytes 655360 | tf_op jit(solution)/shard_map/all_to_all | solution.py:108
  22.3 63.4 %all-to-all-start.1 = ((bf16[32,64,512]{2,1,0:T(8,128)(2,1)}), bf16[32,64,512]{2,1,0:T(8,128)(2,1)S(1)}, u32[]{:S(2)}, u32[]{:S(2)}) async-start(bf16[32,64,512]{2,1,0:T(8,128)(2,1)} %bitcast.15), calls=%async_computation.1 | async-start | bytes 4194304 | tf_op jit(solution)/shard_map/all_to_all | solution.py:112
  29.6 14.4 %collective-permute-start.2 = (bf16[5,256,128]{2,1,0:T(8,128)(2,1)S(1)}, bf16[5,256,128]{2,1,0:T(8,128)(2,1)S(1)}, u32[]{:S(2)}, u32[]{:S(2)}) collective-permute-start(bf16[5,256,128]{2,1,0:T(8,128)(2,1)S(1)} %copy_bitcast_fusion.refs_0_), channel_id=1, source_target_pairs={{0,32},{32,0},{1,33},{33,1},{2,34},{34,2},{3,35},{35,3},{4,36},{36... | collective-permute-start | bytes 983048 | tf_op jit(solution)/shard_map/ppermute | solution.py:115
  33.4 14.7 %collective-permute-start = (bf16[5,256,128]{2,1,0:T(8,128)(2,1)S(1)}, bf16[5,256,128]{2,1,0:T(8,128)(2,1)S(1)}, u32[]{:S(2)}, u32[]{:S(2)}) collective-permute-start(bf16[5,256,128]{2,1,0:T(8,128)(2,1)S(1)} %copy_bitcast_fusion.refs_0_), channel_id=1, source_target_pairs={{0,64},{64,128},{128,192},{192,256},{256,320},{320,384},{384,448},... | collective-permute-start | bytes 983048 | tf_op jit(solution)/shard_map/ppermute | solution.py:120
  44.0 9.3 %collective-permute-start.3 = (bf16[5,256,128]{2,1,0:T(8,128)(2,1)S(1)}, bf16[5,256,128]{2,1,0:T(8,128)(2,1)S(1)}, u32[]{:S(2)}, u32[]{:S(2)}) collective-permute-start(bf16[5,256,128]{2,1,0:T(8,128)(2,1)S(1)} %collective-permute-done.2.refs_5_), channel_id=1, source_target_pairs={{0,64},{64,128},{128,192},{192,256},{256,320},{320,384},{384,448},... | collective-permute-start | bytes 983048 | tf_op jit(solution)/shard_map/ppermute | solution.py:120
  48.0 9.3 %collective-permute-start.1 = (bf16[5,256,128]{2,1,0:T(8,128)(2,1)S(1)}, bf16[5,256,128]{2,1,0:T(8,128)(2,1)S(1)}, u32[]{:S(2)}, u32[]{:S(2)}) collective-permute-start(bf16[5,256,128]{2,1,0:T(8,128)(2,1)S(1)} %collective-permute-done.refs_1_), channel_id=1, source_target_pairs={{0,64},{64,128},{128,192},{192,256},{256,320},{320,384},{384,448},... | collective-permute-start | bytes 983048 | tf_op jit(solution)/shard_map/ppermute | solution.py:120
  53.4 9.3 %collective-permute-start.4 = (bf16[5,256,128]{2,1,0:T(8,128)(2,1)S(1)}, bf16[5,256,128]{2,1,0:T(8,128)(2,1)S(1)}, u32[]{:S(2)}, u32[]{:S(2)}) collective-permute-start(bf16[5,256,128]{2,1,0:T(8,128)(2,1)S(1)} %collective-permute-done.3.refs_6_), channel_id=1, source_target_pairs={{0,64},{64,128},{128,192},{192,256},{256,320},{320,384},{384,448},... | collective-permute-start | bytes 983048 | tf_op jit(solution)/shard_map/ppermute | solution.py:120
  57.3 9.3 %collective-permute-start.5 = (bf16[5,256,128]{2,1,0:T(8,128)(2,1)S(1)}, bf16[5,256,128]{2,1,0:T(8,128)(2,1)S(1)}, u32[]{:S(2)}, u32[]{:S(2)}) collective-permute-start(bf16[5,256,128]{2,1,0:T(8,128)(2,1)S(1)} %collective-permute-done.1.refs_2_), channel_id=1, source_target_pairs={{0,64},{64,128},{128,192},{192,256},{256,320},{320,384},{384,448},... | collective-permute-start | bytes 983048 | tf_op jit(solution)/shard_map/ppermute | solution.py:120
  62.7 13.6 %collective-permute-start.7 = (bf16[5,256,128]{2,1,0:T(8,128)(2,1)S(1)}, bf16[5,256,128]{2,1,0:T(8,128)(2,1)S(1)}, u32[]{:S(2)}, u32[]{:S(2)}) collective-permute-start(bf16[5,256,128]{2,1,0:T(8,128)(2,1)S(1)} %collective-permute-done.4.refs_7_), channel_id=1, source_target_pairs={{0,64},{64,128},{128,192},{192,256},{256,320},{320,384},{384,448},... | collective-permute-start | bytes 983048 | tf_op jit(solution)/shard_map/ppermute | solution.py:120
  66.7 11.7 %collective-permute-start.6 = (bf16[5,256,128]{2,1,0:T(8,128)(2,1)S(1)}, bf16[5,256,128]{2,1,0:T(8,128)(2,1)S(1)}, u32[]{:S(2)}, u32[]{:S(2)}) collective-permute-start(bf16[5,256,128]{2,1,0:T(8,128)(2,1)S(1)} %collective-permute-done.5.refs_3_), channel_id=1, source_target_pairs={{0,64},{64,128},{128,192},{192,256},{256,320},{320,384},{384,448},... | collective-permute-start | bytes 983048 | tf_op jit(solution)/shard_map/ppermute | solution.py:120
  72.0 11.0 %collective-permute-start.8 = (bf16[10,256,128]{2,1,0:T(8,128)(2,1)S(1)}, bf16[10,256,128]{2,1,0:T(8,128)(2,1)S(1)}, u32[]{:S(2)}, u32[]{:S(2)}) collective-permute-start(bf16[10,256,128]{2,1,0:T(8,128)(2,1)S(1)} %pad_maximum_fusion), channel_id=1, source_target_pairs={{0,32},{32,0},{1,33},{33,1},{2,34},{34,2},{3,35},{35,3},{4,36},{36... | collective-permute-start | bytes 1966088 | tf_op jit(solution)/shard_map/ppermute | solution.py:115
  73.9 9.1 %collective-permute-start.9 = (bf16[10,256,128]{2,1,0:T(8,128)(2,1)S(1)}, bf16[10,256,128]{2,1,0:T(8,128)(2,1)S(1)}, u32[]{:S(2)}, u32[]{:S(2)}) collective-permute-start(bf16[10,256,128]{2,1,0:T(8,128)(2,1)S(1)} %pad_maximum_fusion.1), channel_id=1, source_target_pairs={{0,32},{32,0},{1,33},{33,1},{2,34},{34,2},{3,35},{35,3},{4,36},{36... | collective-permute-start | bytes 1966088 | tf_op jit(solution)/shard_map/ppermute | solution.py:115
  76.4 6.6 %collective-permute-start.10 = (bf16[10,256,128]{2,1,0:T(8,128)(2,1)S(1)}, bf16[10,256,128]{2,1,0:T(8,128)(2,1)S(1)}, u32[]{:S(2)}, u32[]{:S(2)}) collective-permute-start(bf16[10,256,128]{2,1,0:T(8,128)(2,1)S(1)} %pad_maximum_fusion.2), channel_id=1, source_target_pairs={{0,32},{32,0},{1,33},{33,1},{2,34},{34,2},{3,35},{35,3},{4,36},{36... | collective-permute-start | bytes 1966088 | tf_op jit(solution)/shard_map/ppermute | solution.py:115
  78.3 4.7 %collective-permute-start.11 = (bf16[5,256,128]{2,1,0:T(8,128)(2,1)S(1)}, bf16[5,256,128]{2,1,0:T(8,128)(2,1)S(1)}, u32[]{:S(2)}, u32[]{:S(2)}) collective-permute-start(bf16[5,256,128]{2,1,0:T(8,128)(2,1)S(1)} %collective-permute-done.6.refs_4_), channel_id=1, source_target_pairs={{0,32},{32,0},{1,33},{33,1},{2,34},{34,2},{3,35},{35,3},{4,36},{36... | collective-permute-start | bytes 983048 | tf_op jit(solution)/shard_map/ppermute | solution.py:115
  83.4 2.3 %copy-start = (bf16[40,512,128]{2,1,0:T(8,128)(2,1)}, bf16[40,512,128]{2,1,0:T(8,128)(2,1)S(1)}, u32[]{:S(2)}) copy-start(bf16[40,512,128]{2,1,0:T(8,128)(2,1)S(1)} %shard_map.37.factor) | copy-start | bytes 15728644

commit v7 on v6

--- a/solution.py
+++ b/solution.py
@@ -7,15 +7,17 @@
 
 NX, NY, NZ = 4, 8, 8
 NAUX = NX * NY
-AHEAD = 3
+AHEAD = 8
 SPLIT = 1
+FIRST = (0, 4)
 UNITS = 5
 ANY = pl.BlockSpec(memory_space=pl.ANY)
 VMEM = pl.BlockSpec(memory_space=pltpu.VMEM)
 
 
 def assemble(*refs):
-    mine, theirs, swapped, factor = refs[:5], refs[5:9], refs[9:13], refs[13]
+    mine, theirs, swapped = refs[:5], refs[5:9], refs[9:13]
+    factor, head = refs[13:]
     z, core = lax.axis_index("z"), lax.axis_index("core")
     along = 1 - 2 * core
     places = []
@@ -33,6 +35,8 @@
         row = pl.multiple_of(half * 256, 256)
         for i in range(UNITS):
             factor[unit + i, pl.ds(row, 256), :] = ref[at + i]
+    for at, block in enumerate(FIRST):
+        head[4 * at : 4 * at + 4] = factor[4 * block : 4 * block + 4]
 
 
 def product(panels, block, solved):
@@ -48,9 +52,9 @@
     )
 
 
-def solve(factor, columns, out, panels, held, sems):
+def solve(factor, head, columns, out, panels, held, sems):
     below = [[4 + k * (k - 1) // 2 + j for j in range(k)] for k in range(4)]
-    order = [b for k in range(4) for b in below[k] + [k]]
+    order = [b for k in range(4) for b in below[k] + [k] if b not in FIRST]
     loads = {}
     for b in order:
         units = pl.ds(4 * b, 4)
@@ -59,10 +63,13 @@
         )
 
     def ready(b):
+        if b in FIRST:
+            return head, FIRST.index(b)
         loads[b].wait()
         ahead = order.index(b) + AHEAD
         if ahead < len(order):
             loads[order[ahead]].start()
+        return panels, b
 
     for b in order[:AHEAD]:
         loads[b].start()
@@ -73,12 +80,12 @@
         cuts = [slice(h * width, (h + 1) * width) for h in range(SPLIT)]
         acc = [columns[rows, cut].astype(jnp.float32) for cut in cuts]
         for j, b in enumerate(below[k]):
-            ready(b)
+            left = ready(b)
             for h, cut in enumerate(cuts):
-                acc[h] = acc[h] - product(panels, b, held[j, :, cut])
-        ready(k)
+                acc[h] = acc[h] - product(*left, held[j, :, cut])
+        left = ready(k)
         for h, cut in enumerate(cuts):
-            held[k, :, cut] = product(panels, k, acc[h].astype(jnp.bfloat16)).astype(
+            held[k, :, cut] = product(*left, acc[h].astype(jnp.bfloat16)).astype(
                 jnp.bfloat16
             )
         stores.append(pltpu.make_async_copy(held.at[k], out.at[rows], sems.at[10 + k]))
@@ -131,11 +138,14 @@
     mine.append(pass_on(mine[3]))
     swapped = [swap(pair) for pair in pairs] + [swap(mine[4])]
 
-    factor = pl.pallas_call(
+    factor, head = pl.pallas_call(
         assemble,
-        out_shape=jax.ShapeDtypeStruct((40, 512, 128), bf16),
+        out_shape=[
+            jax.ShapeDtypeStruct((40, 512, 128), bf16),
+            jax.ShapeDtypeStruct((4 * len(FIRST), 512, 128), bf16),
+        ],
         in_specs=[VMEM] * 13,
-        out_specs=VMEM,
+        out_specs=[VMEM] * 2,
         compiler_params=pltpu.CompilerParams(vmem_limit_bytes=16 << 20),
         cost_estimate=cost(0, 10 << 20),
     )(*mine, *theirs, *swapped)
@@ -143,7 +153,7 @@
     return pl.pallas_call(
         solve,
         out_shape=jax.ShapeDtypeStruct((4 * 512, width), bf16),
-        in_specs=[ANY, VMEM],
+        in_specs=[ANY, VMEM, VMEM],
         out_specs=ANY,
         scratch_shapes=[
             pltpu.VMEM((40, 512, 128), bf16),
@@ -152,7 +162,7 @@
         ],
         compiler_params=pltpu.CompilerParams(vmem_limit_bytes=48 << 20),
         cost_estimate=cost(20 * 512**3, 9 << 20),
-    )(factor, columns.reshape(4 * 512, width))
+    )(factor, head, columns.reshape(4 * 512, width))
 
 
 def solution(mesh):

time: 92.9 us -> 92 us (level)
  no operation moved by 1% of the time
where the time goes in v7:
time: 92 us; the launch traced here: 91.3 us
  starting transfers between devices  66.9 us (73%)
  waiting for transfers between devices  10.9 us (12%)
  local copies, waits for them, and re-layouts  6.35 us (7%)
  Pallas kernels  5.97 us (6%)
  other arithmetic  1.02 us (1%)
    ppermute x7, starting transfers between devices, pass_on(): return lax.ppermute(value, ('z', 'core'), up + down)  35.8 us
    ppermute x5, starting transfers between devices, swap(): return lax.ppermute(value, 'core', ring(2, 1))  13.4 us
    all_to_all x1, starting transfers between devices, local(): piece = lax.all_to_all(piece, ('x', 'y'), 0, 0, tiled=True)  10.5 us
    all_to_all x1, starting transfers between devices, local(): columns = lax.all_to_all(sections, ('x', 'y'), 0, 0, tiled=True)  7.23 us
    all_to_all x1, waiting for transfers between devices, local(): piece = lax.all_to_all(piece, ('x', 'y'), 0, 0, tiled=True)  6.99 us
    pallas_call x1, Pallas kernels, local(): pl.pallas_call(solve, out_shape=jax.ShapeDtypeStruct((4 * 512, width), bf...  5.53 us
    reshape x1, local copies, waits for them, and re-layouts, local(): sections = integrals.reshape(rows, NAUX, width).transpose(1, 0, 2)  3.19 us
    ppermute x7, waiting for transfers between devices, pass_on(): return lax.ppermute(value, ('z', 'core'), up + down)  2.65 us
  transfers between devices with their start and end apart: 14, of which 5 were waited for; matrix products, arithmetic and copies ran while one was open for 4% of the time, Pallas kernels for 0%

profile of v7, /device:TPU:1, one launch (start us, length us, event | category | flops | bytes accessed | tf_op | source)
XLA Modules:
  0.0 91.3 jit_solution(15911846004089611716)
XLA Ops:
  0.0 0.8 fusion
  0.9 0.8 broadcast_in_dim.2
  1.7 10.5 %all-to-all-start = ((bf16[32,5,8,128]{3,2,1,0:T(8,128)(2,1)}), bf16[32,5,8,128]{3,2,1,0:T(8,128)(2,1)S(1)}, u32[]{:S(2)}, u32[]{:S(2)}) async-start(bf16[32,5,8,128]{3,2,1,0:T(8,128)(2,1)} %broadcast_in_dim.2), calls=%async_computation | async-start | bytes 655360 | tf_op jit(solution)/shard_map/all_to_all | solution.py:115
  12.2 3.2 %copy.10 = bf16[8,32,8,512]{3,2,0,1:T(8,128)(2,1)} copy(bf16[8,32,8,512]{3,2,1,0:T(8,128)(2,1)} %bitcast.16) | data formatting | bytes 4194304 | tf_op jit(solution)/shard_map/reshape | solution.py:117
  15.4 7.0 %all-to-all-done = bf16[32,5,8,128]{3,2,1,0:T(8,128)(2,1)S(1)} async-done(((bf16[32,5,8,128]{3,2,1,0:T(8,128)(2,1)}), bf16[32,5,8,128]{3,2,1,0:T(8,128)(2,1)S(1)}, u32[]{:S(2)}, u32[]{:S(2)}) %all-to-all-start) | async-done | bytes 327712 | tf_op jit(solution)/shard_map/all_to_all | solution.py:115
  22.3 7.2 %all-to-all-start.1 = ((bf16[32,64,512]{2,1,0:T(8,128)(2,1)}), bf16[32,64,512]{2,1,0:T(8,128)(2,1)S(1)}, u32[]{:S(2)}, u32[]{:S(2)}) async-start(bf16[32,64,512]{2,1,0:T(8,128)(2,1)} %bitcast.15), calls=%async_computation.1 | async-start | bytes 4194304 | tf_op jit(solution)/shard_map/all_to_all | solution.py:119
  29.6 0.1 copy_bitcast_fusion.refs_0_
  29.6 3.7 %collective-permute-start.2 = (bf16[5,256,128]{2,1,0:T(8,128)(2,1)S(1)}, bf16[5,256,128]{2,1,0:T(8,128)(2,1)S(1)}, u32[]{:S(2)}, u32[]{:S(2)}) collective-permute-start(bf16[5,256,128]{2,1,0:T(8,128)(2,1)S(1)} %copy_bitcast_fusion.refs_0_), channel_id=1, source_target_pairs={{0,32},{32,0},{1,33},{33,1},{2,34},{34,2},{3,35},{35,3},{4,36},{36... | collective-permute-start | bytes 983048 | tf_op jit(solution)/shard_map/ppermute | solution.py:122
  33.4 10.7 %collective-permute-start = (bf16[5,256,128]{2,1,0:T(8,128)(2,1)S(1)}, bf16[5,256,128]{2,1,0:T(8,128)(2,1)S(1)}, u32[]{:S(2)}, u32[]{:S(2)}) collective-permute-start(bf16[5,256,128]{2,1,0:T(8,128)(2,1)S(1)} %copy_bitcast_fusion.refs_0_), channel_id=1, source_target_pairs={{0,64},{64,128},{128,192},{192,256},{256,320},{320,384},{384,448},... | collective-permute-start | bytes 983048 | tf_op jit(solution)/shard_map/ppermute | solution.py:127
  44.0 0.0 collective-permute-done.2.refs_5_
  44.0 2.2 %collective-permute-start.3 = (bf16[5,256,128]{2,1,0:T(8,128)(2,1)S(1)}, bf16[5,256,128]{2,1,0:T(8,128)(2,1)S(1)}, u32[]{:S(2)}, u32[]{:S(2)}) collective-permute-start(bf16[5,256,128]{2,1,0:T(8,128)(2,1)S(1)} %collective-permute-done.2.refs_5_), channel_id=1, source_target_pairs={{0,64},{64,128},{128,192},{192,256},{256,320},{320,384},{384,448},... | collective-permute-start | bytes 983048 | tf_op jit(solution)/shard_map/ppermute | solution.py:127
  46.2 1.8 %collective-permute-done.refs_1_ = bf16[5,256,128]{2,1,0:T(8,128)(2,1)S(1)} collective-permute-done((bf16[5,256,128]{2,1,0:T(8,128)(2,1)S(1)}, bf16[5,256,128]{2,1,0:T(8,128)(2,1)S(1)}, u32[]{:S(2)}, u32[]{:S(2)}) %collective-permute-start) | collective-permute-done | bytes 327712 | tf_op jit(solution)/shard_map/ppermute | solution.py:127
  48.0 5.3 %collective-permute-start.1 = (bf16[5,256,128]{2,1,0:T(8,128)(2,1)S(1)}, bf16[5,256,128]{2,1,0:T(8,128)(2,1)S(1)}, u32[]{:S(2)}, u32[]{:S(2)}) collective-permute-start(bf16[5,256,128]{2,1,0:T(8,128)(2,1)S(1)} %collective-permute-done.refs_1_), channel_id=1, source_target_pairs={{0,64},{64,128},{128,192},{192,256},{256,320},{320,384},{384,448},... | collective-permute-start | bytes 983048 | tf_op jit(solution)/shard_map/ppermute | solution.py:127
  53.4 0.0 collective-permute-done.3.refs_6_
  53.4 3.5 %collective-permute-start.4 = (bf16[5,256,128]{2,1,0:T(8,128)(2,1)S(1)}, bf16[5,256,128]{2,1,0:T(8,128)(2,1)S(1)}, u32[]{:S(2)}, u32[]{:S(2)}) collective-permute-start(bf16[5,256,128]{2,1,0:T(8,128)(2,1)S(1)} %collective-permute-done.3.refs_6_), channel_id=1, source_target_pairs={{0,64},{64,128},{128,192},{192,256},{256,320},{320,384},{384,448},... | collective-permute-start | bytes 983048 | tf_op jit(solution)/shard_map/ppermute | solution.py:127
  56.9 0.5 collective-permute-done.1.refs_2_
  57.4 5.3 %collective-permute-start.5 = (bf16[5,256,128]{2,1,0:T(8,128)(2,1)S(1)}, bf16[5,256,128]{2,1,0:T(8,128)(2,1)S(1)}, u32[]{:S(2)}, u32[]{:S(2)}) collective-permute-start(bf16[5,256,128]{2,1,0:T(8,128)(2,1)S(1)} %collective-permute-done.1.refs_2_), channel_id=1, source_target_pairs={{0,64},{64,128},{128,192},{192,256},{256,320},{320,384},{384,448},... | collective-permute-start | bytes 983048 | tf_op jit(solution)/shard_map/ppermute | solution.py:127
  62.7 0.0 collective-permute-done.4.refs_7_
  62.7 3.5 %collective-permute-start.7 = (bf16[5,256,128]{2,1,0:T(8,128)(2,1)S(1)}, bf16[5,256,128]{2,1,0:T(8,128)(2,1)S(1)}, u32[]{:S(2)}, u32[]{:S(2)}) collective-permute-start(bf16[5,256,128]{2,1,0:T(8,128)(2,1)S(1)} %collective-permute-done.4.refs_7_), channel_id=1, source_target_pairs={{0,64},{64,128},{128,192},{192,256},{256,320},{320,384},{384,448},... | collective-permute-start | bytes 983048 | tf_op jit(solution)/shard_map/ppermute | solution.py:127
  66.2 0.1 pad_maximum_fusion
  66.2 0.1 pad_maximum_fusion.1
  66.3 0.4 collective-permute-done.5.refs_3_
  66.7 5.3 %collective-permute-start.6 = (bf16[5,256,128]{2,1,0:T(8,128)(2,1)S(1)}, bf16[5,256,128]{2,1,0:T(8,128)(2,1)S(1)}, u32[]{:S(2)}, u32[]{:S(2)}) collective-permute-start(bf16[5,256,128]{2,1,0:T(8,128)(2,1)S(1)} %collective-permute-done.5.refs_3_), channel_id=1, source_target_pairs={{0,64},{64,128},{128,192},{192,256},{256,320},{320,384},{384,448},... | collective-permute-start | bytes 983048 | tf_op jit(solution)/shard_map/ppermute | solution.py:127
  72.0 1.9 %collective-permute-start.8 = (bf16[10,256,128]{2,1,0:T(8,128)(2,1)S(1)}, bf16[10,256,128]{2,1,0:T(8,128)(2,1)S(1)}, u32[]{:S(2)}, u32[]{:S(2)}) collective-permute-start(bf16[10,256,128]{2,1,0:T(8,128)(2,1)S(1)} %pad_maximum_fusion), channel_id=1, source_target_pairs={{0,32},{32,0},{1,33},{33,1},{2,34},{34,2},{3,35},{35,3},{4,36},{36... | collective-permute-start | bytes 1966088 | tf_op jit(solution)/shard_map/ppermute | solution.py:122
  73.9 2.4 %collective-permute-start.9 = (bf16[10,256,128]{2,1,0:T(8,128)(2,1)S(1)}, bf16[10,256,128]{2,1,0:T(8,128)(2,1)S(1)}, u32[]{:S(2)}, u32[]{:S(2)}) collective-permute-start(bf16[10,256,128]{2,1,0:T(8,128)(2,1)S(1)} %pad_maximum_fusion.1), channel_id=1, source_target_pairs={{0,32},{32,0},{1,33},{33,1},{2,34},{34,2},{3,35},{35,3},{4,36},{36... | collective-permute-start | bytes 1966088 | tf_op jit(solution)/shard_map/ppermute | solution.py:122
  76.3 0.0 collective-permute-done.7.refs_8_
  76.3 0.1 pad_maximum_fusion.2
  76.4 1.9 %collective-permute-start.10 = (bf16[10,256,128]{2,1,0:T(8,128)(2,1)S(1)}, bf16[10,256,128]{2,1,0:T(8,128)(2,1)S(1)}, u32[]{:S(2)}, u32[]{:S(2)}) collective-permute-start(bf16[10,256,128]{2,1,0:T(8,128)(2,1)S(1)} %pad_maximum_fusion.2), channel_id=1, source_target_pairs={{0,32},{32,0},{1,33},{33,1},{2,34},{34,2},{3,35},{35,3},{4,36},{36... | collective-permute-start | bytes 1966088 | tf_op jit(solution)/shard_map/ppermute | solution.py:122
  78.3 0.0 collective-permute-done.6.refs_4_
  78.3 3.4 %collective-permute-start.11 = (bf16[5,256,128]{2,1,0:T(8,128)(2,1)S(1)}, bf16[5,256,128]{2,1,0:T(8,128)(2,1)S(1)}, u32[]{:S(2)}, u32[]{:S(2)}) collective-permute-start(bf16[5,256,128]{2,1,0:T(8,128)(2,1)S(1)} %collective-permute-done.6.refs_4_), channel_id=1, source_target_pairs={{0,32},{32,0},{1,33},{33,1},{2,34},{34,2},{3,35},{35,3},{4,36},{36... | collective-permute-start | bytes 983048 | tf_op jit(solution)/shard_map/ppermute | solution.py:122
  81.8 1.2 %collective-permute-done.11.refs_12_ = bf16[5,256,128]{2,1,0:T(8,128)(2,1)S(1)} collective-permute-done((bf16[5,256,128]{2,1,0:T(8,128)(2,1)S(1)}, bf16[5,256,128]{2,1,0:T(8,128)(2,1)S(1)}, u32[]{:S(2)}, u32[]{:S(2)}) %collective-permute-start.11) | collective-permute-done | bytes 327712 | tf_op jit(solution)/shard_map/ppermute | solution.py:122
  83.0 0.0 collective-permute-done.8.refs_9_
  83.0 0.0 collective-permute-done.9.refs_10_
  83.0 0.0 collective-permute-done.10.refs_11_
  83.0 0.4 shard_map.37
  83.5 0.0 copy-start
  83.5 2.3 %copy-done = bf16[40,512,128]{2,1,0:T(8,128)(2,1)} copy-done((bf16[40,512,128]{2,1,0:T(8,128)(2,1)}, bf16[40,512,128]{2,1,0:T(8,128)(2,1)S(1)}, u32[]{:S(2)}) %copy-start) | copy-done | bytes 5242904
  85.8 0.0 all-to-all-done.1
  85.8 5.5 %shard_map.38 = bf16[2048,512]{1,0:T(8,128)(2,1)} custom-call(bf16[40,512,128]{2,1,0:T(8,128)(2,1)} %copy-done, bf16[8,512,128]{2,1,0:T(8,128)(2,1)S(1)} %get-tuple-element.17.head, bf16[2048,512]{1,0:T(8,128)(2,1)S(1)} %bitcast.14), custom_call_target="tpu_custom_call" | custom-call | flops 2684354560 | bytes 9437184 | tf_op jit(solution)/shard_map/pallas_call | solution.py:153
  (3 shorter events, 0.0 us)
Async XLA Ops:
  1.7 20.7 %all-to-all-start = ((bf16[32,5,8,128]{3,2,1,0:T(8,128)(2,1)}), bf16[32,5,8,128]{3,2,1,0:T(8,128)(2,1)S(1)}, u32[]{:S(2)}, u32[]{:S(2)}) async-start(bf16[32,5,8,128]{3,2,1,0:T(8,128)(2,1)} %broadcast_in_dim.2), calls=%async_computation | async-start | bytes 655360 | tf_op jit(solution)/shard_map/all_to_all | solution.py:115
  22.3 63.4 %all-to-all-start.1 = ((bf16[32,64,512]{2,1,0:T(8,128)(2,1)}), bf16[32,64,512]{2,1,0:T(8,128)(2,1)S(1)}, u32[]{:S(2)}, u32[]{:S(2)}) async-start(bf16[32,64,512]{2,1,0:T(8,128)(2,1)} %bitcast.15), calls=%async_computation.1 | async-start | bytes 4194304 | tf_op jit(solution)/shard_map/all_to_all | solution.py:119
  29.6 14.4 %collective-permute-start.2 = (bf16[5,256,128]{2,1,0:T(8,128)(2,1)S(1)}, bf16[5,256,128]{2,1,0:T(8,128)(2,1)S(1)}, u32[]{:S(2)}, u32[]{:S(2)}) collective-permute-start(bf16[5,256,128]{2,1,0:T(8,128)(2,1)S(1)} %copy_bitcast_fusion.refs_0_), channel_id=1, source_target_pairs={{0,32},{32,0},{1,33},{33,1},{2,34},{34,2},{3,35},{35,3},{4,36},{36... | collective-permute-start | bytes 983048 | tf_op jit(solution)/shard_map/ppermute | solution.py:122
  33.4 14.7 %collective-permute-start = (bf16[5,256,128]{2,1,0:T(8,128)(2,1)S(1)}, bf16[5,256,128]{2,1,0:T(8,128)(2,1)S(1)}, u32[]{:S(2)}, u32[]{:S(2)}) collective-permute-start(bf16[5,256,128]{2,1,0:T(8,128)(2,1)S(1)} %copy_bitcast_fusion.refs_0_), channel_id=1, source_target_pairs={{0,64},{64,128},{128,192},{192,256},{256,320},{320,384},{384,448},... | collective-permute-start | bytes 983048 | tf_op jit(solution)/shard_map/ppermute | solution.py:127
  44.0 9.3 %collective-permute-start.3 = (bf16[5,256,128]{2,1,0:T(8,128)(2,1)S(1)}, bf16[5,256,128]{2,1,0:T(8,128)(2,1)S(1)}, u32[]{:S(2)}, u32[]{:S(2)}) collective-permute-start(bf16[5,256,128]{2,1,0:T(8,128)(2,1)S(1)} %collective-permute-done.2.refs_5_), channel_id=1, source_target_pairs={{0,64},{64,128},{128,192},{192,256},{256,320},{320,384},{384,448},... | collective-permute-start | bytes 983048 | tf_op jit(solution)/shard_map/ppermute | solution.py:127
  48.0 9.3 %collective-permute-start.1 = (bf16[5,256,128]{2,1,0:T(8,128)(2,1)S(1)}, bf16[5,256,128]{2,1,0:T(8,128)(2,1)S(1)}, u32[]{:S(2)}, u32[]{:S(2)}) collective-permute-start(bf16[5,256,128]{2,1,0:T(8,128)(2,1)S(1)} %collective-permute-done.refs_1_), channel_id=1, source_target_pairs={{0,64},{64,128},{128,192},{192,256},{256,320},{320,384},{384,448},... | collective-permute-start | bytes 983048 | tf_op jit(solution)/shard_map/ppermute | solution.py:127
  53.4 9.3 %collective-permute-start.4 = (bf16[5,256,128]{2,1,0:T(8,128)(2,1)S(1)}, bf16[5,256,128]{2,1,0:T(8,128)(2,1)S(1)}, u32[]{:S(2)}, u32[]{:S(2)}) collective-permute-start(bf16[5,256,128]{2,1,0:T(8,128)(2,1)S(1)} %collective-permute-done.3.refs_6_), channel_id=1, source_target_pairs={{0,64},{64,128},{128,192},{192,256},{256,320},{320,384},{384,448},... | collective-permute-start | bytes 983048 | tf_op jit(solution)/shard_map/ppermute | solution.py:127
  57.4 9.3 %collective-permute-start.5 = (bf16[5,256,128]{2,1,0:T(8,128)(2,1)S(1)}, bf16[5,256,128]{2,1,0:T(8,128)(2,1)S(1)}, u32[]{:S(2)}, u32[]{:S(2)}) collective-permute-start(bf16[5,256,128]{2,1,0:T(8,128)(2,1)S(1)} %collective-permute-done.1.refs_2_), channel_id=1, source_target_pairs={{0,64},{64,128},{128,192},{192,256},{256,320},{320,384},{384,448},... | collective-permute-start | bytes 983048 | tf_op jit(solution)/shard_map/ppermute | solution.py:127
  62.7 13.6 %collective-permute-start.7 = (bf16[5,256,128]{2,1,0:T(8,128)(2,1)S(1)}, bf16[5,256,128]{2,1,0:T(8,128)(2,1)S(1)}, u32[]{:S(2)}, u32[]{:S(2)}) collective-permute-start(bf16[5,256,128]{2,1,0:T(8,128)(2,1)S(1)} %collective-permute-done.4.refs_7_), channel_id=1, source_target_pairs={{0,64},{64,128},{128,192},{192,256},{256,320},{320,384},{384,448},... | collective-permute-start | bytes 983048 | tf_op jit(solution)/shard_map/ppermute | solution.py:127
  66.7 11.7 %collective-permute-start.6 = (bf16[5,256,128]{2,1,0:T(8,128)(2,1)S(1)}, bf16[5,256,128]{2,1,0:T(8,128)(2,1)S(1)}, u32[]{:S(2)}, u32[]{:S(2)}) collective-permute-start(bf16[5,256,128]{2,1,0:T(8,128)(2,1)S(1)} %collective-permute-done.5.refs_3_), channel_id=1, source_target_pairs={{0,64},{64,128},{128,192},{192,256},{256,320},{320,384},{384,448},... | collective-permute-start | bytes 983048 | tf_op jit(solution)/shard_map/ppermute | solution.py:127
  72.0 11.0 %collective-permute-start.8 = (bf16[10,256,128]{2,1,0:T(8,128)(2,1)S(1)}, bf16[10,256,128]{2,1,0:T(8,128)(2,1)S(1)}, u32[]{:S(2)}, u32[]{:S(2)}) collective-permute-start(bf16[10,256,128]{2,1,0:T(8,128)(2,1)S(1)} %pad_maximum_fusion), channel_id=1, source_target_pairs={{0,32},{32,0},{1,33},{33,1},{2,34},{34,2},{3,35},{35,3},{4,36},{36... | collective-permute-start | bytes 1966088 | tf_op jit(solution)/shard_map/ppermute | solution.py:122
  73.9 9.1 %collective-permute-start.9 = (bf16[10,256,128]{2,1,0:T(8,128)(2,1)S(1)}, bf16[10,256,128]{2,1,0:T(8,128)(2,1)S(1)}, u32[]{:S(2)}, u32[]{:S(2)}) collective-permute-start(bf16[10,256,128]{2,1,0:T(8,128)(2,1)S(1)} %pad_maximum_fusion.1), channel_id=1, source_target_pairs={{0,32},{32,0},{1,33},{33,1},{2,34},{34,2},{3,35},{35,3},{4,36},{36... | collective-permute-start | bytes 1966088 | tf_op jit(solution)/shard_map/ppermute | solution.py:122
  76.4 6.6 %collective-permute-start.10 = (bf16[10,256,128]{2,1,0:T(8,128)(2,1)S(1)}, bf16[10,256,128]{2,1,0:T(8,128)(2,1)S(1)}, u32[]{:S(2)}, u32[]{:S(2)}) collective-permute-start(bf16[10,256,128]{2,1,0:T(8,128)(2,1)S(1)} %pad_maximum_fusion.2), channel_id=1, source_target_pairs={{0,32},{32,0},{1,33},{33,1},{2,34},{34,2},{3,35},{35,3},{4,36},{36... | collective-permute-start | bytes 1966088 | tf_op jit(solution)/shard_map/ppermute | solution.py:122
  78.3 4.7 %collective-permute-start.11 = (bf16[5,256,128]{2,1,0:T(8,128)(2,1)S(1)}, bf16[5,256,128]{2,1,0:T(8,128)(2,1)S(1)}, u32[]{:S(2)}, u32[]{:S(2)}) collective-permute-start(bf16[5,256,128]{2,1,0:T(8,128)(2,1)S(1)} %collective-permute-done.6.refs_4_), channel_id=1, source_target_pairs={{0,32},{32,0},{1,33},{33,1},{2,34},{34,2},{3,35},{35,3},{4,36},{36... | collective-permute-start | bytes 983048 | tf_op jit(solution)/shard_map/ppermute | solution.py:122
  83.5 2.3 %copy-start = (bf16[40,512,128]{2,1,0:T(8,128)(2,1)}, bf16[40,512,128]{2,1,0:T(8,128)(2,1)S(1)}, u32[]{:S(2)}) copy-start(bf16[40,512,128]{2,1,0:T(8,128)(2,1)S(1)} %get-tuple-element.16.factor) | copy-start | bytes 15728644
